TPU v7x, 128 devices: a whole 4x4x4 slice. The times are simulated.
128 devices in a mesh: grp: 4 (over y), seq: 32 (over z, x, core).
Axes of the slice: x: 4, y: 4, z: 4, core: 2. Of those that a mesh axis runs over, the one named last changes fastest.
Arguments:
- rows_in: bfloat16 [4, 896, 3072], P('grp', 'seq'), may hold values from -6 to 6
- fresh_qkv: bfloat16 [4, 896, 3, 3072], P('grp', 'seq'), may hold values from -30 to 30
- kv_cache: bfloat16 [4, 4096, 2, 3072], P('grp', 'seq'), may hold values from -6 to 6
- chosen: int32 [4, 896], P('grp', 'seq'), may hold values from 0 to 127, as said below
- counts: int32 [4, 32], P('grp', 'seq'), may hold values from 12 to 28, as said below
- modulation: bfloat16 [4, 4, 3072], P('grp'), may hold values from -3 to 3
- w_up: bfloat16 [3072, 6144], P(None, 'grp'), may hold values from -0.109375 to 0.109375
- b_up: bfloat16 [6144], P('grp'), may hold values from -3 to 3
- w_down: bfloat16 [6144, 3072], P('grp'), may hold values from -0.078125 to 0.078125
- b_down: bfloat16 [3072], replicated, may hold values from -3 to 3
Outputs:
- rows_out: bfloat16 [4, 896, 3072], P('grp', 'seq')
Inputs may be any that keep to these rules, and one draw needn't show every extreme that they name: The 32 counts of one request sum to exactly 512; in every request some device has 28 and some has 12. `chosen`: the 28 entries of one device's list are distinct local token indices; the first counts entries name the tokens to refresh, the rest are unused.
All inputs are finite; a program needn't handle non-finite values.
Results may differ from a plain program's by a relative error of at most 0.0042.
Values may be sent and summed in bfloat16 or wider, within the bound.
No kernel may reach another device: no remote copies, remote signals or barrier semaphores. Data moves between devices by JAX's collectives and lax.ppermute only.
A program may use at most 128 MiB of HBM per device.

v0:
```python
import jax
import jax.numpy as jnp
from jax import lax
from jax.sharding import PartitionSpec as P

HEAD_DIM = 128


eps_norm = 1e-06


def layer_norm(values):
    center = values - jnp.mean(values, axis=-1, keepdims=True)
    spread = jnp.mean(center * center, axis=-1, keepdims=True)
    return center * lax.rsqrt(spread + eps_norm)


def attend(queries, keys_now, values_now):
    row_count, feat_width = queries.shape
    head_count = feat_width // HEAD_DIM
    score_scale = HEAD_DIM ** (-0.5)
    everyone = lax.all_gather(queries, "seq", axis=0, tiled=True)
    total_rows = everyone.shape[0]
    shard_count = lax.axis_size("seq")
    group_size = min(shard_count, 8)
    block_count = shard_count // group_size
    blocks = everyone.reshape(block_count, group_size * row_count, head_count, HEAD_DIM)
    key_heads = keys_now.reshape(-1, head_count, HEAD_DIM)
    value_heads = values_now.reshape(-1, head_count, HEAD_DIM)

    def block_scores(query_block):
        return (
            jnp.einsum("qhd,khd->qhk", query_block, key_heads, preferred_element_type=jnp.float32)
            * score_scale
        )

    local_top = lax.map(lambda query_block: jnp.max(block_scores(query_block), axis=2), blocks)
    row_top = lax.pmax(local_top.reshape(total_rows, head_count), "seq")

    def weigh(pair_in):
        query_block, block_top = pair_in
        exp_scores = jnp.exp(block_scores(query_block) - block_top[:, :, None])
        mass_part = jnp.sum(exp_scores, axis=2)
        mixed_part = jnp.einsum(
            "qhk,khd->qhd",
            exp_scores.astype(jnp.bfloat16),
            value_heads,
            preferred_element_type=jnp.float32,
        )
        return (mixed_part.reshape(-1, feat_width), mass_part)

    mixed_all, mass_all = lax.map(
        weigh, (blocks, row_top.reshape(block_count, group_size * row_count, head_count))
    )
    mixed_sum, mass_sum = (
        lax.psum_scatter(
            mixed_all.reshape(total_rows, feat_width), "seq", scatter_dimension=0, tiled=True
        ),
        lax.psum_scatter(
            mass_all.reshape(total_rows, head_count), "seq", scatter_dimension=0, tiled=True
        ),
    )
    return (mixed_sum.reshape(row_count, head_count, HEAD_DIM) / mass_sum[:, :, None]).reshape(
        row_count, feat_width
    )


def feed_forward(normed, w_up, b_up, w_down, b_down):
    lifted = jnp.dot(
        lax.all_gather(normed, "grp", axis=0, tiled=True), w_up, preferred_element_type=jnp.float32
    ) + b_up.astype(jnp.float32)
    active = jax.nn.gelu(lifted, approximate=True).astype(jnp.bfloat16)
    terms = jnp.dot(active, w_down, preferred_element_type=jnp.float32)
    summed = lax.psum_scatter(terms, "grp", scatter_dimension=0, tiled=True)
    return summed + b_down.astype(jnp.float32)


def body(rows_in, fresh_qkv, kv_cache, chosen, counts, modulation, w_up, b_up, w_down, b_down):
    slot_rows = rows_in.shape[1]
    own_count = counts[0, 0]
    live_slot = jnp.arange(slot_rows) < own_count
    fresh_rows = fresh_qkv[0]
    target = jnp.where(live_slot, chosen[0], kv_cache.shape[1])
    patched = kv_cache[0].at[target].set(fresh_rows[:, 1:3], mode="drop")
    shifts = modulation[0].astype(jnp.float32)
    attended = attend(fresh_rows[:, 0], patched[:, 0], patched[:, 1])
    hidden = rows_in[0].astype(jnp.float32) + shifts[2] * attended
    normed = (layer_norm(hidden) * (1.0 + shifts[1]) + shifts[0]).astype(jnp.bfloat16)
    feed_out = feed_forward(normed, w_up, b_up, w_down, b_down)
    result = (hidden + shifts[3] * feed_out).astype(jnp.bfloat16)
    result = jnp.where(live_slot[:, None], result, jnp.zeros_like(result))
    return result[None]


def solution(mesh):
    placed = (
        P("grp", "seq", None),
        P("grp", "seq", None, None),
        P("grp", "seq", None, None),
        P("grp", "seq"),
        P("grp", "seq"),
        P("grp", None, None),
        P(None, "grp"),
        P("grp"),
        P("grp", None),
        P(),
    )
    return jax.shard_map(
        body, mesh=mesh, in_specs=placed, out_specs=P("grp", "seq", None), check_vma=False
    )
```

profile of v0, /device:TPU:0, one launch (start us, length us, event | category | flops | bytes accessed | tf_op | source)
XLA Modules:
  0.0 550.0 jit_solution(17178468815308200375)
XLA Ops:
  11.8 3.1 fusion.45
  14.9 3.7 copy.36
  19.0 52.4 %all-gather.4.cloned.1.call-done = bf16[896,1,3072]{2,1,0:T(2,128)(2,1)} async-done(((bf16[28,1,3072]{2,1,0:T(2,128)(2,1)}), bf16[896,1,3072]{2,1,0:T(2,128)(2,1)}) %all-gather.4.cloned.1.call-update) | async-done | bytes 5505040 | tf_op jit(solution)/shard_map/all_gather | solution.py:22
  71.4 32.7 %reduce.1 = bf16[896,3072]{1,0:T(8,128)(2,1)} reduce(bf16[896,1,3072]{2,1,0:T(2,128)(2,1)} %all-gather.4.cloned.1.call-done, bf16[]{:T(256)} %constant.73), dimensions={1}, to_apply=%all-gather.reduce_sub_computation | reduce | bytes 11010050 | tf_op jit(solution)/shard_map/all_gather | solution.py:22
  104.1 4.2 copy.51
  108.3 3.2 copy.40
  111.5 12.1 %while.22 = (s32[]{:T(128)}, f32[4,224,24]{1,2,0:T(8,128)}, bf16[4,224,24,128]{3,1,2,0:T(8,128)(2,1)}, bf16[128,24,128]{2,0,1:T(8,128)(2,1)S(1)}, s32[]{:T(128)}) while((s32[]{:T(128)}, f32[4,224,24]{1,2,0:T(8,128)}, bf16[4,224,24,128]{3,1,2,0:T(8,128)(2,1)}, bf16[128,24,128]{2,0,1:T(8,128)(2,1)S(1)}, s32[]{:T(128)}) %tuple.45), condition=%wide.region_3.4_spmd, body=%wide.region_1.3_spmd.sunk | while | flops 177531648 | bytes 2231357 | solution.py:37
  111.5 2.4 multiply_reduce_fusion.3
  114.5 2.4 multiply_reduce_fusion.3
  117.5 2.4 multiply_reduce_fusion.3
  120.6 2.4 multiply_reduce_fusion.3
  128.0 93.6 %all-reduce.8.cloned.1.call-done = f32[4,224,24]{1,2,0:T(8,128)} async-done(((f32[4,224,24]{1,2,0:T(8,128)}), f32[4,224,24]{1,2,0:T(8,128)}) %all-reduce.8.cloned.1.call-update) | async-done | bytes 86032 | tf_op jit(solution)/shard_map/pmax | solution.py:38
  221.6 62.7 %while.23 = (s32[]{:T(128)}, f32[4,224,3072]{2,1,0:T(8,128)}, f32[4,224,24]{1,0,2:T(4,128)}, bf16[4,224,24,128]{3,1,2,0:T(8,128)(2,1)}, bf16[128,24,128]{2,0,1:T...) while((s32[]{:T(128)}, f32[4,224,3072]{2,1,0:T(8,128)}, ...), condition=%wide.region_7.8_spmd, body=%wide.region_5.7_spmd.sunk | while | flops 356444928 | bytes 28002432 | solution.py:52
  222.4 3.6 fusion.65
  228.1 3.1 copy.57
  231.2 2.6 broadcast_in_dim.50
  238.0 3.6 fusion.65
  243.7 3.1 copy.57
  246.8 2.6 broadcast_in_dim.50
  253.7 3.6 fusion.65
  259.4 3.1 copy.57
  262.5 2.6 broadcast_in_dim.50
  269.3 3.6 fusion.65
  275.0 3.1 copy.57
  278.1 2.6 broadcast_in_dim.50
  284.3 91.9 %fusion = f32[32,3072]{1,0:T(8,128)S(1)} fusion(f32[896,3072]{1,0:T(8,128)} %bitcast.101), kind=kCustom, calls=%all-reduce-scatter | all-reduce-scatter fusion | flops 3145729 | bytes 11403776
  386.8 95.9 %all-reduce.10.cloned.1.call-done = f32[896,24]{0,1:T(8,128)} async-done(((f32[896,24]{0,1:T(8,128)}), f32[896,24]{0,1:T(8,128)}) %all-reduce.10.cloned.1.call-update) | async-done | bytes 86032
  484.6 4.1 concatenate
  491.1 13.9 %all-gather.1 = bf16[4,28,3072]{2,1,0:T(8,128)(2,1)S(1)} all-gather(bf16[1,28,3072]{2,1,0:T(8,128)(2,1)S(1)} %fusion.35), channel_id=1, replica_groups=mesh['grp'=4,'seq'=32] {'grp'}, dimensions={0}, use_global_device_ids=true | all-gather | bytes 860160 | tf_op jit(solution)/shard_map/all_gather | solution.py:70
  505.1 9.4 %fusion.24 = f32[112,3072]{1,0:T(8,128)S(1)} fusion(bf16[1536,3072]{1,0:T(8,128)(2,1)} %param.22, bf16[112,3072]{1,0:T(8,128)(2,1)S(1)} %reshape.96, bf16[3072,1536]{1,0:T(8,128)(2,1)} %param.20, f32[1536]{0:T(1024)S(1)} %copy-done.6), kind=kOutput, calls=%fused_computation.31 | convolution fusion | flops 2115649536 | bytes 20944896 | tf_op jit(solution)/shard_map/dot_general | solution.py:73
  514.5 22.4 %fusion.1 = f32[32,3072]{1,0:T(8,128)S(1)} fusion(f32[112,3072]{1,0:T(8,128)S(1)} %fusion.24), kind=kCustom, calls=%all-reduce-scatter.1 | all-reduce-scatter fusion | flops 393217 | bytes 1769984
  536.9 2.3 collective-permute-start.4
  (104 shorter events, 54.5 us)
Async XLA Ops:
  6.5 1.1 copy-start.2
  6.5 3.6 copy-start
  6.5 3.6 copy-start.11
  6.5 64.9 %all-gather.4.cloned.1.call-start = ((), (), s32[]{:S(2)}) async-start(), calls=%async_computation.1 | async-start | bytes 11354112 | tf_op jit(solution)/shard_map/all_gather | solution.py:22
  9.1 212.6 %all-reduce.8.cloned.1.call-start = ((), (), s32[]{:S(2)}) async-start(), calls=%async_computation | async-start | bytes 196608 | tf_op jit(solution)/shard_map/pmax | solution.py:38
  111.5 12.3 %copy-start.4 = (bf16[1,4,3072]{2,1,0:T(4,128)(2,1)S(1)}, bf16[1,4,3072]{2,1,0:T(4,128)(2,1)}, u32[]{:S(2)}) copy-start(bf16[1,4,3072]{2,1,0:T(4,128)(2,1)} %param.19) | copy-start | bytes 73732
  123.6 359.1 %all-reduce.10.cloned.1.call-start = ((), (), s32[]{:S(2)}) async-start(), calls=%async_computation.2 | async-start | bytes 172032
  233.8 1.8 copy-start.1
  249.5 1.8 copy-start.1
  265.1 1.7 copy-start.1
  280.8 1.8 copy-start.1
  284.3 98.0 %copy-start.5 = (f32[4,224,24]{1,0,2:T(4,128)S(1)}, f32[4,224,24]{1,0,2:T(4,128)}, u32[]{:S(2)}) copy-start(f32[4,224,24]{1,0,2:T(4,128)} %get-tuple-element.67) | copy-start | bytes 258052
  284.3 100.2 %copy-start.8 = (bf16[1536]{0:T(1024)(128)(2,1)S(1)}, bf16[1536]{0:T(1024)(128)(2,1)}, u32[]{:S(2)}) copy-start(bf16[1536]{0:T(1024)(128)(2,1)} %param.21) | copy-start | bytes 9220
  284.3 100.8 %copy-start.9 = (u32[128]{0:T(128)S(1)}, u32[128]{0:T(128)}, u32[]{:S(2)}) copy-start(u32[128]{0:T(128)} %constant.63) | copy-start | bytes 1540
  376.3 107.6 %collective-permute-start = (f32[32,3072]{1,0:T(8,128)S(1)}, f32[32,3072]{1,0:T(8,128)S(1)}, u32[]{:S(2)}, u32[]{:S(2)}) collective-permute-start(f32[32,3072]{1,0:T(8,128)S(1)} %fusion), channel_id=1, source_target_pairs={{0,1},{1,2},{2,3},{3,4},{4,5},{5,6},{6,7},{7,8},{8,9},{9,10},{10,1... | collective-permute-start | bytes 1179656
  377.6 106.3 %collective-permute-start.1 = (f32[32,3072]{1,0:T(8,128)S(1)}, f32[32,3072]{1,0:T(8,128)S(1)}, u32[]{:S(2)}, u32[]{:S(2)}) collective-permute-start(f32[32,3072]{1,0:T(8,128)S(1)} %fusion), channel_id=1, source_target_pairs={{0,2},{1,3},{2,4},{3,5},{4,6},{5,7},{6,8},{7,9},{8,10},{9,11},{10,... | collective-permute-start | bytes 1179656
  378.9 105.7 %collective-permute-start.2 = (f32[32,3072]{1,0:T(8,128)S(1)}, f32[32,3072]{1,0:T(8,128)}, u32[]{:S(2)}, u32[]{:S(2)}) collective-permute-start(f32[32,3072]{1,0:T(8,128)S(1)} %fusion), channel_id=1, source_target_pairs={{0,3},{1,4},{2,5},{3,6},{4,7},{5,8},{6,9},{7,10},{8,11},{9,12},{10... | collective-permute-start | bytes 1179656
  381.0 102.9 %collective-permute-start.3 = (f32[28,3072]{1,0:T(8,128)S(1)}, f32[28,3072]{1,0:T(8,128)S(1)}, u32[]{:S(2)}, u32[]{:S(2)}) collective-permute-start(f32[28,3072]{1,0:T(8,128)S(1)} %slice.44), channel_id=1, source_target_pairs={{0,4},{1,5},{2,6},{3,7},{4,8},{5,9},{6,10},{7,11},{8,12},{9,13},{1... | collective-permute-start | bytes 1032200
  483.9 0.8 copy-start.3
  488.8 16.3 %copy-start.6 = (f32[1536]{0:T(1024)S(1)}, f32[1536]{0:T(1024)}, u32[]{:S(2)}) copy-start(f32[1536]{0:T(1024)} %convert_element_type.32) | copy-start | bytes 18436
  505.1 34.0 %copy-start.10 = (u32[128]{0:T(128)S(1)}, u32[128]{0:T(128)}, u32[]{:S(2)}) copy-start(u32[128]{0:T(128)} %constant.71) | copy-start | bytes 1540
  505.1 35.3 %copy-start.7 = (bf16[3072]{0:T(1024)(128)(2,1)S(1)}, bf16[3072]{0:T(1024)(128)(2,1)}, u32[]{:S(2)}) copy-start(bf16[3072]{0:T(1024)(128)(2,1)} %param.23) | copy-start | bytes 18436
  536.9 5.4 collective-permute-start.4
Sparse Core Ops, SparseCore 0:
  9.6 61.7 all-gather.3
  123.7 97.8 all-reduce.7
  383.2 99.4 all-reduce.9
where the time goes:
time: 553 us; the launch traced here: 550 us
  waiting for transfers between devices  244 us (44%)
  blocking collectives  128 us (23%)
  local copies, waits for them, and re-layouts  73.4 us (13%)
  matrix products  41.8 us (8%)
  other arithmetic  38.4 us (7%)
  between operations  15.9 us (3%)
  starting transfers between devices  8.5 us (2%)
    unnamed x2, blocking collectives  114 us
    unnamed x9, waiting for transfers between devices  97.8 us
    pmax x1, waiting for transfers between devices, attend(): row_top = lax.pmax(local_top.reshape(total_rows, head_count), 'seq')  93.6 us
    all_gather x1, waiting for transfers between devices, attend(): everyone = lax.all_gather(queries, 'seq', axis=0, tiled=True)  52.4 us
    all_gather x1, other arithmetic, attend(): everyone = lax.all_gather(queries, 'seq', axis=0, tiled=True)  32.7 us
    dot_general x8, matrix products, block_scores(): jnp.einsum('qhd,khd->qhk', query_block, key_heads, preferred_element_type...  23.8 us
    all_gather x1, blocking collectives, feed_forward(): lax.all_gather(normed, 'grp', axis=0, tiled=True)  13.9 us
    unnamed x34, local copies, waits for them, and re-layouts  13.4 us
  transfers between devices with their start and end apart: 8, of which 4 were waited for; matrix products, arithmetic and copies ran while one was open for 3% of the time, Pallas kernels for 0%

commit v1 on v0

v1 whole, which is shorter than its diff:
```python
import jax
import jax.numpy as jnp
from jax import lax
from jax.experimental import pallas as pl
from jax.experimental.pallas import tpu as pltpu
from jax.sharding import PartitionSpec as P

HEAD_DIM = 128
HEADS_HERE = 3
BLOCK = HEADS_HERE * HEAD_DIM
SLOT_PAD = 32
LOG2E = 1.4426950408889634
EPS = 1e-06
SEQ = ("z", "x", "core")
bf16 = jnp.bfloat16
f32 = jnp.float32
i32 = jnp.int32
MB = 1 << 20


def call(kernel, out_shape, scratch=(), limit=16, smem=(), n_in=None, cost=None, **kw):
    specs = [
        pl.BlockSpec(memory_space=pltpu.SMEM if i in smem else pltpu.VMEM) for i in range(n_in)
    ]
    return pl.pallas_call(
        kernel,
        out_shape=out_shape,
        in_specs=specs,
        scratch_shapes=list(scratch),
        compiler_params=pltpu.CompilerParams(vmem_limit_bytes=limit * MB),
        cost_estimate=cost,
        **kw,
    )


def pack_queries_kernel(q_ref, out_ref):
    rows = q_ref.shape[0]
    for dest in range(32):
        z, x, core = dest // 8, dest // 2 % 4, dest % 2
        group = x if core == 0 else 4 + z
        out_ref[dest, :rows, :] = q_ref[:, group * BLOCK : (group + 1) * BLOCK]
        out_ref[dest, rows:, :] = jnp.zeros((SLOT_PAD - rows, BLOCK), bf16)


def pack_cache_kernel(info_ref, kv_ref, kv_new_ref, chosen_ref, keep_ref, send_ref, patched):
    tokens = kv_ref.shape[0]
    slots = kv_new_ref.shape[1]
    core, ring_x, ring_z, count = info_ref[0], info_ref[1], info_ref[2], info_ref[3]
    token_id = lax.broadcasted_iota(i32, (tokens, slots), 0)
    slot_id = lax.broadcasted_iota(i32, (tokens, slots), 1)
    hit = (token_id == chosen_ref[...]) & (slot_id < count)
    hot = jnp.where(hit, 1.0, 0.0)
    taken = jnp.sum(hot, axis=1, keepdims=True) > 0.5
    hot = hot.astype(bf16)
    old = jnp.swapaxes(kv_ref[...], 0, 1)
    for which in range(2):
        new = jnp.dot(hot, kv_new_ref[which], preferred_element_type=f32)
        patched[which] = jnp.where(taken, new, old[which].astype(f32)).astype(bf16)
    half = 4 * BLOCK
    for k in range(4):
        mine = lax.rem(jnp.where(core == 0, ring_x, ring_z) + k, 4)
        other = lax.rem(jnp.where(core == 0, ring_z, ring_x) + k, 4)
        at_mine = pl.multiple_of(core * half + mine * BLOCK, BLOCK)
        at_other = pl.multiple_of((1 - core) * half + other * BLOCK, BLOCK)
        for which in range(2):
            keep_ref[k, which] = patched[which, :, pl.ds(at_mine, BLOCK)]
            send_ref[k, which] = patched[which, :, pl.ds(at_other, BLOCK)]


def attention_kernel(q_ref, keep_ref, first_ref, r1_ref, r2_ref, r3_ref, out_ref, keys, values_t):
    sources = [keep_ref.at[0], first_ref.at[0]]
    for ref in (r1_ref, r2_ref, r3_ref):
        sources += [ref.at[0], ref.at[1]]
    for i, ref in enumerate(sources):
        keys[i * 128 : (i + 1) * 128, :] = ref[0]
        for h in range(HEADS_HERE):
            cols = slice(h * HEAD_DIM, (h + 1) * HEAD_DIM)
            values_t[h, :, i * 128 : (i + 1) * 128] = ref[1, :, cols].T
    scale = LOG2E * HEAD_DIM**-0.5
    tile = 256
    blocks = tile // SLOT_PAD

    def step(t, _):
        q_all = q_ref[pl.ds(t * blocks, blocks)].reshape(tile, BLOCK)
        for h in range(HEADS_HERE):
            cols = slice(h * HEAD_DIM, (h + 1) * HEAD_DIM)
            scores = lax.dot_general(
                keys[:, cols], q_all[:, cols], (((1,), (1,)), ((), ())), preferred_element_type=f32
            )
            top = jnp.max(scores, axis=0, keepdims=True)
            weights = jnp.exp2((scores - top) * scale)
            mass = jnp.sum(weights, axis=0, keepdims=True)
            mixed = jnp.dot(values_t[h], weights.astype(bf16), preferred_element_type=f32)
            mixed = mixed * (1.0 / mass)
            level = top * scale + jnp.log2(mass)
            p0 = level.astype(bf16).astype(f32)
            rest = level - p0
            p1 = rest.astype(bf16).astype(f32)
            p2 = rest - p1
            for g in range(tile // 128):
                lanes = slice(g * 128, (g + 1) * 128)
                turned = mixed[:, lanes].T
                row = lax.broadcasted_iota(i32, (128, HEAD_DIM), 0) % SLOT_PAD
                turned = jnp.where(row == 28, p0[:, lanes], turned)
                turned = jnp.where(row == 29, p1[:, lanes], turned)
                turned = jnp.where(row == 30, p2[:, lanes], turned)
                out_ref[pl.ds(t * blocks + g * 4, 4), :, cols] = turned.astype(bf16).reshape(
                    4, SLOT_PAD, HEAD_DIM
                )
        return 0

    lax.fori_loop(0, q_ref.shape[0] // blocks, step, 0)


def combine_kernel(info_ref, parts_ref, rows_ref, mod_ref, hidden_ref, normed_ref, levels, turned):
    slots = rows_ref.shape[1]
    heads = 24

    def source(part, group):
        return part * 8 + group * 2 if group < 4 else (group - 4) * 8 + part * 2 + 1

    for part in range(4):
        for group in range(8):
            tail = parts_ref[source(part, group), 24:32, :].astype(f32)
            level = tail[4:5] + tail[5:6] + tail[6:7]
            for h in range(HEADS_HERE):
                at = part * heads + group * HEADS_HERE + h
                levels[at : at + 1, :] = level[:, h * HEAD_DIM : (h + 1) * HEAD_DIM]
    pieces = [levels[p * heads : (p + 1) * heads, :] for p in range(4)]
    top = jnp.maximum(jnp.maximum(pieces[0], pieces[1]), jnp.maximum(pieces[2], pieces[3]))
    weights = [jnp.exp2(piece - top) for piece in pieces]
    total = 1.0 / (weights[0] + weights[1] + weights[2] + weights[3])
    for p in range(4):
        levels[p * heads : (p + 1) * heads, :] = weights[p] * total
    levels[4 * heads :, :] = jnp.zeros((128 - 4 * heads, 128), f32)
    turned[...] = levels[...].T
    mine = turned[pl.ds(pl.multiple_of(info_ref[4] * SLOT_PAD, SLOT_PAD), SLOT_PAD), :]
    shifts = mod_ref[0].astype(f32)
    total_sum = jnp.zeros((SLOT_PAD, 1), f32)
    for group in range(8):
        for h in range(HEADS_HERE):
            head = group * HEADS_HERE + h
            acc = jnp.zeros((SLOT_PAD, HEAD_DIM), f32)
            for part in range(4):
                column = part * heads + head
                block = parts_ref[source(part, group), :, h * HEAD_DIM : (h + 1) * HEAD_DIM]
                acc = acc + mine[:, column : column + 1] * block.astype(f32)
            cols = slice(head * HEAD_DIM, (head + 1) * HEAD_DIM)
            attended = acc[:slots] * shifts[2:3, cols]
            hidden_ref[:slots, cols] = rows_ref[0, :, cols].astype(f32) + attended
    hidden_ref[slots:, :] = jnp.zeros((SLOT_PAD - slots, hidden_ref.shape[1]), f32)
    hidden = hidden_ref[...]
    center = hidden - jnp.mean(hidden, axis=1, keepdims=True)
    spread = jnp.mean(center * center, axis=1, keepdims=True)
    normed = center * lax.rsqrt(spread + EPS) * (1.0 + shifts[1:2]) + shifts[0:1]
    normed_ref[...] = normed.astype(bf16)


def feed_kernel(rows_ref, up_ref, b_up_ref, down_ref, out_ref, acc):
    step = pl.program_id(0)
    lifted = jnp.dot(rows_ref[...], up_ref[...], preferred_element_type=f32)
    lifted = lifted + b_up_ref[...].astype(f32)
    active = jax.nn.gelu(lifted, approximate=True).astype(bf16)
    terms = jnp.dot(active, down_ref[...], preferred_element_type=f32)

    @pl.when(step == 0)
    def _():
        acc[...] = terms

    @pl.when(step > 0)
    def _():
        acc[...] = acc[...] + terms

    @pl.when(step == pl.num_programs(0) - 1)
    def _():
        out_ref[...] = acc[...].astype(bf16)


def feed_forward(rows, w_up, b_up, w_down):
    count, width = rows.shape
    hidden_units = w_up.shape[1]
    tile = 256
    return pl.pallas_call(
        feed_kernel,
        grid=(hidden_units // tile,),
        in_specs=[
            pl.BlockSpec((count, width), lambda i: (0, 0)),
            pl.BlockSpec((width, tile), lambda i: (0, i)),
            pl.BlockSpec((1, tile), lambda i: (0, i)),
            pl.BlockSpec((tile, width), lambda i: (i, 0)),
        ],
        out_specs=pl.BlockSpec((count, width), lambda i: (0, 0)),
        out_shape=jax.ShapeDtypeStruct((count, width), bf16),
        scratch_shapes=[pltpu.VMEM((count, width), f32)],
        compiler_params=pltpu.CompilerParams(vmem_limit_bytes=24 * MB),
    )(rows, w_up, b_up, w_down)


def finish_kernel(info_ref, terms_ref, hidden_ref, mod_ref, b_down_ref, out_ref):
    slots = out_ref.shape[1]
    total = terms_ref[0].astype(f32)
    for p in range(1, 4):
        total = total + terms_ref[p].astype(f32)
    feed_out = total[:slots] + b_down_ref[...].astype(f32)
    result = hidden_ref[:slots] + mod_ref[0, 3:4].astype(f32) * feed_out
    live = lax.broadcasted_iota(i32, result.shape, 0) < info_ref[3]
    out_ref[0] = jnp.where(live, result, 0.0).astype(bf16)


def position(z, x, core):
    return (z % 4) * 8 + (x % 4) * 2 + core


def ring_pairs(k):
    return [
        (position(z, x, c), position(z, x + k, 0) if c == 0 else position(z + k, x, 1))
        for z in range(4)
        for x in range(4)
        for c in range(2)
    ]


def body(rows_in, fresh_qkv, kv_cache, chosen, counts, modulation, w_up, b_up, w_down, b_down):
    shape = jax.ShapeDtypeStruct
    slots, width = rows_in.shape[1], rows_in.shape[2]
    tokens = kv_cache.shape[1]
    core, ring_x, ring_z = (lax.axis_index(a) for a in ("core", "x", "z"))
    me = ring_z * 8 + ring_x * 2 + core
    info = jnp.stack([core, ring_x, ring_z, counts[0, 0], me % 4]).astype(i32)

    q_blocks = call(pack_queries_kernel, shape((32, SLOT_PAD, BLOCK), bf16), n_in=1)(fresh_qkv[0, :, 0])
    q_all = lax.all_to_all(q_blocks, SEQ, 0, 0, tiled=True)

    kv_new = jnp.swapaxes(fresh_qkv[0, :, 1:3], 0, 1)
    keep, send = call(
        pack_cache_kernel,
        [shape((4, 2, tokens, BLOCK), bf16)] * 2,
        scratch=[pltpu.VMEM((2, tokens, width), bf16)],
        n_in=4,
        smem=(0,),
    )(info, kv_cache[0], kv_new, chosen)
    swap = [(position(z, x, c), position(z, x, 1 - c)) for z in range(4) for x in range(4) for c in range(2)]
    first = lax.ppermute(send, SEQ, swap)
    others = [lax.ppermute(jnp.stack([keep[k], first[k]]), SEQ, ring_pairs(k)) for k in (1, 2, 3)]

    parts = call(
        attention_kernel,
        shape((32, SLOT_PAD, BLOCK), bf16),
        scratch=[pltpu.VMEM((8 * tokens, BLOCK), bf16), pltpu.VMEM((HEADS_HERE, HEAD_DIM, 8 * tokens), bf16)],
        n_in=6,
        limit=24,
    )(q_all, keep, first, *others)
    parts = lax.all_to_all(parts, SEQ, 0, 0, tiled=True)

    hidden, normed = call(
        combine_kernel,
        [shape((SLOT_PAD, width), f32), shape((SLOT_PAD, width), bf16)],
        scratch=[pltpu.VMEM((128, 128), f32), pltpu.VMEM((128, 128), f32)],
        n_in=4,
        smem=(0,),
    )(info, parts, rows_in, modulation)

    normed_all = lax.all_gather(normed, "y", axis=0, tiled=True)
    terms = feed_forward(normed_all, w_up, b_up[None], w_down)
    terms = lax.all_to_all(terms.reshape(4, SLOT_PAD, width), "y", 0, 0, tiled=True)
    return call(finish_kernel, shape((1, slots, width), bf16), n_in=5, smem=(0,))(
        info, terms, hidden, modulation, b_down[None]
    )


def solution(mesh):
    whole = jax.sharding.Mesh(mesh.devices.reshape(4, 4, 4, 2), ("y", "z", "x", "core"))
    placed = (
        P("y", SEQ, None),
        P("y", SEQ, None, None),
        P("y", SEQ, None, None),
        P("y", SEQ),
        P("y", SEQ),
        P("y", None, None),
        P(None, "y"),
        P("y"),
        P("y", None),
        P(),
    )
    return jax.shard_map(body, mesh=whole, in_specs=placed, out_specs=P("y", SEQ, None), check_vma=False)
```

time: 553 us -> 117 us (0.21)
  waiting for transfers between devices: 244 us -> 37.3 us
  blocking collectives: 128 us -> 13.9 us
  local copies, waits for them, and re-layouts: 73.4 us -> 13.3 us
  matrix products: 41.8 us -> 0 us
  other arithmetic: 38.4 us -> 2.4 us
  Pallas kernels: 0 us -> 24.2 us
  starting transfers between devices: 8.5 us -> 24.2 us
  between operations: 15.9 us -> 0.78 us
    unnamed x2 -> x0, blocking collectives: 114 us -> none
    unnamed x9 -> x0, waiting for transfers between devices: 97.8 us -> none
    pmax x1 -> x0, waiting for transfers between devices: 93.6 us -> none  [attend(): row_top = lax.pmax(local_top.reshape(total_rows, head_count), 'seq')]
    all_gather x1 -> x0, waiting for transfers between devices: 52.4 us -> none  [attend(): everyone = lax.all_gather(queries, 'seq', axis=0, tiled=True)]
    dot_general x13 -> x0, matrix products: 41.8 us -> none  [the longest x8 23.8 us: block_scores(): jnp.einsum('qhd,khd->qhk', query_block, key_heads, preferred_element_type...]
    all_gather x1 -> x0, other arithmetic: 32.7 us -> none  [attend(): everyone = lax.all_gather(queries, 'seq', axis=0, tiled=True)]
    all_to_all x0 -> x3, waiting for transfers between devices: none -> 30.6 us  [the longest x1 14.5 us: body(): parts = lax.all_to_all(parts, SEQ, 0, 0, tiled=True)]
    pallas_call x0 -> x6, Pallas kernels: none -> 24.2 us  [the longest x1 9.66 us: body(): call(attention_kernel, shape((32, SLOT_PAD, BLOCK), bf16), scratch=[pltpu...]
  transfers between devices with their start and end apart: 8 -> 7, of which waited for: 4 -> 5; matrix products, arithmetic and copies ran while one was open for 3% -> 3% of each run, Pallas kernels for 0% -> 1%
where the time goes in v1:
time: 117 us; the launch traced here: 116 us
  waiting for transfers between devices  37.3 us (32%)
  Pallas kernels  24.2 us (21%)
  starting transfers between devices  24.2 us (21%)
  blocking collectives  13.9 us (12%)
  local copies, waits for them, and re-layouts  13.3 us (11%)
  other arithmetic  2.4 us (2%)
    all_to_all x1, waiting for transfers between devices, body(): parts = lax.all_to_all(parts, SEQ, 0, 0, tiled=True)  14.5 us
    all_gather x1, blocking collectives, body(): normed_all = lax.all_gather(normed, 'y', axis=0, tiled=True)  13.9 us
    unnamed x18, local copies, waits for them, and re-layouts  11.1 us
    all_to_all x1, waiting for transfers between devices, body(): lax.all_to_all(terms.reshape(4, SLOT_PAD, width), 'y', 0, 0, tiled=True)  9.99 us
    pallas_call x1, Pallas kernels, body(): call(attention_kernel, shape((32, SLOT_PAD, BLOCK), bf16), scratch=[pltpu...  9.66 us
    pallas_call x1, Pallas kernels, feed_forward(): pl.pallas_call(feed_kernel, grid=(hidden_units // tile,), in_specs=[pl.Bl...  8.91 us
    all_to_all x1, starting transfers between devices, body(): q_all = lax.all_to_all(q_blocks, SEQ, 0, 0, tiled=True)  8.34 us
    ppermute x3, waiting for transfers between devices, body(): lax.ppermute(jnp.stack([keep[k], first[k]]), SEQ, ring_pairs(k))  6.67 us
  transfers between devices with their start and end apart: 7, of which 5 were waited for; matrix products, arithmetic and copies ran while one was open for 3% of the time, Pallas kernels for 1%

profile of v1, /device:TPU:0, one launch (start us, length us, event | category | flops | bytes accessed | tf_op | source)
XLA Modules:
  0.0 116.0 jit_solution(14517113261345159370)
XLA Ops:
  0.7 1.0 slice_bitcast_fusion.kv_new_ref
  1.7 0.1 stack.28.info_ref
  1.8 1.4 %copy-done.2 = bf16[1,128,2,3072]{3,2,1,0:T(2,128)(2,1)S(1)} copy-done((bf16[1,128,2,3072]{3,2,1,0:T(2,128)(2,1)S(1)}, bf16[1,128,2,3072]{3,2,1,0:T(2,128)(2,1)}, u32[]{:S(2)}) %copy-start.2) | copy-done | bytes 1572888
  3.2 0.7 copy-done.6
  3.9 1.6 %shard_map.101 = (bf16[4,2,128,384]{3,2,1,0:T(8,128)(2,1)S(1)}, bf16[4,2,128,384]{3,2,1,0:T(8,128)(2,1)S(1)}) custom-call(s32[5]{0:T(128)S(1)} %stack.28.info_ref, bf16[128,2,3072]{2,1,0:T(2,128)(2,1)S(1)} %bitcast.14, bf16[2,28,3072]{2,1,0:T(8,128)(2,1)S(1)} %slice_bitcast_fusion.kv_new_ref, s32[1,28]{1,0:T(1,128)S(1)} %copy-done.6), custom_call_target="tpu_custom_call" | custom-call | tf_op jit(solution)/shard_map/pallas_call | solution.py:235
  5.4 0.1 collective-permute-start
  5.5 0.9 slice_bitcast_fusion.1.q_ref
  6.5 1.0 shard_map.100
  7.5 8.3 %all-to-all-start = ((bf16[32,32,384]{2,1,0:T(8,128)(2,1)}), bf16[32,32,384]{2,1,0:T(8,128)(2,1)S(1)}, u32[]{:S(2)}, u32[]{:S(2)}) async-start(bf16[32,32,384]{2,1,0:T(8,128)(2,1)} %shard_map.100), calls=%async_computation | async-start | bytes 1572864 | tf_op jit(solution)/shard_map/all_to_all | solution.py:232
  15.8 0.1 fusion
  16.0 0.8 pad_maximum_fusion
  16.8 1.8 %collective-permute-start.1 = (bf16[2,2,128,384]{3,2,1,0:T(8,128)(2,1)}, bf16[2,2,128,384]{3,2,1,0:T(8,128)(2,1)S(1)}, u32[]{:S(2)}, u32[]{:S(2)}) collective-permute-start(bf16[2,2,128,384]{3,2,1,0:T(8,128)(2,1)} %pad_maximum_fusion), channel_id=1, source_target_pairs={{0,2},{1,9},{2,4},{3,11},{4,6},{5,13},{6,0},{7,15},{8,10},{9,17},{... | collective-permute-start | bytes 1179656 | tf_op jit(solution)/shard_map/ppermute | solution.py:244
  18.6 0.8 pad_maximum_fusion.1
  19.3 2.7 %collective-permute-start.2 = (bf16[2,2,128,384]{3,2,1,0:T(8,128)(2,1)}, bf16[2,2,128,384]{3,2,1,0:T(8,128)(2,1)S(1)}, u32[]{:S(2)}, u32[]{:S(2)}) collective-permute-start(bf16[2,2,128,384]{3,2,1,0:T(8,128)(2,1)} %pad_maximum_fusion.1), channel_id=1, source_target_pairs={{0,4},{1,17},{2,6},{3,19},{4,0},{5,21},{6,2},{7,23},{8,12},{9,25},... | collective-permute-start | bytes 1179656 | tf_op jit(solution)/shard_map/ppermute | solution.py:244
  22.0 0.8 pad_maximum_fusion.2
  22.8 1.5 %collective-permute-start.3 = (bf16[2,2,128,384]{3,2,1,0:T(8,128)(2,1)}, bf16[2,2,128,384]{3,2,1,0:T(8,128)(2,1)S(1)}, u32[]{:S(2)}, u32[]{:S(2)}) collective-permute-start(bf16[2,2,128,384]{3,2,1,0:T(8,128)(2,1)} %pad_maximum_fusion.2), channel_id=1, source_target_pairs={{0,6},{1,25},{2,0},{3,27},{4,2},{5,29},{6,4},{7,31},{8,14},{9,1},{... | collective-permute-start | bytes 1179656 | tf_op jit(solution)/shard_map/ppermute | solution.py:244
  24.3 6.1 %all-to-all-done.q_ref = bf16[32,32,384]{2,1,0:T(8,128)(2,1)S(1)} async-done(((bf16[32,32,384]{2,1,0:T(8,128)(2,1)}), bf16[32,32,384]{2,1,0:T(8,128)(2,1)S(1)}, u32[]{:S(2)}, u32[]{:S(2)}) %all-to-all-start) | async-done | bytes 786464 | tf_op jit(solution)/shard_map/all_to_all | solution.py:232
  30.4 2.2 %collective-permute-done.1.r1_ref = bf16[2,2,128,384]{3,2,1,0:T(8,128)(2,1)S(1)} collective-permute-done((bf16[2,2,128,384]{3,2,1,0:T(8,128)(2,1)}, bf16[2,2,128,384]{3,2,1,0:T(8,128)(2,1)S(1)}, u32[]{:S(2)}, u32[]{:S(2)}) %collective-permute-start.1) | collective-permute-done | bytes 393248 | tf_op jit(solution)/shard_map/ppermute | solution.py:244
  32.5 4.5 %collective-permute-done.2.r2_ref = bf16[2,2,128,384]{3,2,1,0:T(8,128)(2,1)S(1)} collective-permute-done((bf16[2,2,128,384]{3,2,1,0:T(8,128)(2,1)}, bf16[2,2,128,384]{3,2,1,0:T(8,128)(2,1)S(1)}, u32[]{:S(2)}, u32[]{:S(2)}) %collective-permute-start.2) | collective-permute-done | bytes 393248 | tf_op jit(solution)/shard_map/ppermute | solution.py:244
  37.1 9.7 %shard_map.102 = bf16[32,32,384]{2,1,0:T(8,128)(2,1)} custom-call(bf16[32,32,384]{2,1,0:T(8,128)(2,1)S(1)} %all-to-all-done.q_ref, bf16[4,2,128,384]{3,2,1,0:T(8,128)(2,1)S(1)} %get-tuple-element.9.keep_ref, bf16[4,2,128,384]{3,2,1,0:T(8,128)(2,1)S(1)} %collective-permute-done.first_ref, bf16[2,2,128,384]{3,2,1,0:T(8,128)(2,1)S(1)} %collective-permute-done.1.r1_ref, ...), custom_call_target="tpu_custom_call" | custom-call | tf_op jit(solution)/shard_map/pallas_call | solution.py:246
  46.7 5.3 %all-to-all-start.1 = ((bf16[32,32,384]{2,1,0:T(8,128)(2,1)}), bf16[32,32,384]{2,1,0:T(8,128)(2,1)S(1)}, u32[]{:S(2)}, u32[]{:S(2)}) async-start(bf16[32,32,384]{2,1,0:T(8,128)(2,1)} %shard_map.102), calls=%async_computation.1 | async-start | bytes 1572864 | tf_op jit(solution)/shard_map/all_to_all | solution.py:253
  52.1 14.5 %all-to-all-done.1.parts_ref = bf16[32,32,384]{2,1,0:T(8,128)(2,1)S(1)} async-done(((bf16[32,32,384]{2,1,0:T(8,128)(2,1)}), bf16[32,32,384]{2,1,0:T(8,128)(2,1)S(1)}, u32[]{:S(2)}, u32[]{:S(2)}) %all-to-all-start.1) | async-done | bytes 786464 | tf_op jit(solution)/shard_map/all_to_all | solution.py:253
  66.6 0.9 copy-done.3
  67.5 0.7 copy-done.4
  68.3 1.6 %shard_map.103 = (f32[32,3072]{1,0:T(8,128)S(1)}, bf16[32,3072]{1,0:T(8,128)(2,1)S(1)}) custom-call(s32[5]{0:T(128)S(1)} %stack.28.info_ref, bf16[32,32,384]{2,1,0:T(8,128)(2,1)S(1)} %all-to-all-done.1.parts_ref, bf16[1,28,3072]{2,1,0:T(8,128)(2,1)S(1)} %copy-done.3, bf16[1,4,3072]{2,1,0:T(4,128)(2,1)S(1)} %copy-done.4), custom_call_target="tpu_custom_call" | custom-call | tf_op jit(solution)/shard_map/pallas_call | solution.py:255
  69.9 13.9 %all_gather.3.rows_ref = bf16[128,3072]{1,0:T(8,128)(2,1)S(1)} all-gather(bf16[32,3072]{1,0:T(8,128)(2,1)S(1)} %get-tuple-element.11), channel_id=1, replica_groups=mesh['y'=4,'z'=4,'x'=4,'core'=2] {'y'}, dimensions={0}, use_global_device_ids=true | all-gather | bytes 983040 | tf_op jit(solution)/shard_map/all_gather | solution.py:263
  83.8 3.7 %copy-done = bf16[3072,1536]{1,0:T(8,128)(2,1)S(1)} copy-done((bf16[3072,1536]{1,0:T(8,128)(2,1)S(1)}, bf16[3072,1536]{1,0:T(8,128)(2,1)}, u32[]{:S(2)}) %copy-start) | copy-done | bytes 9437208
  87.5 3.7 %copy-done.1 = bf16[1536,3072]{1,0:T(8,128)(2,1)S(1)} copy-done((bf16[1536,3072]{1,0:T(8,128)(2,1)S(1)}, bf16[1536,3072]{1,0:T(8,128)(2,1)}, u32[]{:S(2)}) %copy-start.1) | copy-done | bytes 9437208
  91.1 8.9 %shard_map.104 = bf16[128,3072]{1,0:T(8,128)(2,1)} custom-call(bf16[128,3072]{1,0:T(8,128)(2,1)S(1)} %all_gather.3.rows_ref, bf16[3072,1536]{1,0:T(8,128)(2,1)S(1)} %copy-done, bf16[1,1536]{1,0:T(2,128)(2,1)S(1)} %broadcast_in_dim.6.b_up_ref, bf16[1536,3072]{1,0:T(8,128)(2,1)S(1)} %copy-done.1), custom_call_target="tpu_custom_call" | custom-call | tf_op jit(solution)/shard_map/pallas_call | solution.py:183
  100.1 4.6 %all-to-all-start.2 = ((bf16[4,32,3072]{2,1,0:T(8,128)(2,1)}), bf16[4,32,3072]{2,1,0:T(8,128)(2,1)S(1)}, u32[]{:S(2)}, u32[]{:S(2)}) async-start(bf16[4,32,3072]{2,1,0:T(8,128)(2,1)} %bitcast.9), calls=%async_computation.2 | async-start | bytes 1572864 | tf_op jit(solution)/shard_map/all_to_all | solution.py:265
  104.6 10.0 %all-to-all-done.2.terms_ref = bf16[4,32,3072]{2,1,0:T(8,128)(2,1)S(1)} async-done(((bf16[4,32,3072]{2,1,0:T(8,128)(2,1)}), bf16[4,32,3072]{2,1,0:T(8,128)(2,1)S(1)}, u32[]{:S(2)}, u32[]{:S(2)}) %all-to-all-start.2) | async-done | bytes 786464 | tf_op jit(solution)/shard_map/all_to_all | solution.py:265
  114.6 1.4 %shard_map.105 = bf16[1,28,3072]{2,1,0:T(8,128)(2,1)} custom-call(s32[5]{0:T(128)S(1)} %stack.28.info_ref, bf16[4,32,3072]{2,1,0:T(8,128)(2,1)S(1)} %all-to-all-done.2.terms_ref, f32[32,3072]{1,0:T(8,128)S(1)} %get-tuple-element.12.hidden_ref, bf16[1,4,3072]{2,1,0:T(4,128)(2,1)S(1)} %copy-done.5, bf16[1,3072]{1,0:T(2,128)(2,1)S(1)} %broadcast_in_dim.7.b_down_ref), custom_call_target="tpu_custom_call" | custom-call | tf_op jit(solution)/shard_map/pallas_call | solution.py:266
  (17 shorter events, 0.1 us)
Async XLA Ops:
  0.0 52.1 %copy-start.8 = (bf16[1536]{0:T(1024)(128)(2,1)S(1)}, bf16[1536]{0:T(1024)(128)(2,1)}, u32[]{:S(2)}) copy-start(bf16[1536]{0:T(1024)(128)(2,1)} %param.17) | copy-start | bytes 9220
  1.8 1.4 %copy-start.2 = (bf16[1,128,2,3072]{3,2,1,0:T(2,128)(2,1)S(1)}, bf16[1,128,2,3072]{3,2,1,0:T(2,128)(2,1)}, u32[]{:S(2)}) copy-start(bf16[1,128,2,3072]{3,2,1,0:T(2,128)(2,1)} %param.12) | copy-start | bytes 4718596
  3.2 0.7 copy-start.6
  5.4 10.4 %collective-permute-start = (bf16[4,2,128,384]{3,2,1,0:T(8,128)(2,1)S(1)}, bf16[4,2,128,384]{3,2,1,0:T(8,128)(2,1)S(1)}, u32[]{:S(2)}, u32[]{:S(2)}) collective-permute-start(bf16[4,2,128,384]{3,2,1,0:T(8,128)(2,1)S(1)} %get-tuple-element.10), channel_id=1, source_target_pairs={{0,1},{1,0},{2,3},{3,2},{4,5},{5,4},{6,7},{7,6},{8,9},{9,8},{10,11... | collective-permute-start | bytes 2359304 | tf_op jit(solution)/shard_map/ppermute | solution.py:243
  7.5 22.9 %all-to-all-start = ((bf16[32,32,384]{2,1,0:T(8,128)(2,1)}), bf16[32,32,384]{2,1,0:T(8,128)(2,1)S(1)}, u32[]{:S(2)}, u32[]{:S(2)}) async-start(bf16[32,32,384]{2,1,0:T(8,128)(2,1)} %shard_map.100), calls=%async_computation | async-start | bytes 1572864 | tf_op jit(solution)/shard_map/all_to_all | solution.py:232
  16.8 15.8 %collective-permute-start.1 = (bf16[2,2,128,384]{3,2,1,0:T(8,128)(2,1)}, bf16[2,2,128,384]{3,2,1,0:T(8,128)(2,1)S(1)}, u32[]{:S(2)}, u32[]{:S(2)}) collective-permute-start(bf16[2,2,128,384]{3,2,1,0:T(8,128)(2,1)} %pad_maximum_fusion), channel_id=1, source_target_pairs={{0,2},{1,9},{2,4},{3,11},{4,6},{5,13},{6,0},{7,15},{8,10},{9,17},{... | collective-permute-start | bytes 1179656 | tf_op jit(solution)/shard_map/ppermute | solution.py:244
  19.3 17.7 %collective-permute-start.2 = (bf16[2,2,128,384]{3,2,1,0:T(8,128)(2,1)}, bf16[2,2,128,384]{3,2,1,0:T(8,128)(2,1)S(1)}, u32[]{:S(2)}, u32[]{:S(2)}) collective-permute-start(bf16[2,2,128,384]{3,2,1,0:T(8,128)(2,1)} %pad_maximum_fusion.1), channel_id=1, source_target_pairs={{0,4},{1,17},{2,6},{3,19},{4,0},{5,21},{6,2},{7,23},{8,12},{9,25},... | collective-permute-start | bytes 1179656 | tf_op jit(solution)/shard_map/ppermute | solution.py:244
  22.8 14.2 %collective-permute-start.3 = (bf16[2,2,128,384]{3,2,1,0:T(8,128)(2,1)}, bf16[2,2,128,384]{3,2,1,0:T(8,128)(2,1)S(1)}, u32[]{:S(2)}, u32[]{:S(2)}) collective-permute-start(bf16[2,2,128,384]{3,2,1,0:T(8,128)(2,1)} %pad_maximum_fusion.2), channel_id=1, source_target_pairs={{0,6},{1,25},{2,0},{3,27},{4,2},{5,29},{6,4},{7,31},{8,14},{9,1},{... | collective-permute-start | bytes 1179656 | tf_op jit(solution)/shard_map/ppermute | solution.py:244
  46.7 19.9 %all-to-all-start.1 = ((bf16[32,32,384]{2,1,0:T(8,128)(2,1)}), bf16[32,32,384]{2,1,0:T(8,128)(2,1)S(1)}, u32[]{:S(2)}, u32[]{:S(2)}) async-start(bf16[32,32,384]{2,1,0:T(8,128)(2,1)} %shard_map.102), calls=%async_computation.1 | async-start | bytes 1572864 | tf_op jit(solution)/shard_map/all_to_all | solution.py:253
  66.6 0.9 copy-start.3
  67.5 0.7 copy-start.4
  83.8 3.7 %copy-start = (bf16[3072,1536]{1,0:T(8,128)(2,1)S(1)}, bf16[3072,1536]{1,0:T(8,128)(2,1)}, u32[]{:S(2)}) copy-start(bf16[3072,1536]{1,0:T(8,128)(2,1)} %up_ref.1) | copy-start | bytes 28311556
  87.5 3.7 %copy-start.1 = (bf16[1536,3072]{1,0:T(8,128)(2,1)S(1)}, bf16[1536,3072]{1,0:T(8,128)(2,1)}, u32[]{:S(2)}) copy-start(bf16[1536,3072]{1,0:T(8,128)(2,1)} %down_ref.1) | copy-start | bytes 28311556
  91.1 13.5 %copy-start.7 = (bf16[3072]{0:T(1024)(128)(2,1)S(1)}, bf16[3072]{0:T(1024)(128)(2,1)}, u32[]{:S(2)}) copy-start(bf16[3072]{0:T(1024)(128)(2,1)} %param.19) | copy-start | bytes 18436
  91.1 23.5 %copy-start.5 = (bf16[1,4,3072]{2,1,0:T(4,128)(2,1)S(1)}, bf16[1,4,3072]{2,1,0:T(4,128)(2,1)}, u32[]{:S(2)}) copy-start(bf16[1,4,3072]{2,1,0:T(4,128)(2,1)} %mod_ref.3) | copy-start | bytes 73732
  100.1 14.6 %all-to-all-start.2 = ((bf16[4,32,3072]{2,1,0:T(8,128)(2,1)}), bf16[4,32,3072]{2,1,0:T(8,128)(2,1)S(1)}, u32[]{:S(2)}, u32[]{:S(2)}) async-start(bf16[4,32,3072]{2,1,0:T(8,128)(2,1)} %bitcast.9), calls=%async_computation.2 | async-start | bytes 1572864 | tf_op jit(solution)/shard_map/all_to_all | solution.py:265

commit v2 on v1

--- a/solution.py
+++ b/solution.py
@@ -18,23 +18,31 @@
 MB = 1 << 20
 
 
-def call(kernel, out_shape, scratch=(), limit=16, smem=(), n_in=None, cost=None, **kw):
-    specs = [
-        pl.BlockSpec(memory_space=pltpu.SMEM if i in smem else pltpu.VMEM) for i in range(n_in)
-    ]
+def call(kernel, out_shape, scratch=(), limit=16, smem=(), hbm=(), n_in=None, us=1.0):
+    def space(i):
+        return pltpu.SMEM if i in smem else pltpu.HBM if i in hbm else pltpu.VMEM
+
     return pl.pallas_call(
         kernel,
         out_shape=out_shape,
-        in_specs=specs,
+        in_specs=[pl.BlockSpec(memory_space=space(i)) for i in range(n_in)],
         scratch_shapes=list(scratch),
         compiler_params=pltpu.CompilerParams(vmem_limit_bytes=limit * MB),
-        cost_estimate=cost,
-        **kw,
+        cost_estimate=pl.CostEstimate(flops=0, transcendentals=0, bytes_accessed=int(us * 3.3e6)),
     )
 
 
-def pack_queries_kernel(q_ref, out_ref):
+def fetch(pairs, sems):
+    copies = [pltpu.make_async_copy(src, dst, sems.at[i]) for i, (src, dst) in enumerate(pairs)]
+    for copy in copies:
+        copy.start()
+    for copy in copies:
+        copy.wait()
+
+
+def pack_queries_kernel(fresh_ref, out_ref, q_ref, sems):
     rows = q_ref.shape[0]
+    fetch([(fresh_ref.at[0], q_ref)], sems)
     for dest in range(32):
         z, x, core = dest // 8, dest // 2 % 4, dest % 2
         group = x if core == 0 else 4 + z
@@ -42,7 +50,10 @@
         out_ref[dest, rows:, :] = jnp.zeros((SLOT_PAD - rows, BLOCK), bf16)
 
 
-def pack_cache_kernel(info_ref, kv_ref, kv_new_ref, chosen_ref, keep_ref, send_ref, patched):
+def pack_cache_kernel(
+    info_ref, kv_hbm, fresh_ref, chosen_ref, after_ref, keep_ref, send_ref, kv_ref, kv_new_ref, patched, sems
+):
+    fetch([(kv_hbm, kv_ref), (fresh_ref.at[1:3], kv_new_ref)], sems)
     tokens = kv_ref.shape[0]
     slots = kv_new_ref.shape[1]
     core, ring_x, ring_z, count = info_ref[0], info_ref[1], info_ref[2], info_ref[3]
@@ -67,17 +78,21 @@
             send_ref[k, which] = patched[which, :, pl.ds(at_other, BLOCK)]
 
 
-def attention_kernel(q_ref, keep_ref, first_ref, r1_ref, r2_ref, r3_ref, out_ref, keys, values_t):
-    sources = [keep_ref.at[0], first_ref.at[0]]
-    for ref in (r1_ref, r2_ref, r3_ref):
-        sources += [ref.at[0], ref.at[1]]
+def stack_kernel(keep_ref, first_ref, *out_refs):
+    for k, out_ref in enumerate(out_refs):
+        out_ref[0] = keep_ref[k]
+        out_ref[1] = first_ref[k]
+
+
+def attention_kernel(q_ref, r0_ref, r1_ref, r2_ref, r3_ref, out_ref, keys, values_t):
+    sources = [ref.at[core] for ref in (r0_ref, r1_ref, r2_ref, r3_ref) for core in range(2)]
     for i, ref in enumerate(sources):
         keys[i * 128 : (i + 1) * 128, :] = ref[0]
         for h in range(HEADS_HERE):
             cols = slice(h * HEAD_DIM, (h + 1) * HEAD_DIM)
             values_t[h, :, i * 128 : (i + 1) * 128] = ref[1, :, cols].T
     scale = LOG2E * HEAD_DIM**-0.5
-    tile = 256
+    tile = 1024
     blocks = tile // SLOT_PAD
 
     def step(t, _):
@@ -112,8 +127,16 @@
     lax.fori_loop(0, q_ref.shape[0] // blocks, step, 0)
 
 
-def combine_kernel(info_ref, parts_ref, rows_ref, mod_ref, hidden_ref, normed_ref, levels, turned):
+def combine_kernel(
+    info_ref, parts_ref, rows_hbm, mod_hbm, hidden_ref, normed_ref, levels, turned, rows_ref, mod_ref, sems
+):
     slots = rows_ref.shape[1]
+    copies = [
+        pltpu.make_async_copy(rows_hbm, rows_ref, sems.at[0]),
+        pltpu.make_async_copy(mod_hbm, mod_ref, sems.at[1]),
+    ]
+    for copy in copies:
+        copy.start()
     heads = 24
 
     def source(part, group):
@@ -135,8 +158,9 @@
     levels[4 * heads :, :] = jnp.zeros((128 - 4 * heads, 128), f32)
     turned[...] = levels[...].T
     mine = turned[pl.ds(pl.multiple_of(info_ref[4] * SLOT_PAD, SLOT_PAD), SLOT_PAD), :]
+    for copy in copies:
+        copy.wait()
     shifts = mod_ref[0].astype(f32)
-    total_sum = jnp.zeros((SLOT_PAD, 1), f32)
     for group in range(8):
         for h in range(HEADS_HERE):
             head = group * HEADS_HERE + h
@@ -156,51 +180,44 @@
     normed_ref[...] = normed.astype(bf16)
 
 
-def feed_kernel(rows_ref, up_ref, b_up_ref, down_ref, out_ref, acc):
-    step = pl.program_id(0)
-    lifted = jnp.dot(rows_ref[...], up_ref[...], preferred_element_type=f32)
-    lifted = lifted + b_up_ref[...].astype(f32)
-    active = jax.nn.gelu(lifted, approximate=True).astype(bf16)
-    terms = jnp.dot(active, down_ref[...], preferred_element_type=f32)
-
-    @pl.when(step == 0)
-    def _():
-        acc[...] = terms
-
-    @pl.when(step > 0)
-    def _():
-        acc[...] = acc[...] + terms
-
-    @pl.when(step == pl.num_programs(0) - 1)
-    def _():
-        out_ref[...] = acc[...].astype(bf16)
-
-
-def feed_forward(rows, w_up, b_up, w_down):
-    count, width = rows.shape
-    hidden_units = w_up.shape[1]
-    tile = 256
-    return pl.pallas_call(
-        feed_kernel,
-        grid=(hidden_units // tile,),
-        in_specs=[
-            pl.BlockSpec((count, width), lambda i: (0, 0)),
-            pl.BlockSpec((width, tile), lambda i: (0, i)),
-            pl.BlockSpec((1, tile), lambda i: (0, i)),
-            pl.BlockSpec((tile, width), lambda i: (i, 0)),
-        ],
-        out_specs=pl.BlockSpec((count, width), lambda i: (0, 0)),
-        out_shape=jax.ShapeDtypeStruct((count, width), bf16),
-        scratch_shapes=[pltpu.VMEM((count, width), f32)],
-        compiler_params=pltpu.CompilerParams(vmem_limit_bytes=24 * MB),
-    )(rows, w_up, b_up, w_down)
-
-
-def finish_kernel(info_ref, terms_ref, hidden_ref, mod_ref, b_down_ref, out_ref):
+def load_kernel(after_ref, weight, out_ref, sems):
+    fetch([(weight, out_ref)], sems)
+
+
+def load(after, weight, limit):
+    return call(
+        load_kernel,
+        jax.ShapeDtypeStruct(weight.shape, bf16),
+        scratch=[pltpu.SemaphoreType.DMA((1,))],
+        n_in=2,
+        hbm=(0, 1),
+        limit=limit,
+        us=3.6,
+    )(after, weight)
+
+
+def feed_kernel(r0_ref, r1_ref, r2_ref, r3_ref, up_ref, b_up_ref, down_ref, o0, o1, o2, o3, rows_ref, active):
+    chunk = 512
+    for i, ref in enumerate((r0_ref, r1_ref, r2_ref, r3_ref)):
+        rows_ref[i * SLOT_PAD : (i + 1) * SLOT_PAD, :] = ref[...]
+    rows = rows_ref[...]
+    for start in range(0, up_ref.shape[1], chunk):
+        cols = slice(start, start + chunk)
+        lifted = jnp.dot(rows, up_ref[:, cols], preferred_element_type=f32)
+        lifted = lifted + b_up_ref[:, cols].astype(f32)
+        active[:, cols] = jax.nn.gelu(lifted, approximate=True).astype(bf16)
+    for start in range(0, down_ref.shape[1], chunk):
+        cols = slice(start, start + chunk)
+        terms = jnp.dot(active[...], down_ref[:, cols], preferred_element_type=f32)
+        for i, out_ref in enumerate((o0, o1, o2, o3)):
+            out_ref[:, cols] = terms[i * SLOT_PAD : (i + 1) * SLOT_PAD].astype(bf16)
+
+
+def finish_kernel(info_ref, t0_ref, t1_ref, t2_ref, t3_ref, hidden_ref, mod_ref, b_down_ref, out_ref):
     slots = out_ref.shape[1]
-    total = terms_ref[0].astype(f32)
-    for p in range(1, 4):
-        total = total + terms_ref[p].astype(f32)
+    total = t0_ref[...].astype(f32)
+    for ref in (t1_ref, t2_ref, t3_ref):
+        total = total + ref[...].astype(f32)
     feed_out = total[:slots] + b_down_ref[...].astype(f32)
     result = hidden_ref[:slots] + mod_ref[0, 3:4].astype(f32) * feed_out
     live = lax.broadcasted_iota(i32, result.shape, 0) < info_ref[3]
@@ -220,6 +237,10 @@
     ]
 
 
+def turn(k):
+    return [(y, (y + k) % 4) for y in range(4)]
+
+
 def body(rows_in, fresh_qkv, kv_cache, chosen, counts, modulation, w_up, b_up, w_down, b_down):
     shape = jax.ShapeDtypeStruct
     slots, width = rows_in.shape[1], rows_in.shape[2]
@@ -228,43 +249,76 @@
     me = ring_z * 8 + ring_x * 2 + core
     info = jnp.stack([core, ring_x, ring_z, counts[0, 0], me % 4]).astype(i32)
 
-    q_blocks = call(pack_queries_kernel, shape((32, SLOT_PAD, BLOCK), bf16), n_in=1)(fresh_qkv[0, :, 0])
+    fresh = jnp.swapaxes(fresh_qkv[0], 0, 1)
+    q_blocks = call(
+        pack_queries_kernel,
+        shape((32, SLOT_PAD, BLOCK), bf16),
+        scratch=[pltpu.VMEM((slots, width), bf16), pltpu.SemaphoreType.DMA((1,))],
+        n_in=1,
+        hbm=(0,),
+        limit=61,
+    )(fresh)
     q_all = lax.all_to_all(q_blocks, SEQ, 0, 0, tiled=True)
 
-    kv_new = jnp.swapaxes(fresh_qkv[0, :, 1:3], 0, 1)
     keep, send = call(
         pack_cache_kernel,
         [shape((4, 2, tokens, BLOCK), bf16)] * 2,
-        scratch=[pltpu.VMEM((2, tokens, width), bf16)],
-        n_in=4,
+        scratch=[
+            pltpu.VMEM((tokens, 2, width), bf16),
+            pltpu.VMEM((2, slots, width), bf16),
+            pltpu.VMEM((2, tokens, width), bf16),
+            pltpu.SemaphoreType.DMA((2,)),
+        ],
+        n_in=5,
         smem=(0,),
-    )(info, kv_cache[0], kv_new, chosen)
+        hbm=(1, 2, 4),
+        limit=61,
+        us=3.0,
+    )(info, kv_cache[0], fresh, chosen, q_blocks)
     swap = [(position(z, x, c), position(z, x, 1 - c)) for z in range(4) for x in range(4) for c in range(2)]
     first = lax.ppermute(send, SEQ, swap)
-    others = [lax.ppermute(jnp.stack([keep[k], first[k]]), SEQ, ring_pairs(k)) for k in (1, 2, 3)]
-
-    parts = call(
+    stacked = call(stack_kernel, [shape((2, 2, tokens, BLOCK), bf16)] * 4, n_in=2)(keep, first)
+    others = [lax.ppermute(stacked[k], SEQ, ring_pairs(k)) for k in (1, 2, 3)]
+
+    partial = call(
         attention_kernel,
         shape((32, SLOT_PAD, BLOCK), bf16),
         scratch=[pltpu.VMEM((8 * tokens, BLOCK), bf16), pltpu.VMEM((HEADS_HERE, HEAD_DIM, 8 * tokens), bf16)],
-        n_in=6,
+        n_in=5,
         limit=24,
-    )(q_all, keep, first, *others)
-    parts = lax.all_to_all(parts, SEQ, 0, 0, tiled=True)
-
+        us=6.5,
+    )(q_all, stacked[0], *others)
+    parts = lax.all_to_all(partial, SEQ, 0, 0, tiled=True)
     hidden, normed = call(
         combine_kernel,
         [shape((SLOT_PAD, width), f32), shape((SLOT_PAD, width), bf16)],
-        scratch=[pltpu.VMEM((128, 128), f32), pltpu.VMEM((128, 128), f32)],
+        scratch=[
+            pltpu.VMEM((128, 128), f32),
+            pltpu.VMEM((128, 128), f32),
+            pltpu.VMEM(rows_in.shape, bf16),
+            pltpu.VMEM(modulation.shape, bf16),
+            pltpu.SemaphoreType.DMA((2,)),
+        ],
         n_in=4,
         smem=(0,),
+        hbm=(2, 3),
+        limit=60,
+        us=1.6,
     )(info, parts, rows_in, modulation)
 
-    normed_all = lax.all_gather(normed, "y", axis=0, tiled=True)
-    terms = feed_forward(normed_all, w_up, b_up[None], w_down)
-    terms = lax.all_to_all(terms.reshape(4, SLOT_PAD, width), "y", 0, 0, tiled=True)
-    return call(finish_kernel, shape((1, slots, width), bf16), n_in=5, smem=(0,))(
-        info, terms, hidden, modulation, b_down[None]
+    visits = [lax.ppermute(normed, "y", turn(k)) for k in (1, 2, 3)]
+    up = load(normed, w_up, 44)
+    down = load(normed, w_down, 36)
+    terms = call(
+        feed_kernel,
+        [shape((SLOT_PAD, width), bf16)] * 4,
+        scratch=[pltpu.VMEM((4 * SLOT_PAD, width), bf16), pltpu.VMEM((4 * SLOT_PAD, w_up.shape[1]), bf16)],
+        n_in=7,
+        us=3.7,
+    )(normed, *visits, up, b_up[None], down)
+    back = [lax.ppermute(terms[k], "y", turn(-k)) for k in (1, 2, 3)]
+    return call(finish_kernel, shape((1, slots, width), bf16), n_in=8, smem=(0,), us=1.4)(
+        info, terms[0], *back, hidden, modulation, b_down[None]
     )
 
 

time: 117 us -> 98.8 us (0.84)
  waiting for transfers between devices: 37.3 us -> 24.2 us
  local copies, waits for them, and re-layouts: 13.3 us -> 2.78 us
  blocking collectives: 13.9 us -> 19.8 us
  other arithmetic: 2.4 us -> 0 us
  Pallas kernels: 24.2 us -> 26.2 us
    all_to_all x2 -> x0, waiting for transfers between devices: 24.5 us -> none  [the longest x1 14.5 us: body(): parts = lax.all_to_all(parts, SEQ, 0, 0, tiled=True)]
    all_to_all x0 -> x1, blocking collectives: none -> 19.8 us  [body(): parts = lax.all_to_all(partial, SEQ, 0, 0, tiled=True)]
    all_gather x1 -> x0, blocking collectives: 13.9 us -> none  [body(): normed_all = lax.all_gather(normed, 'y', axis=0, tiled=True)]
    ppermute x3 -> x9, waiting for transfers between devices: 6.67 us -> 16.9 us  [the longest x3 10.2 us: body(): back = [lax.ppermute(terms[k], 'y', turn(-k)) for k in (1, 2, 3)]]
    all_to_all x2 -> x0, starting transfers between devices: 9.89 us -> none  [the longest x1 5.34 us: body(): parts = lax.all_to_all(parts, SEQ, 0, 0, tiled=True)]
    ppermute x3 -> x9, starting transfers between devices: 5.93 us -> 15.3 us  [the longest x3 6 us: body(): others = [lax.ppermute(stacked[k], SEQ, ring_pairs(k)) for k in (1, 2, 3)]]
    unnamed x18 -> x16, local copies, waits for them, and re-layouts: 11.1 us -> 2.1 us
    pallas_call x1, Pallas kernels: 9.66 us -> 4.65 us  [body(): call(attention_kernel, shape((32, SLOT_PAD, BLOCK), bf16), scratch=[pltpu...]
  transfers between devices with their start and end apart: 7 -> 11, of which waited for: 5 -> 6; matrix products, arithmetic and copies ran while one was open for 3% -> 0% of each run, Pallas kernels for 1% -> 8%
where the time goes in v2:
time: 98.8 us; the launch traced here: 97.5 us
  Pallas kernels  26.2 us (27%)
  waiting for transfers between devices  24.2 us (24%)
  starting transfers between devices  23.7 us (24%)
  blocking collectives  19.8 us (20%)
  local copies, waits for them, and re-layouts  2.78 us (3%)
    all_to_all x1, blocking collectives, body(): parts = lax.all_to_all(partial, SEQ, 0, 0, tiled=True)  19.8 us
    ppermute x3, waiting for transfers between devices, body(): back = [lax.ppermute(terms[k], 'y', turn(-k)) for k in (1, 2, 3)]  10.2 us
    all_to_all x1, starting transfers between devices, body(): q_all = lax.all_to_all(q_blocks, SEQ, 0, 0, tiled=True)  8.35 us
    pallas_call x2, Pallas kernels, load(): call(load_kernel, jax.ShapeDtypeStruct(weight.shape, bf16), scratch=[pltp...  7.42 us
    all_to_all x1, waiting for transfers between devices, body(): q_all = lax.all_to_all(q_blocks, SEQ, 0, 0, tiled=True)  7.29 us
    ppermute x3, waiting for transfers between devices, body(): others = [lax.ppermute(stacked[k], SEQ, ring_pairs(k)) for k in (1, 2, 3)]  6.67 us
    ppermute x3, starting transfers between devices, body(): others = [lax.ppermute(stacked[k], SEQ, ring_pairs(k)) for k in (1, 2, 3)]  6 us
    ppermute x3, starting transfers between devices, body(): visits = [lax.ppermute(normed, 'y', turn(k)) for k in (1, 2, 3)]  5.91 us
  transfers between devices with their start and end apart: 11, of which 6 were waited for; matrix products, arithmetic and copies ran while one was open for 0% of the time, Pallas kernels for 8%

profile of v2, /device:TPU:0, one launch (start us, length us, event | category | flops | bytes accessed | tf_op | source)
XLA Modules:
  0.0 97.5 jit_solution(48529244130319418)
XLA Ops:
  0.7 1.9 %shard_map.100.after_ref = bf16[32,32,384]{2,1,0:T(8,128)(2,1)} custom-call(bf16[3,28,3072]{2,1,0:T(8,128)(2,1)} %bitcast.10), custom_call_target="tpu_custom_call" | custom-call | bytes 3300000 | tf_op jit(solution)/shard_map/pallas_call | solution.py:253
  2.6 0.7 stack.19.info_ref
  3.3 4.3 %shard_map.101 = (bf16[4,2,128,384]{3,2,1,0:T(8,128)(2,1)}, bf16[4,2,128,384]{3,2,1,0:T(8,128)(2,1)}) custom-call(s32[5]{0:T(128)} %stack.19.info_ref, bf16[128,2,3072]{2,1,0:T(2,128)(2,1)} %bitcast.12, bf16[3,28,3072]{2,1,0:T(8,128)(2,1)} %bitcast.11, s32[1,28]{1,0:T(1,128)} %chosen_ref.1, bf16[32,32,384]{2,1,0:T(8,128)(2,1)} %shard_map.100.after_ref), custom_call_target="tpu_custom_call" | custom-call | bytes 9900000 | tf_op jit(solution)/shard_map/pallas_call | solution.py:263
  7.5 0.1 collective-permute-start
  7.6 8.4 %all-to-all-start = ((bf16[32,32,384]{2,1,0:T(8,128)(2,1)}), bf16[32,32,384]{2,1,0:T(8,128)(2,1)S(1)}, u32[]{:S(2)}, u32[]{:S(2)}) async-start(bf16[32,32,384]{2,1,0:T(8,128)(2,1)} %shard_map.100.after_ref), calls=%async_computation | async-start | bytes 1572864 | tf_op jit(solution)/shard_map/all_to_all | solution.py:261
  16.0 1.1 %copy-done.2 = bf16[4,2,128,384]{3,2,1,0:T(8,128)(2,1)S(1)} copy-done((bf16[4,2,128,384]{3,2,1,0:T(8,128)(2,1)S(1)}, bf16[4,2,128,384]{3,2,1,0:T(8,128)(2,1)}, u32[]{:S(2)}) %copy-start.2) | copy-done | bytes 786456
  17.1 0.1 shard_map.102
  17.3 1.9 %collective-permute-start.1 = (bf16[2,2,128,384]{3,2,1,0:T(8,128)(2,1)S(1)}, bf16[2,2,128,384]{3,2,1,0:T(8,128)(2,1)S(1)}, u32[]{:S(2)}, u32[]{:S(2)}) collective-permute-start(bf16[2,2,128,384]{3,2,1,0:T(8,128)(2,1)S(1)} %get-tuple-element.20), channel_id=1, source_target_pairs={{0,2},{1,9},{2,4},{3,11},{4,6},{5,13},{6,0},{7,15},{8,10},{9,17},{... | collective-permute-start | bytes 1179656 | tf_op jit(solution)/shard_map/ppermute | solution.py:281
  19.1 2.7 %collective-permute-start.2 = (bf16[2,2,128,384]{3,2,1,0:T(8,128)(2,1)S(1)}, bf16[2,2,128,384]{3,2,1,0:T(8,128)(2,1)S(1)}, u32[]{:S(2)}, u32[]{:S(2)}) collective-permute-start(bf16[2,2,128,384]{3,2,1,0:T(8,128)(2,1)S(1)} %get-tuple-element.21), channel_id=1, source_target_pairs={{0,4},{1,17},{2,6},{3,19},{4,0},{5,21},{6,2},{7,23},{8,12},{9,25},... | collective-permute-start | bytes 1179656 | tf_op jit(solution)/shard_map/ppermute | solution.py:281
  21.8 1.5 %collective-permute-start.3 = (bf16[2,2,128,384]{3,2,1,0:T(8,128)(2,1)S(1)}, bf16[2,2,128,384]{3,2,1,0:T(8,128)(2,1)S(1)}, u32[]{:S(2)}, u32[]{:S(2)}) collective-permute-start(bf16[2,2,128,384]{3,2,1,0:T(8,128)(2,1)S(1)} %get-tuple-element.22), channel_id=1, source_target_pairs={{0,6},{1,25},{2,0},{3,27},{4,2},{5,29},{6,4},{7,31},{8,14},{9,1},{... | collective-permute-start | bytes 1179656 | tf_op jit(solution)/shard_map/ppermute | solution.py:281
  23.3 7.3 %all-to-all-done.q_ref = bf16[32,32,384]{2,1,0:T(8,128)(2,1)S(1)} async-done(((bf16[32,32,384]{2,1,0:T(8,128)(2,1)}), bf16[32,32,384]{2,1,0:T(8,128)(2,1)S(1)}, u32[]{:S(2)}, u32[]{:S(2)}) %all-to-all-start) | async-done | bytes 786464 | tf_op jit(solution)/shard_map/all_to_all | solution.py:261
  30.6 2.2 %collective-permute-done.1.r1_ref = bf16[2,2,128,384]{3,2,1,0:T(8,128)(2,1)S(1)} collective-permute-done((bf16[2,2,128,384]{3,2,1,0:T(8,128)(2,1)S(1)}, bf16[2,2,128,384]{3,2,1,0:T(8,128)(2,1)S(1)}, u32[]{:S(2)}, u32[]{:S(2)}) %collective-permute-start.1) | collective-permute-done | bytes 393248 | tf_op jit(solution)/shard_map/ppermute | solution.py:281
  32.7 4.5 %collective-permute-done.2.r2_ref = bf16[2,2,128,384]{3,2,1,0:T(8,128)(2,1)S(1)} collective-permute-done((bf16[2,2,128,384]{3,2,1,0:T(8,128)(2,1)S(1)}, bf16[2,2,128,384]{3,2,1,0:T(8,128)(2,1)S(1)}, u32[]{:S(2)}, u32[]{:S(2)}) %collective-permute-start.2) | collective-permute-done | bytes 393248 | tf_op jit(solution)/shard_map/ppermute | solution.py:281
  37.2 4.6 %shard_map.103 = bf16[32,32,384]{2,1,0:T(8,128)(2,1)S(1)} custom-call(bf16[32,32,384]{2,1,0:T(8,128)(2,1)S(1)} %all-to-all-done.q_ref, bf16[2,2,128,384]{3,2,1,0:T(8,128)(2,1)S(1)} %get-tuple-element.19.r0_ref, bf16[2,2,128,384]{3,2,1,0:T(8,128)(2,1)S(1)} %collective-permute-done.1.r1_ref, bf16[2,2,128,384]{3,2,1,0:T(8,128)(2,1)S(1)} %collective-permute-done.2.r2_ref, ...), custom_call_target="tpu_custom_call" | custom-call | bytes 21450000 | tf_op jit(solution)/shard_map/pallas_call | solution.py:283
  41.9 19.8 %all_to_all.10.parts_ref = bf16[32,32,384]{2,1,0:T(8,128)(2,1)} all-to-all(bf16[32,32,384]{2,1,0:T(8,128)(2,1)S(1)} %shard_map.103), channel_id=1, replica_groups=mesh['y'=4,'z'=4,'x'=4,'core'=2] {'z','x','core'}, dimensions={0} | all-to-all | bytes 1572864 | tf_op jit(solution)/shard_map/all_to_all | solution.py:291
  61.7 3.6 %shard_map.104 = (f32[32,3072]{1,0:T(8,128)}, bf16[32,3072]{1,0:T(8,128)(2,1)}) custom-call(s32[5]{0:T(128)} %stack.19.info_ref, bf16[32,32,384]{2,1,0:T(8,128)(2,1)} %all_to_all.10.parts_ref, bf16[1,28,3072]{2,1,0:T(8,128)(2,1)} %rows_hbm.1, bf16[1,4,3072]{2,1,0:T(4,128)(2,1)} %mod_ref.1), custom_call_target="tpu_custom_call" | custom-call | bytes 5280000 | tf_op jit(solution)/shard_map/pallas_call | solution.py:292
  65.3 1.6 %collective-permute-start.4 = (bf16[32,3072]{1,0:T(8,128)(2,1)}, bf16[32,3072]{1,0:T(8,128)(2,1)S(1)}, u32[]{:S(2)}, u32[]{:S(2)}) collective-permute-start(bf16[32,3072]{1,0:T(8,128)(2,1)} %get-tuple-element.23.after_ref.r0_ref), channel_id=1, source_target_pairs={{0,32},{32,64},{64,96},{96,0},{1,33},{33,65},{65,97},{97,1},{2,34}... | collective-permute-start | bytes 589832 | tf_op jit(solution)/shard_map/ppermute | solution.py:309
  67.0 2.9 %collective-permute-start.5 = (bf16[32,3072]{1,0:T(8,128)(2,1)}, bf16[32,3072]{1,0:T(8,128)(2,1)S(1)}, u32[]{:S(2)}, u32[]{:S(2)}) collective-permute-start(bf16[32,3072]{1,0:T(8,128)(2,1)} %get-tuple-element.23.after_ref.r0_ref), channel_id=1, source_target_pairs={{0,64},{32,96},{64,0},{96,32},{1,65},{33,97},{65,1},{97,33},{2,66}... | collective-permute-start | bytes 589832 | tf_op jit(solution)/shard_map/ppermute | solution.py:309
  69.9 1.3 %collective-permute-start.6 = (bf16[32,3072]{1,0:T(8,128)(2,1)}, bf16[32,3072]{1,0:T(8,128)(2,1)S(1)}, u32[]{:S(2)}, u32[]{:S(2)}) collective-permute-start(bf16[32,3072]{1,0:T(8,128)(2,1)} %get-tuple-element.23.after_ref.r0_ref), channel_id=1, source_target_pairs={{0,96},{32,0},{64,32},{96,64},{1,97},{33,1},{65,33},{97,65},{2,98}... | collective-permute-start | bytes 589832 | tf_op jit(solution)/shard_map/ppermute | solution.py:309
  71.2 0.0 copy-start
  71.2 0.9 copy-done
  72.2 3.7 %shard_map.105.up_ref = bf16[3072,1536]{1,0:T(8,128)(2,1)S(1)} custom-call(bf16[32,3072]{1,0:T(8,128)(2,1)S(1)} %copy-done, bf16[3072,1536]{1,0:T(8,128)(2,1)} %weight.2), custom_call_target="tpu_custom_call" | custom-call | bytes 11880000 | tf_op jit(solution)/shard_map/pallas_call | solution.py:188
  75.9 3.7 %shard_map.106.down_ref = bf16[1536,3072]{1,0:T(8,128)(2,1)S(1)} custom-call(bf16[32,3072]{1,0:T(8,128)(2,1)S(1)} %copy-done.1, bf16[1536,3072]{1,0:T(8,128)(2,1)} %weight.3), custom_call_target="tpu_custom_call" | custom-call | bytes 11880000 | tf_op jit(solution)/shard_map/pallas_call | solution.py:188
  79.6 0.0 copy-start.4
  79.7 2.7 %shard_map.107 = (bf16[32,3072]{1,0:T(8,128)(2,1)S(1)}, bf16[32,3072]{1,0:T(8,128)(2,1)S(1)}, bf16[32,3072]{1,0:T(8,128)(2,1)S(1)}, bf16[32,3072]{1,0:T(8,128)(2,1)S(1)}) custom-call(bf16[32,3072]{1,0:T(8,128)(2,1)S(1)} %copy-done.1, bf16[32,3072]{1,0:T(8,128)(2,1)S(1)} %collective-permute-done.4.r1_ref, bf16[32,3072]{1,0:T(8,128)(2,1)S(1)} %collective-permute-done.5.r2_ref, ...), custom_call_target="tpu_custom_call" | custom-call | bytes 12210000 | tf_op jit(solution)/shard_map/pallas_call | solution.py:312
  82.4 1.5 %collective-permute-start.7 = (bf16[32,3072]{1,0:T(8,128)(2,1)S(1)}, bf16[32,3072]{1,0:T(8,128)(2,1)S(1)}, u32[]{:S(2)}, u32[]{:S(2)}) collective-permute-start(bf16[32,3072]{1,0:T(8,128)(2,1)S(1)} %get-tuple-element.25), channel_id=1, source_target_pairs={{0,96},{32,0},{64,32},{96,64},{1,97},{33,1},{65,33},{97,65},{2,98}... | collective-permute-start | bytes 589832 | tf_op jit(solution)/shard_map/ppermute | solution.py:319
  84.0 1.3 %collective-permute-start.8 = (bf16[32,3072]{1,0:T(8,128)(2,1)S(1)}, bf16[32,3072]{1,0:T(8,128)(2,1)S(1)}, u32[]{:S(2)}, u32[]{:S(2)}) collective-permute-start(bf16[32,3072]{1,0:T(8,128)(2,1)S(1)} %get-tuple-element.26), channel_id=1, source_target_pairs={{0,64},{32,96},{64,0},{96,32},{1,65},{33,97},{65,1},{97,33},{2,66}... | collective-permute-start | bytes 589832 | tf_op jit(solution)/shard_map/ppermute | solution.py:319
  85.3 0.6 collective-permute-start.9
  85.8 6.6 %collective-permute-done.7.t1_ref = bf16[32,3072]{1,0:T(8,128)(2,1)S(1)} collective-permute-done((bf16[32,3072]{1,0:T(8,128)(2,1)S(1)}, bf16[32,3072]{1,0:T(8,128)(2,1)S(1)}, u32[]{:S(2)}, u32[]{:S(2)}) %collective-permute-start.7) | collective-permute-done | bytes 196640 | tf_op jit(solution)/shard_map/ppermute | solution.py:319
  92.5 0.8 collective-permute-done.8.t2_ref
  93.3 2.7 %collective-permute-done.9.t3_ref = bf16[32,3072]{1,0:T(8,128)(2,1)S(1)} collective-permute-done((bf16[32,3072]{1,0:T(8,128)(2,1)S(1)}, bf16[32,3072]{1,0:T(8,128)(2,1)S(1)}, u32[]{:S(2)}, u32[]{:S(2)}) %collective-permute-start.9) | collective-permute-done | bytes 196640 | tf_op jit(solution)/shard_map/ppermute | solution.py:319
  96.1 1.4 %shard_map.108 = bf16[1,28,3072]{2,1,0:T(8,128)(2,1)} custom-call(s32[5]{0:T(128)S(1)} %copy-done.5, bf16[32,3072]{1,0:T(8,128)(2,1)S(1)} %get-tuple-element.24.t0_ref, bf16[32,3072]{1,0:T(8,128)(2,1)S(1)} %collective-permute-done.7.t1_ref, bf16[32,3072]{1,0:T(8,128)(2,1)S(1)} %collective-permute-done.8.t2_ref, ...), custom_call_target="tpu_custom_call" | custom-call | bytes 4620000 | tf_op jit(solution)/shard_map/pallas_call | solution.py:320
  (19 shorter events, 0.1 us)
Async XLA Ops:
  0.0 71.2 %copy-start.7 = (bf16[1536]{0:T(1024)(128)(2,1)S(1)}, bf16[1536]{0:T(1024)(128)(2,1)}, u32[]{:S(2)}) copy-start(bf16[1536]{0:T(1024)(128)(2,1)} %param.17) | copy-start | bytes 9220
  7.5 8.5 %collective-permute-start = (bf16[4,2,128,384]{3,2,1,0:T(8,128)(2,1)}, bf16[4,2,128,384]{3,2,1,0:T(8,128)(2,1)S(1)}, u32[]{:S(2)}, u32[]{:S(2)}) collective-permute-start(bf16[4,2,128,384]{3,2,1,0:T(8,128)(2,1)} %get-tuple-element.18), channel_id=1, source_target_pairs={{0,1},{1,0},{2,3},{3,2},{4,5},{5,4},{6,7},{7,6},{8,9},{9,8},{10,11... | collective-permute-start | bytes 2359304 | tf_op jit(solution)/shard_map/ppermute | solution.py:279
  7.6 22.9 %all-to-all-start = ((bf16[32,32,384]{2,1,0:T(8,128)(2,1)}), bf16[32,32,384]{2,1,0:T(8,128)(2,1)S(1)}, u32[]{:S(2)}, u32[]{:S(2)}) async-start(bf16[32,32,384]{2,1,0:T(8,128)(2,1)} %shard_map.100.after_ref), calls=%async_computation | async-start | bytes 1572864 | tf_op jit(solution)/shard_map/all_to_all | solution.py:261
  16.0 1.1 %copy-start.2 = (bf16[4,2,128,384]{3,2,1,0:T(8,128)(2,1)S(1)}, bf16[4,2,128,384]{3,2,1,0:T(8,128)(2,1)}, u32[]{:S(2)}) copy-start(bf16[4,2,128,384]{3,2,1,0:T(8,128)(2,1)} %get-tuple-element.17.keep_ref) | copy-start | bytes 2359300
  17.3 15.5 %collective-permute-start.1 = (bf16[2,2,128,384]{3,2,1,0:T(8,128)(2,1)S(1)}, bf16[2,2,128,384]{3,2,1,0:T(8,128)(2,1)S(1)}, u32[]{:S(2)}, u32[]{:S(2)}) collective-permute-start(bf16[2,2,128,384]{3,2,1,0:T(8,128)(2,1)S(1)} %get-tuple-element.20), channel_id=1, source_target_pairs={{0,2},{1,9},{2,4},{3,11},{4,6},{5,13},{6,0},{7,15},{8,10},{9,17},{... | collective-permute-start | bytes 1179656 | tf_op jit(solution)/shard_map/ppermute | solution.py:281
  19.1 18.1 %collective-permute-start.2 = (bf16[2,2,128,384]{3,2,1,0:T(8,128)(2,1)S(1)}, bf16[2,2,128,384]{3,2,1,0:T(8,128)(2,1)S(1)}, u32[]{:S(2)}, u32[]{:S(2)}) collective-permute-start(bf16[2,2,128,384]{3,2,1,0:T(8,128)(2,1)S(1)} %get-tuple-element.21), channel_id=1, source_target_pairs={{0,4},{1,17},{2,6},{3,19},{4,0},{5,21},{6,2},{7,23},{8,12},{9,25},... | collective-permute-start | bytes 1179656 | tf_op jit(solution)/shard_map/ppermute | solution.py:281
  21.8 15.4 %collective-permute-start.3 = (bf16[2,2,128,384]{3,2,1,0:T(8,128)(2,1)S(1)}, bf16[2,2,128,384]{3,2,1,0:T(8,128)(2,1)S(1)}, u32[]{:S(2)}, u32[]{:S(2)}) collective-permute-start(bf16[2,2,128,384]{3,2,1,0:T(8,128)(2,1)S(1)} %get-tuple-element.22), channel_id=1, source_target_pairs={{0,6},{1,25},{2,0},{3,27},{4,2},{5,29},{6,4},{7,31},{8,14},{9,1},{... | collective-permute-start | bytes 1179656 | tf_op jit(solution)/shard_map/ppermute | solution.py:281
  65.3 14.4 %collective-permute-start.4 = (bf16[32,3072]{1,0:T(8,128)(2,1)}, bf16[32,3072]{1,0:T(8,128)(2,1)S(1)}, u32[]{:S(2)}, u32[]{:S(2)}) collective-permute-start(bf16[32,3072]{1,0:T(8,128)(2,1)} %get-tuple-element.23.after_ref.r0_ref), channel_id=1, source_target_pairs={{0,32},{32,64},{64,96},{96,0},{1,33},{33,65},{65,97},{97,1},{2,34}... | collective-permute-start | bytes 589832 | tf_op jit(solution)/shard_map/ppermute | solution.py:309
  67.0 12.7 %collective-permute-start.5 = (bf16[32,3072]{1,0:T(8,128)(2,1)}, bf16[32,3072]{1,0:T(8,128)(2,1)S(1)}, u32[]{:S(2)}, u32[]{:S(2)}) collective-permute-start(bf16[32,3072]{1,0:T(8,128)(2,1)} %get-tuple-element.23.after_ref.r0_ref), channel_id=1, source_target_pairs={{0,64},{32,96},{64,0},{96,32},{1,65},{33,97},{65,1},{97,33},{2,66}... | collective-permute-start | bytes 589832 | tf_op jit(solution)/shard_map/ppermute | solution.py:309
  69.9 9.8 %collective-permute-start.6 = (bf16[32,3072]{1,0:T(8,128)(2,1)}, bf16[32,3072]{1,0:T(8,128)(2,1)S(1)}, u32[]{:S(2)}, u32[]{:S(2)}) collective-permute-start(bf16[32,3072]{1,0:T(8,128)(2,1)} %get-tuple-element.23.after_ref.r0_ref), channel_id=1, source_target_pairs={{0,96},{32,0},{64,32},{96,64},{1,97},{33,1},{65,33},{97,65},{2,98}... | collective-permute-start | bytes 589832 | tf_op jit(solution)/shard_map/ppermute | solution.py:309
  71.2 0.9 copy-start
  72.2 3.7 %copy-start.1 = (bf16[32,3072]{1,0:T(8,128)(2,1)S(1)}, bf16[32,3072]{1,0:T(8,128)(2,1)}, u32[]{:S(2)}) copy-start(bf16[32,3072]{1,0:T(8,128)(2,1)} %get-tuple-element.23.after_ref.r0_ref) | copy-start | bytes 589828
  79.6 6.2 %copy-start.6 = (bf16[3072]{0:T(1024)(128)(2,1)S(1)}, bf16[3072]{0:T(1024)(128)(2,1)}, u32[]{:S(2)}) copy-start(bf16[3072]{0:T(1024)(128)(2,1)} %param.19) | copy-start | bytes 18436
  79.6 16.4 %copy-start.3 = (f32[32,3072]{1,0:T(8,128)S(1)}, f32[32,3072]{1,0:T(8,128)}, u32[]{:S(2)}) copy-start(f32[32,3072]{1,0:T(8,128)} %get-tuple-element.28.hidden_ref) | copy-start | bytes 1179652
  79.6 16.4 %copy-start.4 = (bf16[1,4,3072]{2,1,0:T(4,128)(2,1)S(1)}, bf16[1,4,3072]{2,1,0:T(4,128)(2,1)}, u32[]{:S(2)}) copy-start(bf16[1,4,3072]{2,1,0:T(4,128)(2,1)} %mod_ref.1) | copy-start | bytes 73732
  79.7 16.4 %copy-start.5 = (s32[5]{0:T(128)S(1)}, s32[5]{0:T(128)}, u32[]{:S(2)}) copy-start(s32[5]{0:T(128)} %stack.19.info_ref) | copy-start | bytes 64
  82.4 10.0 %collective-permute-start.7 = (bf16[32,3072]{1,0:T(8,128)(2,1)S(1)}, bf16[32,3072]{1,0:T(8,128)(2,1)S(1)}, u32[]{:S(2)}, u32[]{:S(2)}) collective-permute-start(bf16[32,3072]{1,0:T(8,128)(2,1)S(1)} %get-tuple-element.25), channel_id=1, source_target_pairs={{0,96},{32,0},{64,32},{96,64},{1,97},{33,1},{65,33},{97,65},{2,98}... | collective-permute-start | bytes 589832 | tf_op jit(solution)/shard_map/ppermute | solution.py:319
  84.0 9.3 %collective-permute-start.8 = (bf16[32,3072]{1,0:T(8,128)(2,1)S(1)}, bf16[32,3072]{1,0:T(8,128)(2,1)S(1)}, u32[]{:S(2)}, u32[]{:S(2)}) collective-permute-start(bf16[32,3072]{1,0:T(8,128)(2,1)S(1)} %get-tuple-element.26), channel_id=1, source_target_pairs={{0,64},{32,96},{64,0},{96,32},{1,65},{33,97},{65,1},{97,33},{2,66}... | collective-permute-start | bytes 589832 | tf_op jit(solution)/shard_map/ppermute | solution.py:319
  85.3 10.8 %collective-permute-start.9 = (bf16[32,3072]{1,0:T(8,128)(2,1)S(1)}, bf16[32,3072]{1,0:T(8,128)(2,1)S(1)}, u32[]{:S(2)}, u32[]{:S(2)}) collective-permute-start(bf16[32,3072]{1,0:T(8,128)(2,1)S(1)} %get-tuple-element.27), channel_id=1, source_target_pairs={{0,32},{32,64},{64,96},{96,0},{1,33},{33,65},{65,97},{97,1},{2,34}... | collective-permute-start | bytes 589832 | tf_op jit(solution)/shard_map/ppermute | solution.py:319

commit v3 on v2

--- a/solution.py
+++ b/solution.py
@@ -51,12 +51,12 @@
 
 
 def pack_cache_kernel(
-    info_ref, kv_hbm, fresh_ref, chosen_ref, after_ref, keep_ref, send_ref, kv_ref, kv_new_ref, patched, sems
+    count_ref, kv_ref, fresh_ref, chosen_ref, keep_ref, send_ref, patched
 ):
-    fetch([(kv_hbm, kv_ref), (fresh_ref.at[1:3], kv_new_ref)], sems)
     tokens = kv_ref.shape[0]
-    slots = kv_new_ref.shape[1]
-    core, ring_x, ring_z, count = info_ref[0], info_ref[1], info_ref[2], info_ref[3]
+    slots = fresh_ref.shape[1]
+    core, ring_x, ring_z = (lax.axis_index(a) for a in ("core", "x", "z"))
+    count = count_ref[0, 0]
     token_id = lax.broadcasted_iota(i32, (tokens, slots), 0)
     slot_id = lax.broadcasted_iota(i32, (tokens, slots), 1)
     hit = (token_id == chosen_ref[...]) & (slot_id < count)
@@ -65,7 +65,7 @@
     hot = hot.astype(bf16)
     old = jnp.swapaxes(kv_ref[...], 0, 1)
     for which in range(2):
-        new = jnp.dot(hot, kv_new_ref[which], preferred_element_type=f32)
+        new = jnp.dot(hot, fresh_ref[1 + which], preferred_element_type=f32)
         patched[which] = jnp.where(taken, new, old[which].astype(f32)).astype(bf16)
     half = 4 * BLOCK
     for k in range(4):
@@ -127,16 +127,9 @@
     lax.fori_loop(0, q_ref.shape[0] // blocks, step, 0)
 
 
-def combine_kernel(
-    info_ref, parts_ref, rows_hbm, mod_hbm, hidden_ref, normed_ref, levels, turned, rows_ref, mod_ref, sems
-):
+def combine_kernel(parts_ref, rows_ref, mod_ref, hidden_ref, normed_ref, mark_ref, levels, turned):
     slots = rows_ref.shape[1]
-    copies = [
-        pltpu.make_async_copy(rows_hbm, rows_ref, sems.at[0]),
-        pltpu.make_async_copy(mod_hbm, mod_ref, sems.at[1]),
-    ]
-    for copy in copies:
-        copy.start()
+    place = 2 * lax.rem(lax.axis_index("x"), 2) + lax.axis_index("core")
     heads = 24
 
     def source(part, group):
@@ -157,9 +150,7 @@
         levels[p * heads : (p + 1) * heads, :] = weights[p] * total
     levels[4 * heads :, :] = jnp.zeros((128 - 4 * heads, 128), f32)
     turned[...] = levels[...].T
-    mine = turned[pl.ds(pl.multiple_of(info_ref[4] * SLOT_PAD, SLOT_PAD), SLOT_PAD), :]
-    for copy in copies:
-        copy.wait()
+    mine = turned[pl.ds(pl.multiple_of(place * SLOT_PAD, SLOT_PAD), SLOT_PAD), :]
     shifts = mod_ref[0].astype(f32)
     for group in range(8):
         for h in range(HEADS_HERE):
@@ -178,22 +169,24 @@
     spread = jnp.mean(center * center, axis=1, keepdims=True)
     normed = center * lax.rsqrt(spread + EPS) * (1.0 + shifts[1:2]) + shifts[0:1]
     normed_ref[...] = normed.astype(bf16)
-
-
-def load_kernel(after_ref, weight, out_ref, sems):
-    fetch([(weight, out_ref)], sems)
-
-
-def load(after, weight, limit):
+    mark_ref[...] = jnp.zeros(mark_ref.shape, bf16)
+
+
+def load_kernel(after_ref, *refs):
+    count = len(refs) // 2
+    fetch(list(zip(refs[:count], refs[count : 2 * count])), refs[2 * count])
+
+
+def load(after, arrays, limit):
     return call(
         load_kernel,
-        jax.ShapeDtypeStruct(weight.shape, bf16),
-        scratch=[pltpu.SemaphoreType.DMA((1,))],
-        n_in=2,
-        hbm=(0, 1),
+        [jax.ShapeDtypeStruct(v.shape, bf16) for v in arrays],
+        scratch=[pltpu.SemaphoreType.DMA((len(arrays),))],
+        n_in=1 + len(arrays),
+        hbm=range(1 + len(arrays)),
         limit=limit,
         us=3.6,
-    )(after, weight)
+    )(after, *arrays)
 
 
 def feed_kernel(r0_ref, r1_ref, r2_ref, r3_ref, up_ref, b_up_ref, down_ref, o0, o1, o2, o3, rows_ref, active):
@@ -213,14 +206,14 @@
             out_ref[:, cols] = terms[i * SLOT_PAD : (i + 1) * SLOT_PAD].astype(bf16)
 
 
-def finish_kernel(info_ref, t0_ref, t1_ref, t2_ref, t3_ref, hidden_ref, mod_ref, b_down_ref, out_ref):
+def finish_kernel(count_ref, t0_ref, t1_ref, t2_ref, t3_ref, hidden_ref, mod_ref, b_down_ref, out_ref):
     slots = out_ref.shape[1]
     total = t0_ref[...].astype(f32)
     for ref in (t1_ref, t2_ref, t3_ref):
         total = total + ref[...].astype(f32)
     feed_out = total[:slots] + b_down_ref[...].astype(f32)
     result = hidden_ref[:slots] + mod_ref[0, 3:4].astype(f32) * feed_out
-    live = lax.broadcasted_iota(i32, result.shape, 0) < info_ref[3]
+    live = lax.broadcasted_iota(i32, result.shape, 0) < count_ref[0, 0]
     out_ref[0] = jnp.where(live, result, 0.0).astype(bf16)
 
 
@@ -245,10 +238,6 @@
     shape = jax.ShapeDtypeStruct
     slots, width = rows_in.shape[1], rows_in.shape[2]
     tokens = kv_cache.shape[1]
-    core, ring_x, ring_z = (lax.axis_index(a) for a in ("core", "x", "z"))
-    me = ring_z * 8 + ring_x * 2 + core
-    info = jnp.stack([core, ring_x, ring_z, counts[0, 0], me % 4]).astype(i32)
-
     fresh = jnp.swapaxes(fresh_qkv[0], 0, 1)
     q_blocks = call(
         pack_queries_kernel,
@@ -263,21 +252,14 @@
     keep, send = call(
         pack_cache_kernel,
         [shape((4, 2, tokens, BLOCK), bf16)] * 2,
-        scratch=[
-            pltpu.VMEM((tokens, 2, width), bf16),
-            pltpu.VMEM((2, slots, width), bf16),
-            pltpu.VMEM((2, tokens, width), bf16),
-            pltpu.SemaphoreType.DMA((2,)),
-        ],
-        n_in=5,
+        scratch=[pltpu.VMEM((2, tokens, width), bf16)],
+        n_in=4,
         smem=(0,),
-        hbm=(1, 2, 4),
-        limit=61,
         us=3.0,
-    )(info, kv_cache[0], fresh, chosen, q_blocks)
+    )(counts, kv_cache[0], fresh, chosen)
     swap = [(position(z, x, c), position(z, x, 1 - c)) for z in range(4) for x in range(4) for c in range(2)]
     first = lax.ppermute(send, SEQ, swap)
-    stacked = call(stack_kernel, [shape((2, 2, tokens, BLOCK), bf16)] * 4, n_in=2)(keep, first)
+    stacked = call(stack_kernel, [shape((2, 2, tokens, BLOCK), bf16)] * 4, n_in=2, us=0.5)(keep, first)
     others = [lax.ppermute(stacked[k], SEQ, ring_pairs(k)) for k in (1, 2, 3)]
 
     partial = call(
@@ -289,26 +271,17 @@
         us=6.5,
     )(q_all, stacked[0], *others)
     parts = lax.all_to_all(partial, SEQ, 0, 0, tiled=True)
-    hidden, normed = call(
+    rows, mod = load(partial, [rows_in, modulation], 16)
+    hidden, normed, mark = call(
         combine_kernel,
-        [shape((SLOT_PAD, width), f32), shape((SLOT_PAD, width), bf16)],
-        scratch=[
-            pltpu.VMEM((128, 128), f32),
-            pltpu.VMEM((128, 128), f32),
-            pltpu.VMEM(rows_in.shape, bf16),
-            pltpu.VMEM(modulation.shape, bf16),
-            pltpu.SemaphoreType.DMA((2,)),
-        ],
-        n_in=4,
-        smem=(0,),
-        hbm=(2, 3),
-        limit=60,
+        [shape((SLOT_PAD, width), f32), shape((SLOT_PAD, width), bf16), shape((16, 128), bf16)],
+        scratch=[pltpu.VMEM((128, 128), f32), pltpu.VMEM((128, 128), f32)],
+        n_in=3,
         us=1.6,
-    )(info, parts, rows_in, modulation)
+    )(parts, rows, mod)
 
     visits = [lax.ppermute(normed, "y", turn(k)) for k in (1, 2, 3)]
-    up = load(normed, w_up, 44)
-    down = load(normed, w_down, 36)
+    up, down = load(mark, [w_up, w_down], 34)
     terms = call(
         feed_kernel,
         [shape((SLOT_PAD, width), bf16)] * 4,
@@ -318,7 +291,7 @@
     )(normed, *visits, up, b_up[None], down)
     back = [lax.ppermute(terms[k], "y", turn(-k)) for k in (1, 2, 3)]
     return call(finish_kernel, shape((1, slots, width), bf16), n_in=8, smem=(0,), us=1.4)(
-        info, terms[0], *back, hidden, modulation, b_down[None]
+        counts, terms[0], *back, hidden, modulation, b_down[None]
     )
 
 

time: 98.8 us -> 96.6 us (0.978)
  blocking collectives: 19.8 us -> 0 us
  waiting for transfers between devices: 24.2 us -> 39.8 us
  starting transfers between devices: 23.7 us -> 29.6 us
  Pallas kernels: 26.2 us -> 22 us
    all_to_all x1 -> x0, blocking collectives: 19.8 us -> none  [body(): parts = lax.all_to_all(partial, SEQ, 0, 0, tiled=True)]
    all_to_all x0 -> x1, waiting for transfers between devices: none -> 14.2 us  [body(): parts = lax.all_to_all(partial, SEQ, 0, 0, tiled=True)]
    all_to_all x0 -> x1, starting transfers between devices: none -> 5.32 us  [body(): parts = lax.all_to_all(partial, SEQ, 0, 0, tiled=True)]
    pallas_call x1, Pallas kernels: 3.64 us -> 1.11 us  [body(): call(combine_kernel, [shape((SLOT_PAD, width), f32), shape((SLOT_PAD, wid...]
    pallas_call x1, Pallas kernels: 4.27 us -> 1.96 us  [body(): call(pack_cache_kernel, [shape((4, 2, tokens, BLOCK), bf16)] * 2, scratch...]
    ppermute x3, waiting for transfers between devices: 0.01 us -> 1.18 us  [body(): visits = [lax.ppermute(normed, 'y', turn(k)) for k in (1, 2, 3)]]
    unnamed x16 -> x14, local copies, waits for them, and re-layouts: 2.1 us -> 3.14 us
  transfers between devices with their start and end apart: 11 -> 12, of which waited for: 6 -> 8; matrix products, arithmetic and copies ran while one was open for 0% -> 0% of each run, Pallas kernels for 8% -> 10%
where the time goes in v3:
time: 96.6 us; the launch traced here: 95.3 us
  waiting for transfers between devices  39.8 us (41%)
  starting transfers between devices  29.6 us (31%)
  Pallas kernels  22 us (23%)
  local copies, waits for them, and re-layouts  3.15 us (3%)
    all_to_all x1, waiting for transfers between devices, body(): parts = lax.all_to_all(partial, SEQ, 0, 0, tiled=True)  14.2 us
    ppermute x3, waiting for transfers between devices, body(): back = [lax.ppermute(terms[k], 'y', turn(-k)) for k in (1, 2, 3)]  10.2 us
    all_to_all x1, starting transfers between devices, body(): q_all = lax.all_to_all(q_blocks, SEQ, 0, 0, tiled=True)  8.37 us
    all_to_all x1, waiting for transfers between devices, body(): q_all = lax.all_to_all(q_blocks, SEQ, 0, 0, tiled=True)  7.55 us
    pallas_call x2, Pallas kernels, load(): call(load_kernel, [jax.ShapeDtypeStruct(v.shape, bf16) for v in arrays],...  6.69 us
    ppermute x3, waiting for transfers between devices, body(): others = [lax.ppermute(stacked[k], SEQ, ring_pairs(k)) for k in (1, 2, 3)]  6.67 us
    ppermute x3, starting transfers between devices, body(): others = [lax.ppermute(stacked[k], SEQ, ring_pairs(k)) for k in (1, 2, 3)]  5.93 us
    ppermute x3, starting transfers between devices, body(): visits = [lax.ppermute(normed, 'y', turn(k)) for k in (1, 2, 3)]  5.9 us
  transfers between devices with their start and end apart: 12, of which 8 were waited for; matrix products, arithmetic and copies ran while one was open for 0% of the time, Pallas kernels for 10%

profile of v3, /device:TPU:0, one launch (start us, length us, event | category | flops | bytes accessed | tf_op | source)
XLA Modules:
  0.0 95.3 jit_solution(16193766234261892303)
XLA Ops:
  0.7 0.0 copy-start
  0.7 1.1 %copy-done = bf16[1,28,3,3072]{3,1,2,0:T(8,128)(2,1)S(1)} copy-done((bf16[1,28,3,3072]{3,1,2,0:T(8,128)(2,1)S(1)}, bf16[1,28,3,3072]{3,1,2,0:T(8,128)(2,1)}, u32[]{:S(2)}) %copy-start) | copy-done | bytes 516120
  1.7 1.4 %copy-done.1 = bf16[1,128,2,3072]{3,2,1,0:T(2,128)(2,1)S(1)} copy-done((bf16[1,128,2,3072]{3,2,1,0:T(2,128)(2,1)S(1)}, bf16[1,128,2,3072]{3,2,1,0:T(2,128)(2,1)}, u32[]{:S(2)}) %copy-start.1) | copy-done | bytes 1572888
  3.1 0.7 copy-done.4
  3.8 2.0 %shard_map.101 = (bf16[4,2,128,384]{3,2,1,0:T(8,128)(2,1)S(1)}, bf16[4,2,128,384]{3,2,1,0:T(8,128)(2,1)}) custom-call(s32[1,1]{1,0:T(1,128)S(6)} %copy.11.count_ref, bf16[128,2,3072]{2,1,0:T(2,128)(2,1)S(1)} %bitcast.6, bf16[3,28,3072]{2,1,0:T(8,128)(2,1)S(1)} %bitcast.5, s32[1,28]{1,0:T(1,128)S(1)} %copy-done.4), custom_call_target="tpu_custom_call" | custom-call | bytes 9900000 | tf_op jit(solution)/shard_map/pallas_call | solution.py:252
  5.8 1.9 %shard_map.100 = bf16[32,32,384]{2,1,0:T(8,128)(2,1)} custom-call(bf16[3,28,3072]{2,1,0:T(8,128)(2,1)} %bitcast.4), custom_call_target="tpu_custom_call" | custom-call | bytes 3300000 | tf_op jit(solution)/shard_map/pallas_call | solution.py:242
  7.7 8.4 %all-to-all-start = ((bf16[32,32,384]{2,1,0:T(8,128)(2,1)}), bf16[32,32,384]{2,1,0:T(8,128)(2,1)S(1)}, u32[]{:S(2)}, u32[]{:S(2)}) async-start(bf16[32,32,384]{2,1,0:T(8,128)(2,1)} %shard_map.100), calls=%async_computation | async-start | bytes 1572864 | tf_op jit(solution)/shard_map/all_to_all | solution.py:250
  16.1 1.1 %shard_map.102 = (bf16[2,2,128,384]{3,2,1,0:T(8,128)(2,1)S(1)}, bf16[2,2,128,384]{3,2,1,0:T(8,128)(2,1)}, bf16[2,2,128,384]{3,2,1,0:T(8,128)(2,1)}, bf16[2,2,128,384]{3,2,1,0:T(8,128)(2,1)S(1)}) custom-call(bf16[4,2,128,384]{3,2,1,0:T(8,128)(2,1)S(1)} %get-tuple-element.22.keep_ref, bf16[4,2,128,384]{3,2,1,0:T(8,128)(2,1)S(1)} %collective-permute-done.first_ref), custom_call_target="tpu_custom_call" | custom-call | bytes 1650000 | tf_op jit(solution)/shard_map/pallas_call | solution.py:262
  17.2 1.8 %collective-permute-start.1 = (bf16[2,2,128,384]{3,2,1,0:T(8,128)(2,1)}, bf16[2,2,128,384]{3,2,1,0:T(8,128)(2,1)S(1)}, u32[]{:S(2)}, u32[]{:S(2)}) collective-permute-start(bf16[2,2,128,384]{3,2,1,0:T(8,128)(2,1)} %get-tuple-element.25), channel_id=1, source_target_pairs={{0,2},{1,9},{2,4},{3,11},{4,6},{5,13},{6,0},{7,15},{8,10},{9,17},{... | collective-permute-start | bytes 1179656 | tf_op jit(solution)/shard_map/ppermute | solution.py:263
  18.9 2.7 %collective-permute-start.2 = (bf16[2,2,128,384]{3,2,1,0:T(8,128)(2,1)}, bf16[2,2,128,384]{3,2,1,0:T(8,128)(2,1)S(1)}, u32[]{:S(2)}, u32[]{:S(2)}) collective-permute-start(bf16[2,2,128,384]{3,2,1,0:T(8,128)(2,1)} %get-tuple-element.26), channel_id=1, source_target_pairs={{0,4},{1,17},{2,6},{3,19},{4,0},{5,21},{6,2},{7,23},{8,12},{9,25},... | collective-permute-start | bytes 1179656 | tf_op jit(solution)/shard_map/ppermute | solution.py:263
  21.6 1.5 %collective-permute-start.3 = (bf16[2,2,128,384]{3,2,1,0:T(8,128)(2,1)S(1)}, bf16[2,2,128,384]{3,2,1,0:T(8,128)(2,1)S(1)}, u32[]{:S(2)}, u32[]{:S(2)}) collective-permute-start(bf16[2,2,128,384]{3,2,1,0:T(8,128)(2,1)S(1)} %get-tuple-element.27), channel_id=1, source_target_pairs={{0,6},{1,25},{2,0},{3,27},{4,2},{5,29},{6,4},{7,31},{8,14},{9,1},{... | collective-permute-start | bytes 1179656 | tf_op jit(solution)/shard_map/ppermute | solution.py:263
  23.1 7.5 %all-to-all-done.q_ref = bf16[32,32,384]{2,1,0:T(8,128)(2,1)S(1)} async-done(((bf16[32,32,384]{2,1,0:T(8,128)(2,1)}), bf16[32,32,384]{2,1,0:T(8,128)(2,1)S(1)}, u32[]{:S(2)}, u32[]{:S(2)}) %all-to-all-start) | async-done | bytes 786464 | tf_op jit(solution)/shard_map/all_to_all | solution.py:250
  30.6 2.2 %collective-permute-done.1.r1_ref = bf16[2,2,128,384]{3,2,1,0:T(8,128)(2,1)S(1)} collective-permute-done((bf16[2,2,128,384]{3,2,1,0:T(8,128)(2,1)}, bf16[2,2,128,384]{3,2,1,0:T(8,128)(2,1)S(1)}, u32[]{:S(2)}, u32[]{:S(2)}) %collective-permute-start.1) | collective-permute-done | bytes 393248 | tf_op jit(solution)/shard_map/ppermute | solution.py:263
  32.8 4.5 %collective-permute-done.2.r2_ref = bf16[2,2,128,384]{3,2,1,0:T(8,128)(2,1)S(1)} collective-permute-done((bf16[2,2,128,384]{3,2,1,0:T(8,128)(2,1)}, bf16[2,2,128,384]{3,2,1,0:T(8,128)(2,1)S(1)}, u32[]{:S(2)}, u32[]{:S(2)}) %collective-permute-start.2) | collective-permute-done | bytes 393248 | tf_op jit(solution)/shard_map/ppermute | solution.py:263
  37.3 5.5 %shard_map.103.after_ref = bf16[32,32,384]{2,1,0:T(8,128)(2,1)} custom-call(bf16[32,32,384]{2,1,0:T(8,128)(2,1)S(1)} %all-to-all-done.q_ref, bf16[2,2,128,384]{3,2,1,0:T(8,128)(2,1)S(1)} %get-tuple-element.24.r0_ref, bf16[2,2,128,384]{3,2,1,0:T(8,128)(2,1)S(1)} %collective-permute-done.1.r1_ref, bf16[2,2,128,384]{3,2,1,0:T(8,128)(2,1)S(1)} %collective-permute-done.2.r2_ref, ...), custom_call_target="tpu_custom_call" | custom-call | bytes 21450000 | tf_op jit(solution)/shard_map/pallas_call | solution.py:265
  42.8 5.3 %all-to-all-start.1 = ((bf16[32,32,384]{2,1,0:T(8,128)(2,1)}), bf16[32,32,384]{2,1,0:T(8,128)(2,1)S(1)}, u32[]{:S(2)}, u32[]{:S(2)}) async-start(bf16[32,32,384]{2,1,0:T(8,128)(2,1)} %shard_map.103.after_ref), calls=%async_computation.1 | async-start | bytes 1572864 | tf_op jit(solution)/shard_map/all_to_all | solution.py:273
  48.2 0.3 shard_map.104
  48.5 14.2 %all-to-all-done.1.parts_ref = bf16[32,32,384]{2,1,0:T(8,128)(2,1)S(1)} async-done(((bf16[32,32,384]{2,1,0:T(8,128)(2,1)}), bf16[32,32,384]{2,1,0:T(8,128)(2,1)S(1)}, u32[]{:S(2)}, u32[]{:S(2)}) %all-to-all-start.1) | async-done | bytes 786464 | tf_op jit(solution)/shard_map/all_to_all | solution.py:273
  62.7 1.1 %shard_map.105 = (f32[32,3072]{1,0:T(8,128)S(1)}, bf16[32,3072]{1,0:T(8,128)(2,1)S(1)}, bf16[16,128]{1,0:T(8,128)(2,1)S(1)}) custom-call(bf16[32,32,384]{2,1,0:T(8,128)(2,1)S(1)} %all-to-all-done.1.parts_ref, bf16[1,28,3072]{2,1,0:T(8,128)(2,1)S(1)} %get-tuple-element.28.rows_ref, bf16[1,4,3072]{2,1,0:T(4,128)(2,1)S(1)} %get-tuple-element.29.mod_ref), custom_call_target="tpu_custom_call" | custom-call | bytes 5280000 | tf_op jit(solution)/shard_map/pallas_call | solution.py:275
  63.8 1.6 %collective-permute-start.4 = (bf16[32,3072]{1,0:T(8,128)(2,1)S(1)}, bf16[32,3072]{1,0:T(8,128)(2,1)S(1)}, u32[]{:S(2)}, u32[]{:S(2)}) collective-permute-start(bf16[32,3072]{1,0:T(8,128)(2,1)S(1)} %get-tuple-element.30.r0_ref), channel_id=1, source_target_pairs={{0,32},{32,64},{64,96},{96,0},{1,33},{33,65},{65,97},{97,1},{2,34}... | collective-permute-start | bytes 589832 | tf_op jit(solution)/shard_map/ppermute | solution.py:283
  65.5 2.9 %collective-permute-start.5 = (bf16[32,3072]{1,0:T(8,128)(2,1)S(1)}, bf16[32,3072]{1,0:T(8,128)(2,1)S(1)}, u32[]{:S(2)}, u32[]{:S(2)}) collective-permute-start(bf16[32,3072]{1,0:T(8,128)(2,1)S(1)} %get-tuple-element.30.r0_ref), channel_id=1, source_target_pairs={{0,64},{32,96},{64,0},{96,32},{1,65},{33,97},{65,1},{97,33},{2,66}... | collective-permute-start | bytes 589832 | tf_op jit(solution)/shard_map/ppermute | solution.py:283
  68.4 1.3 %collective-permute-start.6 = (bf16[32,3072]{1,0:T(8,128)(2,1)S(1)}, bf16[32,3072]{1,0:T(8,128)(2,1)S(1)}, u32[]{:S(2)}, u32[]{:S(2)}) collective-permute-start(bf16[32,3072]{1,0:T(8,128)(2,1)S(1)} %get-tuple-element.30.r0_ref), channel_id=1, source_target_pairs={{0,96},{32,0},{64,32},{96,64},{1,97},{33,1},{65,33},{97,65},{2,98}... | collective-permute-start | bytes 589832 | tf_op jit(solution)/shard_map/ppermute | solution.py:283
  69.8 6.4 %shard_map.106 = (bf16[3072,1536]{1,0:T(8,128)(2,1)S(1)}, bf16[1536,3072]{1,0:T(8,128)(2,1)S(1)}) custom-call(bf16[16,128]{1,0:T(8,128)(2,1)S(1)} %get-tuple-element.31.after_ref, bf16[3072,1536]{1,0:T(8,128)(2,1)} %refs_0_.3, bf16[1536,3072]{1,0:T(8,128)(2,1)} %refs_1_.3), custom_call_target="tpu_custom_call" | custom-call | bytes 11880000 | tf_op jit(solution)/shard_map/pallas_call | solution.py:181
  76.2 1.2 %collective-permute-done.5.r2_ref = bf16[32,3072]{1,0:T(8,128)(2,1)S(1)} collective-permute-done((bf16[32,3072]{1,0:T(8,128)(2,1)S(1)}, bf16[32,3072]{1,0:T(8,128)(2,1)S(1)}, u32[]{:S(2)}, u32[]{:S(2)}) %collective-permute-start.5) | collective-permute-done | bytes 196640 | tf_op jit(solution)/shard_map/ppermute | solution.py:283
  77.3 2.8 %shard_map.107 = (bf16[32,3072]{1,0:T(8,128)(2,1)S(1)}, bf16[32,3072]{1,0:T(8,128)(2,1)S(1)}, bf16[32,3072]{1,0:T(8,128)(2,1)S(1)}, bf16[32,3072]{1,0:T(8,128)(2,1)S(1)}) custom-call(bf16[32,3072]{1,0:T(8,128)(2,1)S(1)} %get-tuple-element.30.r0_ref, bf16[32,3072]{1,0:T(8,128)(2,1)S(1)} %collective-permute-done.4.r1_ref, ...), custom_call_target="tpu_custom_call" | custom-call | bytes 12210000 | tf_op jit(solution)/shard_map/pallas_call | solution.py:285
  80.2 2.2 %collective-permute-start.7 = (bf16[32,3072]{1,0:T(8,128)(2,1)S(1)}, bf16[32,3072]{1,0:T(8,128)(2,1)S(1)}, u32[]{:S(2)}, u32[]{:S(2)}) collective-permute-start(bf16[32,3072]{1,0:T(8,128)(2,1)S(1)} %get-tuple-element.35), channel_id=1, source_target_pairs={{0,96},{32,0},{64,32},{96,64},{1,97},{33,1},{65,33},{97,65},{2,98}... | collective-permute-start | bytes 589832 | tf_op jit(solution)/shard_map/ppermute | solution.py:292
  82.4 1.1 %collective-permute-start.8 = (bf16[32,3072]{1,0:T(8,128)(2,1)S(1)}, bf16[32,3072]{1,0:T(8,128)(2,1)S(1)}, u32[]{:S(2)}, u32[]{:S(2)}) collective-permute-start(bf16[32,3072]{1,0:T(8,128)(2,1)S(1)} %get-tuple-element.36), channel_id=1, source_target_pairs={{0,64},{32,96},{64,0},{96,32},{1,65},{33,97},{65,1},{97,33},{2,66}... | collective-permute-start | bytes 589832 | tf_op jit(solution)/shard_map/ppermute | solution.py:292
  83.5 0.7 collective-permute-start.9
  84.3 6.6 %collective-permute-done.7.t1_ref = bf16[32,3072]{1,0:T(8,128)(2,1)S(1)} collective-permute-done((bf16[32,3072]{1,0:T(8,128)(2,1)S(1)}, bf16[32,3072]{1,0:T(8,128)(2,1)S(1)}, u32[]{:S(2)}, u32[]{:S(2)}) %collective-permute-start.7) | collective-permute-done | bytes 196640 | tf_op jit(solution)/shard_map/ppermute | solution.py:292
  90.9 0.9 collective-permute-done.8.t2_ref
  91.7 2.7 %collective-permute-done.9.t3_ref = bf16[32,3072]{1,0:T(8,128)(2,1)S(1)} collective-permute-done((bf16[32,3072]{1,0:T(8,128)(2,1)S(1)}, bf16[32,3072]{1,0:T(8,128)(2,1)S(1)}, u32[]{:S(2)}, u32[]{:S(2)}) %collective-permute-start.9) | collective-permute-done | bytes 196640 | tf_op jit(solution)/shard_map/ppermute | solution.py:292
  94.5 0.9 shard_map.108
  (17 shorter events, 0.0 us)
Async XLA Ops:
  0.0 69.8 %copy-start.6 = (bf16[1536]{0:T(1024)(128)(2,1)S(1)}, bf16[1536]{0:T(1024)(128)(2,1)}, u32[]{:S(2)}) copy-start(bf16[1536]{0:T(1024)(128)(2,1)} %param.17) | copy-start | bytes 9220
  0.7 1.1 %copy-start = (bf16[1,28,3,3072]{3,1,2,0:T(8,128)(2,1)S(1)}, bf16[1,28,3,3072]{3,1,2,0:T(8,128)(2,1)}, u32[]{:S(2)}) copy-start(bf16[1,28,3,3072]{3,1,2,0:T(8,128)(2,1)} %param.11) | copy-start | bytes 1548292
  1.7 1.4 %copy-start.1 = (bf16[1,128,2,3072]{3,2,1,0:T(2,128)(2,1)S(1)}, bf16[1,128,2,3072]{3,2,1,0:T(2,128)(2,1)}, u32[]{:S(2)}) copy-start(bf16[1,128,2,3072]{3,2,1,0:T(2,128)(2,1)} %param.12) | copy-start | bytes 4718596
  3.1 0.7 copy-start.4
  3.8 44.4 %copy-start.2 = (bf16[1,28,3072]{2,1,0:T(8,128)(2,1)S(1)}, bf16[1,28,3072]{2,1,0:T(8,128)(2,1)}, u32[]{:S(2)}) copy-start(bf16[1,28,3072]{2,1,0:T(8,128)(2,1)} %refs_0_.2) | copy-start | bytes 516100
  3.8 44.4 %copy-start.3 = (bf16[1,4,3072]{2,1,0:T(4,128)(2,1)S(1)}, bf16[1,4,3072]{2,1,0:T(4,128)(2,1)}, u32[]{:S(2)}) copy-start(bf16[1,4,3072]{2,1,0:T(4,128)(2,1)} %mod_ref.1) | copy-start | bytes 73732
  5.8 10.3 %collective-permute-start = (bf16[4,2,128,384]{3,2,1,0:T(8,128)(2,1)}, bf16[4,2,128,384]{3,2,1,0:T(8,128)(2,1)S(1)}, u32[]{:S(2)}, u32[]{:S(2)}) collective-permute-start(bf16[4,2,128,384]{3,2,1,0:T(8,128)(2,1)} %get-tuple-element.23), channel_id=1, source_target_pairs={{0,1},{1,0},{2,3},{3,2},{4,5},{5,4},{6,7},{7,6},{8,9},{9,8},{10,11... | collective-permute-start | bytes 2359304 | tf_op jit(solution)/shard_map/ppermute | solution.py:261
  7.7 22.9 %all-to-all-start = ((bf16[32,32,384]{2,1,0:T(8,128)(2,1)}), bf16[32,32,384]{2,1,0:T(8,128)(2,1)S(1)}, u32[]{:S(2)}, u32[]{:S(2)}) async-start(bf16[32,32,384]{2,1,0:T(8,128)(2,1)} %shard_map.100), calls=%async_computation | async-start | bytes 1572864 | tf_op jit(solution)/shard_map/all_to_all | solution.py:250
  17.2 15.6 %collective-permute-start.1 = (bf16[2,2,128,384]{3,2,1,0:T(8,128)(2,1)}, bf16[2,2,128,384]{3,2,1,0:T(8,128)(2,1)S(1)}, u32[]{:S(2)}, u32[]{:S(2)}) collective-permute-start(bf16[2,2,128,384]{3,2,1,0:T(8,128)(2,1)} %get-tuple-element.25), channel_id=1, source_target_pairs={{0,2},{1,9},{2,4},{3,11},{4,6},{5,13},{6,0},{7,15},{8,10},{9,17},{... | collective-permute-start | bytes 1179656 | tf_op jit(solution)/shard_map/ppermute | solution.py:263
  18.9 18.4 %collective-permute-start.2 = (bf16[2,2,128,384]{3,2,1,0:T(8,128)(2,1)}, bf16[2,2,128,384]{3,2,1,0:T(8,128)(2,1)S(1)}, u32[]{:S(2)}, u32[]{:S(2)}) collective-permute-start(bf16[2,2,128,384]{3,2,1,0:T(8,128)(2,1)} %get-tuple-element.26), channel_id=1, source_target_pairs={{0,4},{1,17},{2,6},{3,19},{4,0},{5,21},{6,2},{7,23},{8,12},{9,25},... | collective-permute-start | bytes 1179656 | tf_op jit(solution)/shard_map/ppermute | solution.py:263
  21.6 15.7 %collective-permute-start.3 = (bf16[2,2,128,384]{3,2,1,0:T(8,128)(2,1)S(1)}, bf16[2,2,128,384]{3,2,1,0:T(8,128)(2,1)S(1)}, u32[]{:S(2)}, u32[]{:S(2)}) collective-permute-start(bf16[2,2,128,384]{3,2,1,0:T(8,128)(2,1)S(1)} %get-tuple-element.27), channel_id=1, source_target_pairs={{0,6},{1,25},{2,0},{3,27},{4,2},{5,29},{6,4},{7,31},{8,14},{9,1},{... | collective-permute-start | bytes 1179656 | tf_op jit(solution)/shard_map/ppermute | solution.py:263
  42.8 19.9 %all-to-all-start.1 = ((bf16[32,32,384]{2,1,0:T(8,128)(2,1)}), bf16[32,32,384]{2,1,0:T(8,128)(2,1)S(1)}, u32[]{:S(2)}, u32[]{:S(2)}) async-start(bf16[32,32,384]{2,1,0:T(8,128)(2,1)} %shard_map.103.after_ref), calls=%async_computation.1 | async-start | bytes 1572864 | tf_op jit(solution)/shard_map/all_to_all | solution.py:273
  63.8 12.3 %collective-permute-start.4 = (bf16[32,3072]{1,0:T(8,128)(2,1)S(1)}, bf16[32,3072]{1,0:T(8,128)(2,1)S(1)}, u32[]{:S(2)}, u32[]{:S(2)}) collective-permute-start(bf16[32,3072]{1,0:T(8,128)(2,1)S(1)} %get-tuple-element.30.r0_ref), channel_id=1, source_target_pairs={{0,32},{32,64},{64,96},{96,0},{1,33},{33,65},{65,97},{97,1},{2,34}... | collective-permute-start | bytes 589832 | tf_op jit(solution)/shard_map/ppermute | solution.py:283
  65.5 11.8 %collective-permute-start.5 = (bf16[32,3072]{1,0:T(8,128)(2,1)S(1)}, bf16[32,3072]{1,0:T(8,128)(2,1)S(1)}, u32[]{:S(2)}, u32[]{:S(2)}) collective-permute-start(bf16[32,3072]{1,0:T(8,128)(2,1)S(1)} %get-tuple-element.30.r0_ref), channel_id=1, source_target_pairs={{0,64},{32,96},{64,0},{96,32},{1,65},{33,97},{65,1},{97,33},{2,66}... | collective-permute-start | bytes 589832 | tf_op jit(solution)/shard_map/ppermute | solution.py:283
  68.4 8.9 %collective-permute-start.6 = (bf16[32,3072]{1,0:T(8,128)(2,1)S(1)}, bf16[32,3072]{1,0:T(8,128)(2,1)S(1)}, u32[]{:S(2)}, u32[]{:S(2)}) collective-permute-start(bf16[32,3072]{1,0:T(8,128)(2,1)S(1)} %get-tuple-element.30.r0_ref), channel_id=1, source_target_pairs={{0,96},{32,0},{64,32},{96,64},{1,97},{33,1},{65,33},{97,65},{2,98}... | collective-permute-start | bytes 589832 | tf_op jit(solution)/shard_map/ppermute | solution.py:283
  77.3 6.9 %copy-start.5 = (bf16[3072]{0:T(1024)(128)(2,1)S(1)}, bf16[3072]{0:T(1024)(128)(2,1)}, u32[]{:S(2)}) copy-start(bf16[3072]{0:T(1024)(128)(2,1)} %param.19) | copy-start | bytes 18436
  80.2 10.7 %collective-permute-start.7 = (bf16[32,3072]{1,0:T(8,128)(2,1)S(1)}, bf16[32,3072]{1,0:T(8,128)(2,1)S(1)}, u32[]{:S(2)}, u32[]{:S(2)}) collective-permute-start(bf16[32,3072]{1,0:T(8,128)(2,1)S(1)} %get-tuple-element.35), channel_id=1, source_target_pairs={{0,96},{32,0},{64,32},{96,64},{1,97},{33,1},{65,33},{97,65},{2,98}... | collective-permute-start | bytes 589832 | tf_op jit(solution)/shard_map/ppermute | solution.py:292
  82.4 9.3 %collective-permute-start.8 = (bf16[32,3072]{1,0:T(8,128)(2,1)S(1)}, bf16[32,3072]{1,0:T(8,128)(2,1)S(1)}, u32[]{:S(2)}, u32[]{:S(2)}) collective-permute-start(bf16[32,3072]{1,0:T(8,128)(2,1)S(1)} %get-tuple-element.36), channel_id=1, source_target_pairs={{0,64},{32,96},{64,0},{96,32},{1,65},{33,97},{65,1},{97,33},{2,66}... | collective-permute-start | bytes 589832 | tf_op jit(solution)/shard_map/ppermute | solution.py:292
  83.5 10.9 %collective-permute-start.9 = (bf16[32,3072]{1,0:T(8,128)(2,1)S(1)}, bf16[32,3072]{1,0:T(8,128)(2,1)S(1)}, u32[]{:S(2)}, u32[]{:S(2)}) collective-permute-start(bf16[32,3072]{1,0:T(8,128)(2,1)S(1)} %get-tuple-element.37), channel_id=1, source_target_pairs={{0,32},{32,64},{64,96},{96,0},{1,33},{33,65},{65,97},{97,1},{2,34}... | collective-permute-start | bytes 589832 | tf_op jit(solution)/shard_map/ppermute | solution.py:292

commit v4 on v3

--- a/solution.py
+++ b/solution.py
@@ -40,23 +40,34 @@
         copy.wait()
 
 
-def pack_queries_kernel(fresh_ref, out_ref, q_ref, sems):
-    rows = q_ref.shape[0]
-    fetch([(fresh_ref.at[0], q_ref)], sems)
+def pack_kernel(
+    count_ref, kv_hbm, fresh_hbm, chosen_hbm, q_hbm, keep_hbm, send_hbm,
+    kv_ref, fresh_ref, chosen_ref, patched, q_out, in_sems, out_sems,
+):
+    sources = [
+        (fresh_hbm.at[0], fresh_ref.at[0]),
+        (kv_hbm, kv_ref),
+        (fresh_hbm.at[1:3], fresh_ref.at[1:3]),
+        (chosen_hbm, chosen_ref),
+    ]
+    copies = [pltpu.make_async_copy(src, dst, in_sems.at[i]) for i, (src, dst) in enumerate(sources)]
+    for copy in copies:
+        copy.start()
+    tokens = kv_ref.shape[0]
+    slots = fresh_ref.shape[1]
+    copies[0].wait()
     for dest in range(32):
         z, x, core = dest // 8, dest // 2 % 4, dest % 2
         group = x if core == 0 else 4 + z
-        out_ref[dest, :rows, :] = q_ref[:, group * BLOCK : (group + 1) * BLOCK]
-        out_ref[dest, rows:, :] = jnp.zeros((SLOT_PAD - rows, BLOCK), bf16)
-
-
-def pack_cache_kernel(
-    count_ref, kv_ref, fresh_ref, chosen_ref, keep_ref, send_ref, patched
-):
-    tokens = kv_ref.shape[0]
-    slots = fresh_ref.shape[1]
+        q_out[dest, :slots, :] = fresh_ref[0, :, group * BLOCK : (group + 1) * BLOCK]
+        q_out[dest, slots:, :] = jnp.zeros((SLOT_PAD - slots, BLOCK), bf16)
+    outs = [pltpu.make_async_copy(q_out, q_hbm, out_sems.at[0])]
+    outs[0].start()
+
     core, ring_x, ring_z = (lax.axis_index(a) for a in ("core", "x", "z"))
     count = count_ref[0, 0]
+    for copy in copies[1:]:
+        copy.wait()
     token_id = lax.broadcasted_iota(i32, (tokens, slots), 0)
     slot_id = lax.broadcasted_iota(i32, (tokens, slots), 1)
     hit = (token_id == chosen_ref[...]) & (slot_id < count)
@@ -64,18 +75,23 @@
     taken = jnp.sum(hot, axis=1, keepdims=True) > 0.5
     hot = hot.astype(bf16)
     old = jnp.swapaxes(kv_ref[...], 0, 1)
+    half = 4 * BLOCK
     for which in range(2):
         new = jnp.dot(hot, fresh_ref[1 + which], preferred_element_type=f32)
         patched[which] = jnp.where(taken, new, old[which].astype(f32)).astype(bf16)
-    half = 4 * BLOCK
-    for k in range(4):
-        mine = lax.rem(jnp.where(core == 0, ring_x, ring_z) + k, 4)
-        other = lax.rem(jnp.where(core == 0, ring_z, ring_x) + k, 4)
-        at_mine = pl.multiple_of(core * half + mine * BLOCK, BLOCK)
-        at_other = pl.multiple_of((1 - core) * half + other * BLOCK, BLOCK)
-        for which in range(2):
-            keep_ref[k, which] = patched[which, :, pl.ds(at_mine, BLOCK)]
-            send_ref[k, which] = patched[which, :, pl.ds(at_other, BLOCK)]
+        for k in range(4):
+            mine = lax.rem(jnp.where(core == 0, ring_x, ring_z) + k, 4)
+            other = lax.rem(jnp.where(core == 0, ring_z, ring_x) + k, 4)
+            at_mine = pl.multiple_of(core * half + mine * BLOCK, BLOCK)
+            at_other = pl.multiple_of((1 - core) * half + other * BLOCK, BLOCK)
+            for at, target in ((at_other, send_hbm), (at_mine, keep_hbm)):
+                copy = pltpu.make_async_copy(
+                    patched.at[which, :, pl.ds(at, BLOCK)], target.at[k, which], out_sems.at[len(outs)]
+                )
+                copy.start()
+                outs.append(copy)
+    for copy in outs:
+        copy.wait()
 
 
 def stack_kernel(keep_ref, first_ref, *out_refs):
@@ -127,6 +143,16 @@
     lax.fori_loop(0, q_ref.shape[0] // blocks, step, 0)
 
 
+def fold(rows):
+    half = rows.shape[1] // 2
+    return jnp.concatenate([rows[:, :half], rows[:, half:]], axis=0)
+
+
+def unfold(folded):
+    count = folded.shape[0] // 2
+    return jnp.concatenate([folded[:count], folded[count:]], axis=1)
+
+
 def combine_kernel(parts_ref, rows_ref, mod_ref, hidden_ref, normed_ref, mark_ref, levels, turned):
     slots = rows_ref.shape[1]
     place = 2 * lax.rem(lax.axis_index("x"), 2) + lax.axis_index("core")
@@ -162,13 +188,12 @@
                 acc = acc + mine[:, column : column + 1] * block.astype(f32)
             cols = slice(head * HEAD_DIM, (head + 1) * HEAD_DIM)
             attended = acc[:slots] * shifts[2:3, cols]
-            hidden_ref[:slots, cols] = rows_ref[0, :, cols].astype(f32) + attended
-    hidden_ref[slots:, :] = jnp.zeros((SLOT_PAD - slots, hidden_ref.shape[1]), f32)
+            hidden_ref[:, cols] = rows_ref[0, :, cols].astype(f32) + attended
     hidden = hidden_ref[...]
     center = hidden - jnp.mean(hidden, axis=1, keepdims=True)
     spread = jnp.mean(center * center, axis=1, keepdims=True)
     normed = center * lax.rsqrt(spread + EPS) * (1.0 + shifts[1:2]) + shifts[0:1]
-    normed_ref[...] = normed.astype(bf16)
+    normed_ref[...] = fold(normed).astype(bf16)
     mark_ref[...] = jnp.zeros(mark_ref.shape, bf16)
 
 
@@ -189,10 +214,15 @@
     )(after, *arrays)
 
 
-def feed_kernel(r0_ref, r1_ref, r2_ref, r3_ref, up_ref, b_up_ref, down_ref, o0, o1, o2, o3, rows_ref, active):
+def feed_kernel(
+    r0_ref, r1_ref, r2_ref, r3_ref, up_ref, b_up_ref, down_ref, o0, o1, o2, o3, rows_ref, active, terms
+):
     chunk = 512
+    slots = r0_ref.shape[0] // 2
+    none = jnp.zeros((SLOT_PAD - slots, rows_ref.shape[1]), f32)
     for i, ref in enumerate((r0_ref, r1_ref, r2_ref, r3_ref)):
-        rows_ref[i * SLOT_PAD : (i + 1) * SLOT_PAD, :] = ref[...]
+        block = jnp.concatenate([unfold(ref[...].astype(f32)), none], axis=0)
+        rows_ref[i * SLOT_PAD : (i + 1) * SLOT_PAD, :] = block.astype(bf16)
     rows = rows_ref[...]
     for start in range(0, up_ref.shape[1], chunk):
         cols = slice(start, start + chunk)
@@ -201,18 +231,17 @@
         active[:, cols] = jax.nn.gelu(lifted, approximate=True).astype(bf16)
     for start in range(0, down_ref.shape[1], chunk):
         cols = slice(start, start + chunk)
-        terms = jnp.dot(active[...], down_ref[:, cols], preferred_element_type=f32)
-        for i, out_ref in enumerate((o0, o1, o2, o3)):
-            out_ref[:, cols] = terms[i * SLOT_PAD : (i + 1) * SLOT_PAD].astype(bf16)
+        terms[:, cols] = jnp.dot(active[...], down_ref[:, cols], preferred_element_type=f32)
+    for i, out_ref in enumerate((o0, o1, o2, o3)):
+        out_ref[...] = fold(terms[i * SLOT_PAD : i * SLOT_PAD + slots, :]).astype(bf16)
 
 
 def finish_kernel(count_ref, t0_ref, t1_ref, t2_ref, t3_ref, hidden_ref, mod_ref, b_down_ref, out_ref):
-    slots = out_ref.shape[1]
     total = t0_ref[...].astype(f32)
     for ref in (t1_ref, t2_ref, t3_ref):
         total = total + ref[...].astype(f32)
-    feed_out = total[:slots] + b_down_ref[...].astype(f32)
-    result = hidden_ref[:slots] + mod_ref[0, 3:4].astype(f32) * feed_out
+    feed_out = unfold(total) + b_down_ref[...].astype(f32)
+    result = hidden_ref[...] + mod_ref[0, 3:4].astype(f32) * feed_out
     live = lax.broadcasted_iota(i32, result.shape, 0) < count_ref[0, 0]
     out_ref[0] = jnp.where(live, result, 0.0).astype(bf16)
 
@@ -239,27 +268,26 @@
     slots, width = rows_in.shape[1], rows_in.shape[2]
     tokens = kv_cache.shape[1]
     fresh = jnp.swapaxes(fresh_qkv[0], 0, 1)
-    q_blocks = call(
-        pack_queries_kernel,
-        shape((32, SLOT_PAD, BLOCK), bf16),
-        scratch=[pltpu.VMEM((slots, width), bf16), pltpu.SemaphoreType.DMA((1,))],
-        n_in=1,
-        hbm=(0,),
-        limit=61,
-    )(fresh)
+    q_blocks, keep, send = pl.pallas_call(
+        pack_kernel,
+        out_shape=[shape((32, SLOT_PAD, BLOCK), bf16)] + [shape((4, 2, tokens, BLOCK), bf16)] * 2,
+        in_specs=[pl.BlockSpec(memory_space=pltpu.SMEM)] + [pl.BlockSpec(memory_space=pltpu.HBM)] * 3,
+        out_specs=[pl.BlockSpec(memory_space=pltpu.HBM)] * 3,
+        scratch_shapes=[
+            pltpu.VMEM((tokens, 2, width), bf16),
+            pltpu.VMEM((3, slots, width), bf16),
+            pltpu.VMEM((1, slots), i32),
+            pltpu.VMEM((2, tokens, width), bf16),
+            pltpu.VMEM((32, SLOT_PAD, BLOCK), bf16),
+            pltpu.SemaphoreType.DMA((4,)),
+            pltpu.SemaphoreType.DMA((17,)),
+        ],
+        compiler_params=pltpu.CompilerParams(vmem_limit_bytes=61 * MB),
+    )(counts, kv_cache[0], fresh, chosen)
     q_all = lax.all_to_all(q_blocks, SEQ, 0, 0, tiled=True)
-
-    keep, send = call(
-        pack_cache_kernel,
-        [shape((4, 2, tokens, BLOCK), bf16)] * 2,
-        scratch=[pltpu.VMEM((2, tokens, width), bf16)],
-        n_in=4,
-        smem=(0,),
-        us=3.0,
-    )(counts, kv_cache[0], fresh, chosen)
     swap = [(position(z, x, c), position(z, x, 1 - c)) for z in range(4) for x in range(4) for c in range(2)]
     first = lax.ppermute(send, SEQ, swap)
-    stacked = call(stack_kernel, [shape((2, 2, tokens, BLOCK), bf16)] * 4, n_in=2, us=0.5)(keep, first)
+    stacked = call(stack_kernel, [shape((2, 2, tokens, BLOCK), bf16)] * 4, n_in=2)(keep, first)
     others = [lax.ppermute(stacked[k], SEQ, ring_pairs(k)) for k in (1, 2, 3)]
 
     partial = call(
@@ -274,7 +302,7 @@
     rows, mod = load(partial, [rows_in, modulation], 16)
     hidden, normed, mark = call(
         combine_kernel,
-        [shape((SLOT_PAD, width), f32), shape((SLOT_PAD, width), bf16), shape((16, 128), bf16)],
+        [shape((slots, width), f32), shape((2 * slots, width // 2), bf16), shape((16, 128), bf16)],
         scratch=[pltpu.VMEM((128, 128), f32), pltpu.VMEM((128, 128), f32)],
         n_in=3,
         us=1.6,
@@ -284,8 +312,12 @@
     up, down = load(mark, [w_up, w_down], 34)
     terms = call(
         feed_kernel,
-        [shape((SLOT_PAD, width), bf16)] * 4,
-        scratch=[pltpu.VMEM((4 * SLOT_PAD, width), bf16), pltpu.VMEM((4 * SLOT_PAD, w_up.shape[1]), bf16)],
+        [shape((2 * slots, width // 2), bf16)] * 4,
+        scratch=[
+            pltpu.VMEM((4 * SLOT_PAD, width), bf16),
+            pltpu.VMEM((4 * SLOT_PAD, w_up.shape[1]), bf16),
+            pltpu.VMEM((4 * SLOT_PAD, width), f32),
+        ],
         n_in=7,
         us=3.7,
     )(normed, *visits, up, b_up[None], down)

time: 96.6 us -> 90.9 us (0.941)
  waiting for transfers between devices: 39.8 us -> 36.5 us
  local copies, waits for them, and re-layouts: 3.15 us -> 1.16 us
    unnamed x14 -> x10, local copies, waits for them, and re-layouts: 3.14 us -> 1.14 us
    ppermute x3, waiting for transfers between devices: 10.2 us -> 8.91 us  [body(): back = [lax.ppermute(terms[k], 'y', turn(-k)) for k in (1, 2, 3)]]
    ppermute x3, waiting for transfers between devices: 1.18 us -> 0.12 us  [body(): visits = [lax.ppermute(normed, 'y', turn(k)) for k in (1, 2, 3)]]
    pallas_call x5 -> x4, Pallas kernels: 8.89 us -> 8.48 us  [the longest x1 3.57 us: body(): pl.pallas_call(pack_kernel, out_shape=[shape((32, SLOT_PAD, BLOCK), bf16)...]
  transfers between devices with their start and end apart: 12 -> 12, of which waited for: 8 -> 8; matrix products, arithmetic and copies ran while one was open for 0% -> 0% of each run, Pallas kernels for 10% -> 8%
where the time goes in v4:
time: 90.9 us; the launch traced here: 89.7 us
  waiting for transfers between devices  36.5 us (40%)
  starting transfers between devices  29.6 us (33%)
  Pallas kernels  21.6 us (24%)
  local copies, waits for them, and re-layouts  1.16 us (1%)
    all_to_all x1, waiting for transfers between devices, body(): parts = lax.all_to_all(partial, SEQ, 0, 0, tiled=True)  14.2 us
    ppermute x3, waiting for transfers between devices, body(): back = [lax.ppermute(terms[k], 'y', turn(-k)) for k in (1, 2, 3)]  8.91 us
    all_to_all x1, starting transfers between devices, body(): q_all = lax.all_to_all(q_blocks, SEQ, 0, 0, tiled=True)  8.34 us
    pallas_call x2, Pallas kernels, load(): call(load_kernel, [jax.ShapeDtypeStruct(v.shape, bf16) for v in arrays],...  6.69 us
    ppermute x3, waiting for transfers between devices, body(): others = [lax.ppermute(stacked[k], SEQ, ring_pairs(k)) for k in (1, 2, 3)]  6.67 us
    all_to_all x1, waiting for transfers between devices, body(): q_all = lax.all_to_all(q_blocks, SEQ, 0, 0, tiled=True)  6.59 us
    ppermute x3, starting transfers between devices, body(): others = [lax.ppermute(stacked[k], SEQ, ring_pairs(k)) for k in (1, 2, 3)]  5.93 us
    ppermute x3, starting transfers between devices, body(): visits = [lax.ppermute(normed, 'y', turn(k)) for k in (1, 2, 3)]  5.91 us
  transfers between devices with their start and end apart: 12, of which 8 were waited for; matrix products, arithmetic and copies ran while one was open for 0% of the time, Pallas kernels for 8%

profile of v4, /device:TPU:0, one launch (start us, length us, event | category | flops | bytes accessed | tf_op | source)
XLA Modules:
  0.0 89.7 jit_solution(3381235616372434943)
XLA Ops:
  0.7 3.6 %shard_map.100 = (bf16[32,32,384]{2,1,0:T(8,128)(2,1)}, bf16[4,2,128,384]{3,2,1,0:T(8,128)(2,1)}, bf16[4,2,128,384]{3,2,1,0:T(8,128)(2,1)}) custom-call(s32[1,1]{1,0:T(1,128)S(6)} %copy.11.count_ref, bf16[128,2,3072]{2,1,0:T(2,128)(2,1)} %bitcast.4, bf16[3,28,3072]{2,1,0:T(8,128)(2,1)} %bitcast.5, s32[1,28]{1,0:T(1,128)} %chosen_hbm.1), custom_call_target="tpu_custom_call" | custom-call | tf_op jit(solution)/shard_map/pallas_call | solution.py:271
  4.3 0.1 collective-permute-start
  4.4 8.3 %all-to-all-start = ((bf16[32,32,384]{2,1,0:T(8,128)(2,1)}), bf16[32,32,384]{2,1,0:T(8,128)(2,1)S(1)}, u32[]{:S(2)}, u32[]{:S(2)}) async-start(bf16[32,32,384]{2,1,0:T(8,128)(2,1)} %get-tuple-element.23), calls=%async_computation | async-start | bytes 1572864 | tf_op jit(solution)/shard_map/all_to_all | solution.py:287
  12.7 0.0 collective-permute-done.first_ref
  12.7 1.1 %copy-done = bf16[4,2,128,384]{3,2,1,0:T(8,128)(2,1)S(1)} copy-done((bf16[4,2,128,384]{3,2,1,0:T(8,128)(2,1)S(1)}, bf16[4,2,128,384]{3,2,1,0:T(8,128)(2,1)}, u32[]{:S(2)}) %copy-start) | copy-done | bytes 786456
  13.9 0.9 %shard_map.101 = (bf16[2,2,128,384]{3,2,1,0:T(8,128)(2,1)S(1)}, bf16[2,2,128,384]{3,2,1,0:T(8,128)(2,1)}, bf16[2,2,128,384]{3,2,1,0:T(8,128)(2,1)S(1)}, bf16[2,2,128,384]{3,2,1,0:T(8,128)(2,1)S(1)}) custom-call(bf16[4,2,128,384]{3,2,1,0:T(8,128)(2,1)S(1)} %copy-done, bf16[4,2,128,384]{3,2,1,0:T(8,128)(2,1)S(1)} %collective-permute-done.first_ref), custom_call_target="tpu_custom_call" | custom-call | bytes 3300000 | tf_op jit(solution)/shard_map/pallas_call | solution.py:290
  14.8 1.8 %collective-permute-start.1 = (bf16[2,2,128,384]{3,2,1,0:T(8,128)(2,1)}, bf16[2,2,128,384]{3,2,1,0:T(8,128)(2,1)S(1)}, u32[]{:S(2)}, u32[]{:S(2)}) collective-permute-start(bf16[2,2,128,384]{3,2,1,0:T(8,128)(2,1)} %get-tuple-element.27), channel_id=1, source_target_pairs={{0,2},{1,9},{2,4},{3,11},{4,6},{5,13},{6,0},{7,15},{8,10},{9,17},{... | collective-permute-start | bytes 1179656 | tf_op jit(solution)/shard_map/ppermute | solution.py:291
  16.6 2.7 %collective-permute-start.2 = (bf16[2,2,128,384]{3,2,1,0:T(8,128)(2,1)S(1)}, bf16[2,2,128,384]{3,2,1,0:T(8,128)(2,1)S(1)}, u32[]{:S(2)}, u32[]{:S(2)}) collective-permute-start(bf16[2,2,128,384]{3,2,1,0:T(8,128)(2,1)S(1)} %get-tuple-element.28), channel_id=1, source_target_pairs={{0,4},{1,17},{2,6},{3,19},{4,0},{5,21},{6,2},{7,23},{8,12},{9,25},... | collective-permute-start | bytes 1179656 | tf_op jit(solution)/shard_map/ppermute | solution.py:291
  19.2 1.5 %collective-permute-start.3 = (bf16[2,2,128,384]{3,2,1,0:T(8,128)(2,1)S(1)}, bf16[2,2,128,384]{3,2,1,0:T(8,128)(2,1)S(1)}, u32[]{:S(2)}, u32[]{:S(2)}) collective-permute-start(bf16[2,2,128,384]{3,2,1,0:T(8,128)(2,1)S(1)} %get-tuple-element.29), channel_id=1, source_target_pairs={{0,6},{1,25},{2,0},{3,27},{4,2},{5,29},{6,4},{7,31},{8,14},{9,1},{... | collective-permute-start | bytes 1179656 | tf_op jit(solution)/shard_map/ppermute | solution.py:291
  20.7 6.6 %all-to-all-done.q_ref = bf16[32,32,384]{2,1,0:T(8,128)(2,1)S(1)} async-done(((bf16[32,32,384]{2,1,0:T(8,128)(2,1)}), bf16[32,32,384]{2,1,0:T(8,128)(2,1)S(1)}, u32[]{:S(2)}, u32[]{:S(2)}) %all-to-all-start) | async-done | bytes 786464 | tf_op jit(solution)/shard_map/all_to_all | solution.py:287
  27.3 2.2 %collective-permute-done.1.r1_ref = bf16[2,2,128,384]{3,2,1,0:T(8,128)(2,1)S(1)} collective-permute-done((bf16[2,2,128,384]{3,2,1,0:T(8,128)(2,1)}, bf16[2,2,128,384]{3,2,1,0:T(8,128)(2,1)S(1)}, u32[]{:S(2)}, u32[]{:S(2)}) %collective-permute-start.1) | collective-permute-done | bytes 393248 | tf_op jit(solution)/shard_map/ppermute | solution.py:291
  29.5 4.5 %collective-permute-done.2.r2_ref = bf16[2,2,128,384]{3,2,1,0:T(8,128)(2,1)S(1)} collective-permute-done((bf16[2,2,128,384]{3,2,1,0:T(8,128)(2,1)S(1)}, bf16[2,2,128,384]{3,2,1,0:T(8,128)(2,1)S(1)}, u32[]{:S(2)}, u32[]{:S(2)}) %collective-permute-start.2) | collective-permute-done | bytes 393248 | tf_op jit(solution)/shard_map/ppermute | solution.py:291
  34.0 0.0 collective-permute-done.3.r3_ref
  34.0 5.6 %shard_map.102.after_ref = bf16[32,32,384]{2,1,0:T(8,128)(2,1)} custom-call(bf16[32,32,384]{2,1,0:T(8,128)(2,1)S(1)} %all-to-all-done.q_ref, bf16[2,2,128,384]{3,2,1,0:T(8,128)(2,1)S(1)} %get-tuple-element.26.r0_ref, bf16[2,2,128,384]{3,2,1,0:T(8,128)(2,1)S(1)} %collective-permute-done.1.r1_ref, bf16[2,2,128,384]{3,2,1,0:T(8,128)(2,1)S(1)} %collective-permute-done.2.r2_ref, ...), custom_call_target="tpu_custom_call" | custom-call | bytes 21450000 | tf_op jit(solution)/shard_map/pallas_call | solution.py:293
  39.6 5.3 %all-to-all-start.1 = ((bf16[32,32,384]{2,1,0:T(8,128)(2,1)}), bf16[32,32,384]{2,1,0:T(8,128)(2,1)S(1)}, u32[]{:S(2)}, u32[]{:S(2)}) async-start(bf16[32,32,384]{2,1,0:T(8,128)(2,1)} %shard_map.102.after_ref), calls=%async_computation.1 | async-start | bytes 1572864 | tf_op jit(solution)/shard_map/all_to_all | solution.py:301
  44.9 0.3 shard_map.103
  45.2 14.2 %all-to-all-done.1.parts_ref = bf16[32,32,384]{2,1,0:T(8,128)(2,1)S(1)} async-done(((bf16[32,32,384]{2,1,0:T(8,128)(2,1)}), bf16[32,32,384]{2,1,0:T(8,128)(2,1)S(1)}, u32[]{:S(2)}, u32[]{:S(2)}) %all-to-all-start.1) | async-done | bytes 786464 | tf_op jit(solution)/shard_map/all_to_all | solution.py:301
  59.4 1.1 %shard_map.104 = (f32[28,3072]{1,0:T(8,128)S(1)}, bf16[56,1536]{1,0:T(8,128)(2,1)S(1)}, bf16[16,128]{1,0:T(8,128)(2,1)S(1)}) custom-call(bf16[32,32,384]{2,1,0:T(8,128)(2,1)S(1)} %all-to-all-done.1.parts_ref, bf16[1,28,3072]{2,1,0:T(8,128)(2,1)S(1)} %get-tuple-element.30.rows_ref, bf16[1,4,3072]{2,1,0:T(4,128)(2,1)S(1)} %get-tuple-element.31.mod_ref), custom_call_target="tpu_custom_call" | custom-call | bytes 5280000 | tf_op jit(solution)/shard_map/pallas_call | solution.py:303
  60.6 1.6 %collective-permute-start.4 = (bf16[56,1536]{1,0:T(8,128)(2,1)S(1)}, bf16[56,1536]{1,0:T(8,128)(2,1)S(1)}, u32[]{:S(2)}, u32[]{:S(2)}) collective-permute-start(bf16[56,1536]{1,0:T(8,128)(2,1)S(1)} %get-tuple-element.32.r0_ref), channel_id=1, source_target_pairs={{0,32},{32,64},{64,96},{96,0},{1,33},{33,65},{65,97},{97,1},{2,34}... | collective-permute-start | bytes 516104 | tf_op jit(solution)/shard_map/ppermute | solution.py:311
  62.2 2.9 %collective-permute-start.5 = (bf16[56,1536]{1,0:T(8,128)(2,1)S(1)}, bf16[56,1536]{1,0:T(8,128)(2,1)S(1)}, u32[]{:S(2)}, u32[]{:S(2)}) collective-permute-start(bf16[56,1536]{1,0:T(8,128)(2,1)S(1)} %get-tuple-element.32.r0_ref), channel_id=1, source_target_pairs={{0,64},{32,96},{64,0},{96,32},{1,65},{33,97},{65,1},{97,33},{2,66}... | collective-permute-start | bytes 516104 | tf_op jit(solution)/shard_map/ppermute | solution.py:311
  65.1 1.3 %collective-permute-start.6 = (bf16[56,1536]{1,0:T(8,128)(2,1)S(1)}, bf16[56,1536]{1,0:T(8,128)(2,1)S(1)}, u32[]{:S(2)}, u32[]{:S(2)}) collective-permute-start(bf16[56,1536]{1,0:T(8,128)(2,1)S(1)} %get-tuple-element.32.r0_ref), channel_id=1, source_target_pairs={{0,96},{32,0},{64,32},{96,64},{1,97},{33,1},{65,33},{97,65},{2,98}... | collective-permute-start | bytes 516104 | tf_op jit(solution)/shard_map/ppermute | solution.py:311
  66.5 6.4 %shard_map.105 = (bf16[3072,1536]{1,0:T(8,128)(2,1)S(1)}, bf16[1536,3072]{1,0:T(8,128)(2,1)S(1)}) custom-call(bf16[16,128]{1,0:T(8,128)(2,1)S(1)} %get-tuple-element.33.after_ref, bf16[3072,1536]{1,0:T(8,128)(2,1)} %refs_0_.3, bf16[1536,3072]{1,0:T(8,128)(2,1)} %refs_1_.3), custom_call_target="tpu_custom_call" | custom-call | bytes 11880000 | tf_op jit(solution)/shard_map/pallas_call | solution.py:206
  72.9 0.0 collective-permute-done.4.r1_ref
  72.9 0.1 collective-permute-done.5.r2_ref
  73.0 2.9 %shard_map.106 = (bf16[56,1536]{1,0:T(8,128)(2,1)S(1)}, bf16[56,1536]{1,0:T(8,128)(2,1)S(1)}, bf16[56,1536]{1,0:T(8,128)(2,1)S(1)}, bf16[56,1536]{1,0:T(8,128)(2,1)S(1)}) custom-call(bf16[56,1536]{1,0:T(8,128)(2,1)S(1)} %get-tuple-element.32.r0_ref, bf16[56,1536]{1,0:T(8,128)(2,1)S(1)} %collective-permute-done.4.r1_ref, ...), custom_call_target="tpu_custom_call" | custom-call | bytes 12210000 | tf_op jit(solution)/shard_map/pallas_call | solution.py:313
  75.9 2.2 %collective-permute-start.7 = (bf16[56,1536]{1,0:T(8,128)(2,1)S(1)}, bf16[56,1536]{1,0:T(8,128)(2,1)S(1)}, u32[]{:S(2)}, u32[]{:S(2)}) collective-permute-start(bf16[56,1536]{1,0:T(8,128)(2,1)S(1)} %get-tuple-element.37), channel_id=1, source_target_pairs={{0,96},{32,0},{64,32},{96,64},{1,97},{33,1},{65,33},{97,65},{2,98}... | collective-permute-start | bytes 516104 | tf_op jit(solution)/shard_map/ppermute | solution.py:324
  78.1 1.1 %collective-permute-start.8 = (bf16[56,1536]{1,0:T(8,128)(2,1)S(1)}, bf16[56,1536]{1,0:T(8,128)(2,1)S(1)}, u32[]{:S(2)}, u32[]{:S(2)}) collective-permute-start(bf16[56,1536]{1,0:T(8,128)(2,1)S(1)} %get-tuple-element.38), channel_id=1, source_target_pairs={{0,64},{32,96},{64,0},{96,32},{1,65},{33,97},{65,1},{97,33},{2,66}... | collective-permute-start | bytes 516104 | tf_op jit(solution)/shard_map/ppermute | solution.py:324
  79.2 0.7 collective-permute-start.9
  80.0 5.2 %collective-permute-done.7.t1_ref = bf16[56,1536]{1,0:T(8,128)(2,1)S(1)} collective-permute-done((bf16[56,1536]{1,0:T(8,128)(2,1)S(1)}, bf16[56,1536]{1,0:T(8,128)(2,1)S(1)}, u32[]{:S(2)}, u32[]{:S(2)}) %collective-permute-start.7) | collective-permute-done | bytes 172064 | tf_op jit(solution)/shard_map/ppermute | solution.py:324
  85.2 1.7 %collective-permute-done.8.t2_ref = bf16[56,1536]{1,0:T(8,128)(2,1)S(1)} collective-permute-done((bf16[56,1536]{1,0:T(8,128)(2,1)S(1)}, bf16[56,1536]{1,0:T(8,128)(2,1)S(1)}, u32[]{:S(2)}, u32[]{:S(2)}) %collective-permute-start.8) | collective-permute-done | bytes 172064 | tf_op jit(solution)/shard_map/ppermute | solution.py:324
  86.9 1.9 %collective-permute-done.9.t3_ref = bf16[56,1536]{1,0:T(8,128)(2,1)S(1)} collective-permute-done((bf16[56,1536]{1,0:T(8,128)(2,1)S(1)}, bf16[56,1536]{1,0:T(8,128)(2,1)S(1)}, u32[]{:S(2)}, u32[]{:S(2)}) %collective-permute-start.9) | collective-permute-done | bytes 172064 | tf_op jit(solution)/shard_map/ppermute | solution.py:324
  88.9 0.9 shard_map.107
  (12 shorter events, 0.0 us)
Async XLA Ops:
  0.0 44.9 %copy-start.1 = (bf16[1,28,3072]{2,1,0:T(8,128)(2,1)S(1)}, bf16[1,28,3072]{2,1,0:T(8,128)(2,1)}, u32[]{:S(2)}) copy-start(bf16[1,28,3072]{2,1,0:T(8,128)(2,1)} %refs_0_.2) | copy-start | bytes 516100
  0.0 44.9 %copy-start.2 = (bf16[1,4,3072]{2,1,0:T(4,128)(2,1)S(1)}, bf16[1,4,3072]{2,1,0:T(4,128)(2,1)}, u32[]{:S(2)}) copy-start(bf16[1,4,3072]{2,1,0:T(4,128)(2,1)} %mod_ref.1) | copy-start | bytes 73732
  0.0 66.5 %copy-start.4 = (bf16[1536]{0:T(1024)(128)(2,1)S(1)}, bf16[1536]{0:T(1024)(128)(2,1)}, u32[]{:S(2)}) copy-start(bf16[1536]{0:T(1024)(128)(2,1)} %param.17) | copy-start | bytes 9220
  4.3 8.4 %collective-permute-start = (bf16[4,2,128,384]{3,2,1,0:T(8,128)(2,1)}, bf16[4,2,128,384]{3,2,1,0:T(8,128)(2,1)S(1)}, u32[]{:S(2)}, u32[]{:S(2)}) collective-permute-start(bf16[4,2,128,384]{3,2,1,0:T(8,128)(2,1)} %get-tuple-element.25), channel_id=1, source_target_pairs={{0,1},{1,0},{2,3},{3,2},{4,5},{5,4},{6,7},{7,6},{8,9},{9,8},{10,11... | collective-permute-start | bytes 2359304 | tf_op jit(solution)/shard_map/ppermute | solution.py:289
  4.4 22.9 %all-to-all-start = ((bf16[32,32,384]{2,1,0:T(8,128)(2,1)}), bf16[32,32,384]{2,1,0:T(8,128)(2,1)S(1)}, u32[]{:S(2)}, u32[]{:S(2)}) async-start(bf16[32,32,384]{2,1,0:T(8,128)(2,1)} %get-tuple-element.23), calls=%async_computation | async-start | bytes 1572864 | tf_op jit(solution)/shard_map/all_to_all | solution.py:287
  12.7 1.1 %copy-start = (bf16[4,2,128,384]{3,2,1,0:T(8,128)(2,1)S(1)}, bf16[4,2,128,384]{3,2,1,0:T(8,128)(2,1)}, u32[]{:S(2)}) copy-start(bf16[4,2,128,384]{3,2,1,0:T(8,128)(2,1)} %get-tuple-element.24.keep_ref) | copy-start | bytes 2359300
  14.8 14.7 %collective-permute-start.1 = (bf16[2,2,128,384]{3,2,1,0:T(8,128)(2,1)}, bf16[2,2,128,384]{3,2,1,0:T(8,128)(2,1)S(1)}, u32[]{:S(2)}, u32[]{:S(2)}) collective-permute-start(bf16[2,2,128,384]{3,2,1,0:T(8,128)(2,1)} %get-tuple-element.27), channel_id=1, source_target_pairs={{0,2},{1,9},{2,4},{3,11},{4,6},{5,13},{6,0},{7,15},{8,10},{9,17},{... | collective-permute-start | bytes 1179656 | tf_op jit(solution)/shard_map/ppermute | solution.py:291
  16.6 17.4 %collective-permute-start.2 = (bf16[2,2,128,384]{3,2,1,0:T(8,128)(2,1)S(1)}, bf16[2,2,128,384]{3,2,1,0:T(8,128)(2,1)S(1)}, u32[]{:S(2)}, u32[]{:S(2)}) collective-permute-start(bf16[2,2,128,384]{3,2,1,0:T(8,128)(2,1)S(1)} %get-tuple-element.28), channel_id=1, source_target_pairs={{0,4},{1,17},{2,6},{3,19},{4,0},{5,21},{6,2},{7,23},{8,12},{9,25},... | collective-permute-start | bytes 1179656 | tf_op jit(solution)/shard_map/ppermute | solution.py:291
  19.2 14.7 %collective-permute-start.3 = (bf16[2,2,128,384]{3,2,1,0:T(8,128)(2,1)S(1)}, bf16[2,2,128,384]{3,2,1,0:T(8,128)(2,1)S(1)}, u32[]{:S(2)}, u32[]{:S(2)}) collective-permute-start(bf16[2,2,128,384]{3,2,1,0:T(8,128)(2,1)S(1)} %get-tuple-element.29), channel_id=1, source_target_pairs={{0,6},{1,25},{2,0},{3,27},{4,2},{5,29},{6,4},{7,31},{8,14},{9,1},{... | collective-permute-start | bytes 1179656 | tf_op jit(solution)/shard_map/ppermute | solution.py:291
  39.6 19.9 %all-to-all-start.1 = ((bf16[32,32,384]{2,1,0:T(8,128)(2,1)}), bf16[32,32,384]{2,1,0:T(8,128)(2,1)S(1)}, u32[]{:S(2)}, u32[]{:S(2)}) async-start(bf16[32,32,384]{2,1,0:T(8,128)(2,1)} %shard_map.102.after_ref), calls=%async_computation.1 | async-start | bytes 1572864 | tf_op jit(solution)/shard_map/all_to_all | solution.py:301
  60.6 12.3 %collective-permute-start.4 = (bf16[56,1536]{1,0:T(8,128)(2,1)S(1)}, bf16[56,1536]{1,0:T(8,128)(2,1)S(1)}, u32[]{:S(2)}, u32[]{:S(2)}) collective-permute-start(bf16[56,1536]{1,0:T(8,128)(2,1)S(1)} %get-tuple-element.32.r0_ref), channel_id=1, source_target_pairs={{0,32},{32,64},{64,96},{96,0},{1,33},{33,65},{65,97},{97,1},{2,34}... | collective-permute-start | bytes 516104 | tf_op jit(solution)/shard_map/ppermute | solution.py:311
  62.2 10.8 %collective-permute-start.5 = (bf16[56,1536]{1,0:T(8,128)(2,1)S(1)}, bf16[56,1536]{1,0:T(8,128)(2,1)S(1)}, u32[]{:S(2)}, u32[]{:S(2)}) collective-permute-start(bf16[56,1536]{1,0:T(8,128)(2,1)S(1)} %get-tuple-element.32.r0_ref), channel_id=1, source_target_pairs={{0,64},{32,96},{64,0},{96,32},{1,65},{33,97},{65,1},{97,33},{2,66}... | collective-permute-start | bytes 516104 | tf_op jit(solution)/shard_map/ppermute | solution.py:311
  65.1 7.9 %collective-permute-start.6 = (bf16[56,1536]{1,0:T(8,128)(2,1)S(1)}, bf16[56,1536]{1,0:T(8,128)(2,1)S(1)}, u32[]{:S(2)}, u32[]{:S(2)}) collective-permute-start(bf16[56,1536]{1,0:T(8,128)(2,1)S(1)} %get-tuple-element.32.r0_ref), channel_id=1, source_target_pairs={{0,96},{32,0},{64,32},{96,64},{1,97},{33,1},{65,33},{97,65},{2,98}... | collective-permute-start | bytes 516104 | tf_op jit(solution)/shard_map/ppermute | solution.py:311
  73.0 7.0 %copy-start.3 = (bf16[3072]{0:T(1024)(128)(2,1)S(1)}, bf16[3072]{0:T(1024)(128)(2,1)}, u32[]{:S(2)}) copy-start(bf16[3072]{0:T(1024)(128)(2,1)} %param.19) | copy-start | bytes 18436
  75.9 9.3 %collective-permute-start.7 = (bf16[56,1536]{1,0:T(8,128)(2,1)S(1)}, bf16[56,1536]{1,0:T(8,128)(2,1)S(1)}, u32[]{:S(2)}, u32[]{:S(2)}) collective-permute-start(bf16[56,1536]{1,0:T(8,128)(2,1)S(1)} %get-tuple-element.37), channel_id=1, source_target_pairs={{0,96},{32,0},{64,32},{96,64},{1,97},{33,1},{65,33},{97,65},{2,98}... | collective-permute-start | bytes 516104 | tf_op jit(solution)/shard_map/ppermute | solution.py:324
  78.1 8.8 %collective-permute-start.8 = (bf16[56,1536]{1,0:T(8,128)(2,1)S(1)}, bf16[56,1536]{1,0:T(8,128)(2,1)S(1)}, u32[]{:S(2)}, u32[]{:S(2)}) collective-permute-start(bf16[56,1536]{1,0:T(8,128)(2,1)S(1)} %get-tuple-element.38), channel_id=1, source_target_pairs={{0,64},{32,96},{64,0},{96,32},{1,65},{33,97},{65,1},{97,33},{2,66}... | collective-permute-start | bytes 516104 | tf_op jit(solution)/shard_map/ppermute | solution.py:324
  79.2 9.6 %collective-permute-start.9 = (bf16[56,1536]{1,0:T(8,128)(2,1)S(1)}, bf16[56,1536]{1,0:T(8,128)(2,1)S(1)}, u32[]{:S(2)}, u32[]{:S(2)}) collective-permute-start(bf16[56,1536]{1,0:T(8,128)(2,1)S(1)} %get-tuple-element.39), channel_id=1, source_target_pairs={{0,32},{32,64},{64,96},{96,0},{1,33},{33,65},{65,97},{97,1},{2,34}... | collective-permute-start | bytes 516104 | tf_op jit(solution)/shard_map/ppermute | solution.py:324

commit v5 on v4

--- a/solution.py
+++ b/solution.py
@@ -41,8 +41,8 @@
 
 
 def pack_kernel(
-    count_ref, kv_hbm, fresh_hbm, chosen_hbm, q_hbm, keep_hbm, send_hbm,
-    kv_ref, fresh_ref, chosen_ref, patched, q_out, in_sems, out_sems,
+    count_ref, kv_hbm, fresh_hbm, chosen_hbm, keep_hbm, send_hbm,
+    kv_ref, fresh_ref, chosen_ref, patched, queries, in_sems, out_sems,
 ):
     sources = [
         (fresh_hbm.at[0], fresh_ref.at[0]),
@@ -55,17 +55,28 @@
         copy.start()
     tokens = kv_ref.shape[0]
     slots = fresh_ref.shape[1]
-    copies[0].wait()
-    for dest in range(32):
-        z, x, core = dest // 8, dest // 2 % 4, dest % 2
-        group = x if core == 0 else 4 + z
-        q_out[dest, :slots, :] = fresh_ref[0, :, group * BLOCK : (group + 1) * BLOCK]
-        q_out[dest, slots:, :] = jnp.zeros((SLOT_PAD - slots, BLOCK), bf16)
-    outs = [pltpu.make_async_copy(q_out, q_hbm, out_sems.at[0])]
-    outs[0].start()
-
     core, ring_x, ring_z = (lax.axis_index(a) for a in ("core", "x", "z"))
     count = count_ref[0, 0]
+    half = 4 * BLOCK
+    outs = []
+
+    def send_out(source, first_row, rows, k, mine, other):
+        at_mine = pl.multiple_of(core * half + mine * BLOCK, BLOCK)
+        at_other = pl.multiple_of((1 - core) * half + other * BLOCK, BLOCK)
+        for at, target in ((at_other, send_hbm), (at_mine, keep_hbm)):
+            copy = pltpu.make_async_copy(
+                source.at[:, pl.ds(at, BLOCK)],
+                target.at[k, pl.ds(first_row, rows)],
+                out_sems.at[len(outs)],
+            )
+            copy.start()
+            outs.append(copy)
+
+    copies[0].wait()
+    queries[:slots, :] = fresh_ref[0]
+    queries[slots:, :] = jnp.zeros((SLOT_PAD - slots, queries.shape[1]), bf16)
+    for k in range(4):
+        send_out(queries, 2 * tokens, SLOT_PAD, k, k, k)
     for copy in copies[1:]:
         copy.wait()
     token_id = lax.broadcasted_iota(i32, (tokens, slots), 0)
@@ -75,72 +86,90 @@
     taken = jnp.sum(hot, axis=1, keepdims=True) > 0.5
     hot = hot.astype(bf16)
     old = jnp.swapaxes(kv_ref[...], 0, 1)
-    half = 4 * BLOCK
     for which in range(2):
         new = jnp.dot(hot, fresh_ref[1 + which], preferred_element_type=f32)
         patched[which] = jnp.where(taken, new, old[which].astype(f32)).astype(bf16)
         for k in range(4):
             mine = lax.rem(jnp.where(core == 0, ring_x, ring_z) + k, 4)
             other = lax.rem(jnp.where(core == 0, ring_z, ring_x) + k, 4)
-            at_mine = pl.multiple_of(core * half + mine * BLOCK, BLOCK)
-            at_other = pl.multiple_of((1 - core) * half + other * BLOCK, BLOCK)
-            for at, target in ((at_other, send_hbm), (at_mine, keep_hbm)):
-                copy = pltpu.make_async_copy(
-                    patched.at[which, :, pl.ds(at, BLOCK)], target.at[k, which], out_sems.at[len(outs)]
-                )
-                copy.start()
-                outs.append(copy)
+            send_out(patched.at[which], which * tokens, tokens, k, mine, other)
     for copy in outs:
         copy.wait()
 
 
-def stack_kernel(keep_ref, first_ref, *out_refs):
-    for k, out_ref in enumerate(out_refs):
-        out_ref[0] = keep_ref[k]
-        out_ref[1] = first_ref[k]
-
-
-def attention_kernel(q_ref, r0_ref, r1_ref, r2_ref, r3_ref, out_ref, keys, values_t):
-    sources = [ref.at[core] for ref in (r0_ref, r1_ref, r2_ref, r3_ref) for core in range(2)]
-    for i, ref in enumerate(sources):
-        keys[i * 128 : (i + 1) * 128, :] = ref[0]
-        for h in range(HEADS_HERE):
-            cols = slice(h * HEAD_DIM, (h + 1) * HEAD_DIM)
-            values_t[h, :, i * 128 : (i + 1) * 128] = ref[1, :, cols].T
-    scale = LOG2E * HEAD_DIM**-0.5
-    tile = 1024
-    blocks = tile // SLOT_PAD
-
-    def step(t, _):
-        q_all = q_ref[pl.ds(t * blocks, blocks)].reshape(tile, BLOCK)
-        for h in range(HEADS_HERE):
-            cols = slice(h * HEAD_DIM, (h + 1) * HEAD_DIM)
-            scores = lax.dot_general(
-                keys[:, cols], q_all[:, cols], (((1,), (1,)), ((), ())), preferred_element_type=f32
-            )
-            top = jnp.max(scores, axis=0, keepdims=True)
-            weights = jnp.exp2((scores - top) * scale)
-            mass = jnp.sum(weights, axis=0, keepdims=True)
-            mixed = jnp.dot(values_t[h], weights.astype(bf16), preferred_element_type=f32)
-            mixed = mixed * (1.0 / mass)
-            level = top * scale + jnp.log2(mass)
-            p0 = level.astype(bf16).astype(f32)
-            rest = level - p0
-            p1 = rest.astype(bf16).astype(f32)
-            p2 = rest - p1
-            for g in range(tile // 128):
-                lanes = slice(g * 128, (g + 1) * 128)
-                turned = mixed[:, lanes].T
-                row = lax.broadcasted_iota(i32, (128, HEAD_DIM), 0) % SLOT_PAD
-                turned = jnp.where(row == 28, p0[:, lanes], turned)
-                turned = jnp.where(row == 29, p1[:, lanes], turned)
-                turned = jnp.where(row == 30, p2[:, lanes], turned)
-                out_ref[pl.ds(t * blocks + g * 4, 4), :, cols] = turned.astype(bf16).reshape(
-                    4, SLOT_PAD, HEAD_DIM
-                )
-        return 0
-
-    lax.fori_loop(0, q_ref.shape[0] // blocks, step, 0)
+def stack_kernel(keep_ref, first_ref, *refs):
+    core = lax.axis_index("core")
+    rows = refs[0].shape[1]
+    for k, out_ref in enumerate(refs[:4]):
+        out_ref[0] = keep_ref[k, :rows]
+        out_ref[1] = first_ref[k, :rows]
+    q_ref = refs[4]
+    for chip in range(16):
+        group = jnp.where(core == 0, chip % 4, chip // 4)
+        q_ref[chip, core] = keep_ref[group, rows:]
+        q_ref[chip, 1 - core] = first_ref[group, rows:]
+
+
+def gather_keys(sources, keys, values_t):
+    rows = 128
+    at = 0
+    for ref in sources:
+        for core in range(2):
+            keys[at : at + rows, :] = ref[core, :rows, :]
+            for h in range(HEADS_HERE):
+                cols = slice(h * HEAD_DIM, (h + 1) * HEAD_DIM)
+                values_t[h, :, at : at + rows] = ref[core, rows:, cols].T
+            at += rows
+
+
+def head_scores(q_all, keys, h):
+    cols = slice(h * HEAD_DIM, (h + 1) * HEAD_DIM)
+    return lax.dot_general(
+        keys[:, cols], q_all[:, cols], (((1,), (1,)), ((), ())), preferred_element_type=f32
+    )
+
+
+SCALE = LOG2E * HEAD_DIM**-0.5
+
+
+def attention_first_kernel(q_ref, r0_ref, r1_ref, mixed_ref, stats_ref, keys, values_t):
+    gather_keys((r0_ref, r1_ref), keys, values_t)
+    q_all = q_ref[...].reshape(-1, BLOCK)
+    for h in range(HEADS_HERE):
+        scores = head_scores(q_all, keys, h)
+        top = jnp.max(scores, axis=0, keepdims=True)
+        weights = jnp.exp2((scores - top) * SCALE)
+        stats_ref[h : h + 1, :] = top
+        stats_ref[4 + h : 5 + h, :] = jnp.sum(weights, axis=0, keepdims=True)
+        mixed_ref[h] = jnp.dot(values_t[h], weights.astype(bf16), preferred_element_type=f32)
+
+
+def attention_second_kernel(q_ref, r2_ref, r3_ref, mixed_ref, stats_ref, out_ref, keys, values_t):
+    gather_keys((r2_ref, r3_ref), keys, values_t)
+    q_all = q_ref[...].reshape(-1, BLOCK)
+    for h in range(HEADS_HERE):
+        cols = slice(h * HEAD_DIM, (h + 1) * HEAD_DIM)
+        scores = head_scores(q_all, keys, h)
+        before = stats_ref[h : h + 1, :]
+        top = jnp.maximum(jnp.max(scores, axis=0, keepdims=True), before)
+        weights = jnp.exp2((scores - top) * SCALE)
+        shrink = jnp.exp2((before - top) * SCALE)
+        mass = jnp.sum(weights, axis=0, keepdims=True) + shrink * stats_ref[4 + h : 5 + h, :]
+        mixed = jnp.dot(values_t[h], weights.astype(bf16), preferred_element_type=f32)
+        mixed = (mixed + shrink * mixed_ref[h]) * (1.0 / mass)
+        level = top * SCALE + jnp.log2(mass)
+        p0 = level.astype(bf16).astype(f32)
+        rest = level - p0
+        p1 = rest.astype(bf16).astype(f32)
+        p2 = rest - p1
+        for g in range(q_all.shape[0] // 128):
+            lanes = slice(g * 128, (g + 1) * 128)
+            turned = mixed[:, lanes].T
+            row = lax.broadcasted_iota(i32, (128, HEAD_DIM), 0) % SLOT_PAD
+            turned = jnp.where(row == 28, p0[:, lanes], turned)
+            turned = jnp.where(row == 29, p1[:, lanes], turned)
+            turned = jnp.where(row == 30, p2[:, lanes], turned)
+            out_ref[g * 4 : (g + 1) * 4, :, cols] = turned.astype(bf16).reshape(4, SLOT_PAD, HEAD_DIM)
 
 
 def fold(rows):
@@ -268,36 +297,52 @@
     slots, width = rows_in.shape[1], rows_in.shape[2]
     tokens = kv_cache.shape[1]
     fresh = jnp.swapaxes(fresh_qkv[0], 0, 1)
-    q_blocks, keep, send = pl.pallas_call(
+    packed = shape((4, 2 * tokens + SLOT_PAD, BLOCK), bf16)
+    keep, send = pl.pallas_call(
         pack_kernel,
-        out_shape=[shape((32, SLOT_PAD, BLOCK), bf16)] + [shape((4, 2, tokens, BLOCK), bf16)] * 2,
+        out_shape=[packed] * 2,
         in_specs=[pl.BlockSpec(memory_space=pltpu.SMEM)] + [pl.BlockSpec(memory_space=pltpu.HBM)] * 3,
-        out_specs=[pl.BlockSpec(memory_space=pltpu.HBM)] * 3,
+        out_specs=[pl.BlockSpec(memory_space=pltpu.HBM)] * 2,
         scratch_shapes=[
             pltpu.VMEM((tokens, 2, width), bf16),
             pltpu.VMEM((3, slots, width), bf16),
             pltpu.VMEM((1, slots), i32),
             pltpu.VMEM((2, tokens, width), bf16),
-            pltpu.VMEM((32, SLOT_PAD, BLOCK), bf16),
+            pltpu.VMEM((SLOT_PAD, width), bf16),
             pltpu.SemaphoreType.DMA((4,)),
-            pltpu.SemaphoreType.DMA((17,)),
+            pltpu.SemaphoreType.DMA((24,)),
         ],
         compiler_params=pltpu.CompilerParams(vmem_limit_bytes=61 * MB),
     )(counts, kv_cache[0], fresh, chosen)
-    q_all = lax.all_to_all(q_blocks, SEQ, 0, 0, tiled=True)
     swap = [(position(z, x, c), position(z, x, 1 - c)) for z in range(4) for x in range(4) for c in range(2)]
     first = lax.ppermute(send, SEQ, swap)
-    stacked = call(stack_kernel, [shape((2, 2, tokens, BLOCK), bf16)] * 4, n_in=2)(keep, first)
+    *stacked, q_blocks = call(
+        stack_kernel,
+        [shape((2, 2 * tokens, BLOCK), bf16)] * 4 + [shape((16, 2, SLOT_PAD, BLOCK), bf16)],
+        n_in=2,
+    )(keep, first)
     others = [lax.ppermute(stacked[k], SEQ, ring_pairs(k)) for k in (1, 2, 3)]
-
+    q_all = lax.all_to_all(q_blocks.reshape(16, 2 * SLOT_PAD, BLOCK), ("z", "x"), 0, 0, tiled=True)
+    q_all = q_all.reshape(32, SLOT_PAD, BLOCK)
+
+    rows = 32 * SLOT_PAD
+    scratch = [pltpu.VMEM((4 * tokens, BLOCK), bf16), pltpu.VMEM((HEADS_HERE, HEAD_DIM, 4 * tokens), bf16)]
+    mixed, stats = call(
+        attention_first_kernel,
+        [shape((HEADS_HERE, HEAD_DIM, rows), f32), shape((8, rows), f32)],
+        scratch=scratch,
+        n_in=3,
+        limit=24,
+        us=2.8,
+    )(q_all, stacked[0], others[0])
     partial = call(
-        attention_kernel,
+        attention_second_kernel,
         shape((32, SLOT_PAD, BLOCK), bf16),
-        scratch=[pltpu.VMEM((8 * tokens, BLOCK), bf16), pltpu.VMEM((HEADS_HERE, HEAD_DIM, 8 * tokens), bf16)],
+        scratch=scratch,
         n_in=5,
         limit=24,
-        us=6.5,
-    )(q_all, stacked[0], *others)
+        us=3.0,
+    )(q_all, others[1], others[2], mixed, stats)
     parts = lax.all_to_all(partial, SEQ, 0, 0, tiled=True)
     rows, mod = load(partial, [rows_in, modulation], 16)
     hidden, normed, mark = call(
@@ -308,7 +353,8 @@
         us=1.6,
     )(parts, rows, mod)
 
-    visits = [lax.ppermute(normed, "y", turn(k)) for k in (1, 2, 3)]
+    far, near, last = (lax.ppermute(normed, "y", turn(k)) for k in (2, 1, 3))
+    visits = [near, far, last]
     up, down = load(mark, [w_up, w_down], 34)
     terms = call(
         feed_kernel,
@@ -321,7 +367,7 @@
         n_in=7,
         us=3.7,
     )(normed, *visits, up, b_up[None], down)
-    back = [lax.ppermute(terms[k], "y", turn(-k)) for k in (1, 2, 3)]
+    back = [lax.ppermute(terms[k], "y", turn(-k)) for k in (2, 1, 3)]
     return call(finish_kernel, shape((1, slots, width), bf16), n_in=8, smem=(0,), us=1.4)(
         counts, terms[0], *back, hidden, modulation, b_down[None]
     )

time: 90.9 us -> 93.2 us (1.025)
  starting transfers between devices: 29.6 us -> 32.3 us
  Pallas kernels: 21.6 us -> 22.7 us
    all_to_all x1, waiting for transfers between devices: 6.59 us -> 0.01 us  [body(): lax.all_to_all(q_blocks.reshape(16, 2 * SLOT_PAD, BLOCK), ('z', 'x'), 0,...]
    ppermute x3, waiting for transfers between devices: 6.67 us -> 12.2 us  [body(): others = [lax.ppermute(stacked[k], SEQ, ring_pairs(k)) for k in (1, 2, 3)]]
    ppermute x1, waiting for transfers between devices: 0.01 us -> 2.62 us  [body(): first = lax.ppermute(send, SEQ, swap)]
    all_to_all x1, starting transfers between devices: 5.3 us -> 7.61 us  [body(): parts = lax.all_to_all(partial, SEQ, 0, 0, tiled=True)]
    ppermute x6, waiting for transfers between devices: 9.03 us -> 6.8 us  [the longest x3 6.68 us: body(): back = [lax.ppermute(terms[k], 'y', turn(-k)) for k in (2, 1, 3)]]
    pallas_call x3 -> x4, Pallas kernels: 10.1 us -> 11.2 us  [the longest x1 3.64 us: body(): call(attention_second_kernel, shape((32, SLOT_PAD, BLOCK), bf16), scratch...]
  transfers between devices with their start and end apart: 12 -> 12, of which waited for: 8 -> 8; matrix products, arithmetic and copies ran while one was open for 0% -> 0% of each run, Pallas kernels for 8% -> 10%
where the time goes in v5:
time: 93.2 us; the launch traced here: 92.8 us
  waiting for transfers between devices  35.8 us (38%)
  starting transfers between devices  32.3 us (35%)
  Pallas kernels  22.7 us (24%)
  local copies, waits for them, and re-layouts  1.2 us (1%)
    all_to_all x1, waiting for transfers between devices, body(): parts = lax.all_to_all(partial, SEQ, 0, 0, tiled=True)  14.2 us
    ppermute x3, waiting for transfers between devices, body(): others = [lax.ppermute(stacked[k], SEQ, ring_pairs(k)) for k in (1, 2, 3)]  12.2 us
    all_to_all x1, starting transfers between devices, body(): lax.all_to_all(q_blocks.reshape(16, 2 * SLOT_PAD, BLOCK), ('z', 'x'), 0,...  7.95 us
    all_to_all x1, starting transfers between devices, body(): parts = lax.all_to_all(partial, SEQ, 0, 0, tiled=True)  7.61 us
    pallas_call x2, Pallas kernels, load(): call(load_kernel, [jax.ShapeDtypeStruct(v.shape, bf16) for v in arrays],...  6.69 us
    ppermute x3, waiting for transfers between devices, body(): back = [lax.ppermute(terms[k], 'y', turn(-k)) for k in (2, 1, 3)]  6.68 us
    ppermute x3, starting transfers between devices, body(): others = [lax.ppermute(stacked[k], SEQ, ring_pairs(k)) for k in (1, 2, 3)]  6.06 us
    ppermute x3, starting transfers between devices, body(): far, near, last = (lax.ppermute(normed, 'y', turn(k)) for k in (2, 1, 3))  5.9 us
  transfers between devices with their start and end apart: 12, of which 8 were waited for; matrix products, arithmetic and copies ran while one was open for 0% of the time, Pallas kernels for 10%

profile of v5, /device:TPU:0, one launch (start us, length us, event | category | flops | bytes accessed | tf_op | source)
XLA Modules:
  0.0 92.8 jit_solution(15034673821074133483)
XLA Ops:
  0.7 3.6 %shard_map.100 = (bf16[4,288,384]{2,1,0:T(8,128)(2,1)}, bf16[4,288,384]{2,1,0:T(8,128)(2,1)}) custom-call(s32[1,1]{1,0:T(1,128)S(6)} %copy.11.count_ref, bf16[128,2,3072]{2,1,0:T(2,128)(2,1)} %bitcast.8, bf16[3,28,3072]{2,1,0:T(8,128)(2,1)} %bitcast.9, s32[1,28]{1,0:T(1,128)} %chosen_hbm.1), custom_call_target="tpu_custom_call" | custom-call | tf_op jit(solution)/shard_map/pallas_call | solution.py:301
  4.3 0.1 collective-permute-start
  4.4 2.6 %collective-permute-done.first_ref = bf16[4,288,384]{2,1,0:T(8,128)(2,1)S(1)} collective-permute-done((bf16[4,288,384]{2,1,0:T(8,128)(2,1)}, bf16[4,288,384]{2,1,0:T(8,128)(2,1)S(1)}, u32[]{:S(2)}, u32[]{:S(2)}) %collective-permute-start) | collective-permute-done | bytes 884768 | tf_op jit(solution)/shard_map/ppermute | solution.py:318
  7.0 1.2 %copy-done = bf16[4,288,384]{2,1,0:T(8,128)(2,1)S(1)} copy-done((bf16[4,288,384]{2,1,0:T(8,128)(2,1)S(1)}, bf16[4,288,384]{2,1,0:T(8,128)(2,1)}, u32[]{:S(2)}) %copy-start) | copy-done | bytes 884760
  8.2 1.2 %shard_map.101 = (bf16[2,256,384]{2,1,0:T(8,128)(2,1)S(1)}, bf16[2,256,384]{2,1,0:T(8,128)(2,1)}, bf16[2,256,384]{2,1,0:T(8,128)(2,1)S(1)}, bf16[2,256,384]{2,1,0:T(8,128)(2,1)S(1)}, bf16[16,2,32,384]{3,2,1,0:T(8,128)(2,1)}) custom-call(bf16[4,288,384]{2,1,0:T(8,128)(2,1)S(1)} %copy-done, bf16[4,288,384]{2,1,0:T(8,128)(2,1)S(1)} %collective-permute-done.first_ref), custom_call_target="tpu_custom_call" | custom-call | bytes 3300000 | tf_op jit(solution)/shard_map/pallas_call | solution.py:319
  9.4 8.0 %all-to-all-start = ((bf16[16,64,384]{2,1,0:T(8,128)(2,1)}), bf16[16,64,384]{2,1,0:T(8,128)(2,1)S(1)}, u32[]{:S(2)}, u32[]{:S(2)}) async-start(bf16[16,64,384]{2,1,0:T(8,128)(2,1)} %bitcast.3), calls=%async_computation | async-start | bytes 1572864 | tf_op jit(solution)/shard_map/all_to_all | solution.py:325
  17.4 1.9 %collective-permute-start.3 = (bf16[2,256,384]{2,1,0:T(8,128)(2,1)}, bf16[2,256,384]{2,1,0:T(8,128)(2,1)S(1)}, u32[]{:S(2)}, u32[]{:S(2)}) collective-permute-start(bf16[2,256,384]{2,1,0:T(8,128)(2,1)} %get-tuple-element.31), channel_id=1, source_target_pairs={{0,2},{1,9},{2,4},{3,11},{4,6},{5,13},{6,0},{7,15},{8,10},{9,17},{... | collective-permute-start | bytes 1179656 | tf_op jit(solution)/shard_map/ppermute | solution.py:324
  19.3 2.7 %collective-permute-start.1 = (bf16[2,256,384]{2,1,0:T(8,128)(2,1)S(1)}, bf16[2,256,384]{2,1,0:T(8,128)(2,1)S(1)}, u32[]{:S(2)}, u32[]{:S(2)}) collective-permute-start(bf16[2,256,384]{2,1,0:T(8,128)(2,1)S(1)} %get-tuple-element.28), channel_id=1, source_target_pairs={{0,4},{1,17},{2,6},{3,19},{4,0},{5,21},{6,2},{7,23},{8,12},{9,25},... | collective-permute-start | bytes 1179656 | tf_op jit(solution)/shard_map/ppermute | solution.py:324
  22.0 1.5 %collective-permute-start.2 = (bf16[2,256,384]{2,1,0:T(8,128)(2,1)S(1)}, bf16[2,256,384]{2,1,0:T(8,128)(2,1)S(1)}, u32[]{:S(2)}, u32[]{:S(2)}) collective-permute-start(bf16[2,256,384]{2,1,0:T(8,128)(2,1)S(1)} %get-tuple-element.29), channel_id=1, source_target_pairs={{0,6},{1,25},{2,0},{3,27},{4,2},{5,29},{6,4},{7,31},{8,14},{9,1},{... | collective-permute-start | bytes 1179656 | tf_op jit(solution)/shard_map/ppermute | solution.py:324
  23.4 10.3 %collective-permute-done.3.r1_ref = bf16[2,256,384]{2,1,0:T(8,128)(2,1)S(1)} collective-permute-done((bf16[2,256,384]{2,1,0:T(8,128)(2,1)}, bf16[2,256,384]{2,1,0:T(8,128)(2,1)S(1)}, u32[]{:S(2)}, u32[]{:S(2)}) %collective-permute-start.3) | collective-permute-done | bytes 393248 | tf_op jit(solution)/shard_map/ppermute | solution.py:324
  33.8 2.7 %shard_map.102 = (f32[3,128,1024]{2,1,0:T(8,128)S(1)}, f32[8,1024]{1,0:T(8,128)S(1)}) custom-call(bf16[32,32,384]{2,1,0:T(8,128)(2,1)S(1)} %bitcast.6, bf16[2,256,384]{2,1,0:T(8,128)(2,1)S(1)} %get-tuple-element.30.r0_ref, bf16[2,256,384]{2,1,0:T(8,128)(2,1)S(1)} %collective-permute-done.3.r1_ref), custom_call_target="tpu_custom_call" | custom-call | bytes 9240000 | tf_op jit(solution)/shard_map/pallas_call | solution.py:330
  36.5 1.8 %collective-permute-done.1.r2_ref = bf16[2,256,384]{2,1,0:T(8,128)(2,1)S(1)} collective-permute-done((bf16[2,256,384]{2,1,0:T(8,128)(2,1)S(1)}, bf16[2,256,384]{2,1,0:T(8,128)(2,1)S(1)}, u32[]{:S(2)}, u32[]{:S(2)}) %collective-permute-start.1) | collective-permute-done | bytes 393248 | tf_op jit(solution)/shard_map/ppermute | solution.py:324
  38.3 0.0 collective-permute-done.2.r3_ref
  38.3 3.6 %shard_map.103.after_ref = bf16[32,32,384]{2,1,0:T(8,128)(2,1)} custom-call(bf16[32,32,384]{2,1,0:T(8,128)(2,1)S(1)} %bitcast.7, bf16[2,256,384]{2,1,0:T(8,128)(2,1)S(1)} %collective-permute-done.1.r2_ref, bf16[2,256,384]{2,1,0:T(8,128)(2,1)S(1)} %collective-permute-done.2.r3_ref, f32[3,128,1024]{2,1,0:T(8,128)S(1)} %get-tuple-element.32.mixed_ref, ...), custom_call_target="tpu_custom_call" | custom-call | bytes 9900000 | tf_op jit(solution)/shard_map/pallas_call | solution.py:338
  42.0 7.6 %all-to-all-start.1 = ((bf16[32,32,384]{2,1,0:T(8,128)(2,1)}), bf16[32,32,384]{2,1,0:T(8,128)(2,1)S(1)}, u32[]{:S(2)}, u32[]{:S(2)}) async-start(bf16[32,32,384]{2,1,0:T(8,128)(2,1)} %shard_map.103.after_ref), calls=%async_computation.1 | async-start | bytes 1572864 | tf_op jit(solution)/shard_map/all_to_all | solution.py:346
  49.6 0.3 shard_map.104
  49.9 14.2 %all-to-all-done.1.parts_ref = bf16[32,32,384]{2,1,0:T(8,128)(2,1)S(1)} async-done(((bf16[32,32,384]{2,1,0:T(8,128)(2,1)}), bf16[32,32,384]{2,1,0:T(8,128)(2,1)S(1)}, u32[]{:S(2)}, u32[]{:S(2)}) %all-to-all-start.1) | async-done | bytes 786464 | tf_op jit(solution)/shard_map/all_to_all | solution.py:346
  64.1 1.1 %shard_map.105 = (f32[28,3072]{1,0:T(8,128)S(1)}, bf16[56,1536]{1,0:T(8,128)(2,1)S(1)}, bf16[16,128]{1,0:T(8,128)(2,1)S(1)}) custom-call(bf16[32,32,384]{2,1,0:T(8,128)(2,1)S(1)} %all-to-all-done.1.parts_ref, bf16[1,28,3072]{2,1,0:T(8,128)(2,1)S(1)} %get-tuple-element.34.rows_ref, bf16[1,4,3072]{2,1,0:T(4,128)(2,1)S(1)} %get-tuple-element.35.mod_ref), custom_call_target="tpu_custom_call" | custom-call | bytes 5280000 | tf_op jit(solution)/shard_map/pallas_call | solution.py:348
  65.3 1.6 %collective-permute-start.4 = (bf16[56,1536]{1,0:T(8,128)(2,1)S(1)}, bf16[56,1536]{1,0:T(8,128)(2,1)S(1)}, u32[]{:S(2)}, u32[]{:S(2)}) collective-permute-start(bf16[56,1536]{1,0:T(8,128)(2,1)S(1)} %get-tuple-element.36.r0_ref), channel_id=1, source_target_pairs={{0,32},{32,64},{64,96},{96,0},{1,33},{33,65},{65,97},{97,1},{2,34}... | collective-permute-start | bytes 516104 | tf_op jit(solution)/shard_map/ppermute | solution.py:356
  66.9 2.9 %collective-permute-start.5 = (bf16[56,1536]{1,0:T(8,128)(2,1)S(1)}, bf16[56,1536]{1,0:T(8,128)(2,1)S(1)}, u32[]{:S(2)}, u32[]{:S(2)}) collective-permute-start(bf16[56,1536]{1,0:T(8,128)(2,1)S(1)} %get-tuple-element.36.r0_ref), channel_id=1, source_target_pairs={{0,64},{32,96},{64,0},{96,32},{1,65},{33,97},{65,1},{97,33},{2,66}... | collective-permute-start | bytes 516104 | tf_op jit(solution)/shard_map/ppermute | solution.py:356
  69.8 1.3 %collective-permute-start.6 = (bf16[56,1536]{1,0:T(8,128)(2,1)S(1)}, bf16[56,1536]{1,0:T(8,128)(2,1)S(1)}, u32[]{:S(2)}, u32[]{:S(2)}) collective-permute-start(bf16[56,1536]{1,0:T(8,128)(2,1)S(1)} %get-tuple-element.36.r0_ref), channel_id=1, source_target_pairs={{0,96},{32,0},{64,32},{96,64},{1,97},{33,1},{65,33},{97,65},{2,98}... | collective-permute-start | bytes 516104 | tf_op jit(solution)/shard_map/ppermute | solution.py:356
  71.2 6.4 %shard_map.106 = (bf16[3072,1536]{1,0:T(8,128)(2,1)S(1)}, bf16[1536,3072]{1,0:T(8,128)(2,1)S(1)}) custom-call(bf16[16,128]{1,0:T(8,128)(2,1)S(1)} %get-tuple-element.37.after_ref, bf16[3072,1536]{1,0:T(8,128)(2,1)} %refs_0_.3, bf16[1536,3072]{1,0:T(8,128)(2,1)} %refs_1_.3), custom_call_target="tpu_custom_call" | custom-call | bytes 11880000 | tf_op jit(solution)/shard_map/pallas_call | solution.py:235
  77.6 0.0 collective-permute-done.4.r1_ref
  77.6 0.1 collective-permute-done.5.r2_ref
  77.7 2.9 %shard_map.107 = (bf16[56,1536]{1,0:T(8,128)(2,1)S(1)}, bf16[56,1536]{1,0:T(8,128)(2,1)S(1)}, bf16[56,1536]{1,0:T(8,128)(2,1)S(1)}, bf16[56,1536]{1,0:T(8,128)(2,1)S(1)}) custom-call(bf16[56,1536]{1,0:T(8,128)(2,1)S(1)} %get-tuple-element.36.r0_ref, bf16[56,1536]{1,0:T(8,128)(2,1)S(1)} %collective-permute-done.4.r1_ref, ...), custom_call_target="tpu_custom_call" | custom-call | bytes 12210000 | tf_op jit(solution)/shard_map/pallas_call | solution.py:359
  80.6 2.7 %collective-permute-start.7 = (bf16[56,1536]{1,0:T(8,128)(2,1)S(1)}, bf16[56,1536]{1,0:T(8,128)(2,1)S(1)}, u32[]{:S(2)}, u32[]{:S(2)}) collective-permute-start(bf16[56,1536]{1,0:T(8,128)(2,1)S(1)} %get-tuple-element.41), channel_id=1, source_target_pairs={{0,64},{32,96},{64,0},{96,32},{1,65},{33,97},{65,1},{97,33},{2,66}... | collective-permute-start | bytes 516104 | tf_op jit(solution)/shard_map/ppermute | solution.py:370
  83.3 1.3 %collective-permute-start.8 = (bf16[56,1536]{1,0:T(8,128)(2,1)S(1)}, bf16[56,1536]{1,0:T(8,128)(2,1)S(1)}, u32[]{:S(2)}, u32[]{:S(2)}) collective-permute-start(bf16[56,1536]{1,0:T(8,128)(2,1)S(1)} %get-tuple-element.42), channel_id=1, source_target_pairs={{0,96},{32,0},{64,32},{96,64},{1,97},{33,1},{65,33},{97,65},{2,98}... | collective-permute-start | bytes 516104 | tf_op jit(solution)/shard_map/ppermute | solution.py:370
  84.6 0.7 collective-permute-start.9
  85.3 4.2 %collective-permute-done.7.t1_ref = bf16[56,1536]{1,0:T(8,128)(2,1)S(1)} collective-permute-done((bf16[56,1536]{1,0:T(8,128)(2,1)S(1)}, bf16[56,1536]{1,0:T(8,128)(2,1)S(1)}, u32[]{:S(2)}, u32[]{:S(2)}) %collective-permute-start.7) | collective-permute-done | bytes 172064 | tf_op jit(solution)/shard_map/ppermute | solution.py:370
  89.5 1.7 %collective-permute-done.8.t2_ref = bf16[56,1536]{1,0:T(8,128)(2,1)S(1)} collective-permute-done((bf16[56,1536]{1,0:T(8,128)(2,1)S(1)}, bf16[56,1536]{1,0:T(8,128)(2,1)S(1)}, u32[]{:S(2)}, u32[]{:S(2)}) %collective-permute-start.8) | collective-permute-done | bytes 172064 | tf_op jit(solution)/shard_map/ppermute | solution.py:370
  91.2 0.8 collective-permute-done.9.t3_ref
  92.0 0.9 shard_map.108
  (13 shorter events, 0.0 us)
Async XLA Ops:
  0.0 49.6 %copy-start.1 = (bf16[1,28,3072]{2,1,0:T(8,128)(2,1)S(1)}, bf16[1,28,3072]{2,1,0:T(8,128)(2,1)}, u32[]{:S(2)}) copy-start(bf16[1,28,3072]{2,1,0:T(8,128)(2,1)} %refs_0_.2) | copy-start | bytes 516100
  0.0 49.6 %copy-start.2 = (bf16[1,4,3072]{2,1,0:T(4,128)(2,1)S(1)}, bf16[1,4,3072]{2,1,0:T(4,128)(2,1)}, u32[]{:S(2)}) copy-start(bf16[1,4,3072]{2,1,0:T(4,128)(2,1)} %mod_ref.1) | copy-start | bytes 73732
  0.0 71.2 %copy-start.4 = (bf16[1536]{0:T(1024)(128)(2,1)S(1)}, bf16[1536]{0:T(1024)(128)(2,1)}, u32[]{:S(2)}) copy-start(bf16[1536]{0:T(1024)(128)(2,1)} %param.17) | copy-start | bytes 9220
  4.3 2.7 %collective-permute-start = (bf16[4,288,384]{2,1,0:T(8,128)(2,1)}, bf16[4,288,384]{2,1,0:T(8,128)(2,1)S(1)}, u32[]{:S(2)}, u32[]{:S(2)}) collective-permute-start(bf16[4,288,384]{2,1,0:T(8,128)(2,1)} %get-tuple-element.26), channel_id=1, source_target_pairs={{0,1},{1,0},{2,3},{3,2},{4,5},{5,4},{6,7},{7,6},{8,9},{9,8},{10,11... | collective-permute-start | bytes 2654216 | tf_op jit(solution)/shard_map/ppermute | solution.py:318
  7.0 1.2 %copy-start = (bf16[4,288,384]{2,1,0:T(8,128)(2,1)S(1)}, bf16[4,288,384]{2,1,0:T(8,128)(2,1)}, u32[]{:S(2)}) copy-start(bf16[4,288,384]{2,1,0:T(8,128)(2,1)} %get-tuple-element.25.keep_ref) | copy-start | bytes 2654212
  9.4 24.4 %all-to-all-start = ((bf16[16,64,384]{2,1,0:T(8,128)(2,1)}), bf16[16,64,384]{2,1,0:T(8,128)(2,1)S(1)}, u32[]{:S(2)}, u32[]{:S(2)}) async-start(bf16[16,64,384]{2,1,0:T(8,128)(2,1)} %bitcast.3), calls=%async_computation | async-start | bytes 1572864 | tf_op jit(solution)/shard_map/all_to_all | solution.py:325
  17.4 16.4 %collective-permute-start.3 = (bf16[2,256,384]{2,1,0:T(8,128)(2,1)}, bf16[2,256,384]{2,1,0:T(8,128)(2,1)S(1)}, u32[]{:S(2)}, u32[]{:S(2)}) collective-permute-start(bf16[2,256,384]{2,1,0:T(8,128)(2,1)} %get-tuple-element.31), channel_id=1, source_target_pairs={{0,2},{1,9},{2,4},{3,11},{4,6},{5,13},{6,0},{7,15},{8,10},{9,17},{... | collective-permute-start | bytes 1179656 | tf_op jit(solution)/shard_map/ppermute | solution.py:324
  19.3 19.0 %collective-permute-start.1 = (bf16[2,256,384]{2,1,0:T(8,128)(2,1)S(1)}, bf16[2,256,384]{2,1,0:T(8,128)(2,1)S(1)}, u32[]{:S(2)}, u32[]{:S(2)}) collective-permute-start(bf16[2,256,384]{2,1,0:T(8,128)(2,1)S(1)} %get-tuple-element.28), channel_id=1, source_target_pairs={{0,4},{1,17},{2,6},{3,19},{4,0},{5,21},{6,2},{7,23},{8,12},{9,25},... | collective-permute-start | bytes 1179656 | tf_op jit(solution)/shard_map/ppermute | solution.py:324
  22.0 16.4 %collective-permute-start.2 = (bf16[2,256,384]{2,1,0:T(8,128)(2,1)S(1)}, bf16[2,256,384]{2,1,0:T(8,128)(2,1)S(1)}, u32[]{:S(2)}, u32[]{:S(2)}) collective-permute-start(bf16[2,256,384]{2,1,0:T(8,128)(2,1)S(1)} %get-tuple-element.29), channel_id=1, source_target_pairs={{0,6},{1,25},{2,0},{3,27},{4,2},{5,29},{6,4},{7,31},{8,14},{9,1},{... | collective-permute-start | bytes 1179656 | tf_op jit(solution)/shard_map/ppermute | solution.py:324
  42.0 22.2 %all-to-all-start.1 = ((bf16[32,32,384]{2,1,0:T(8,128)(2,1)}), bf16[32,32,384]{2,1,0:T(8,128)(2,1)S(1)}, u32[]{:S(2)}, u32[]{:S(2)}) async-start(bf16[32,32,384]{2,1,0:T(8,128)(2,1)} %shard_map.103.after_ref), calls=%async_computation.1 | async-start | bytes 1572864 | tf_op jit(solution)/shard_map/all_to_all | solution.py:346
  65.3 12.3 %collective-permute-start.4 = (bf16[56,1536]{1,0:T(8,128)(2,1)S(1)}, bf16[56,1536]{1,0:T(8,128)(2,1)S(1)}, u32[]{:S(2)}, u32[]{:S(2)}) collective-permute-start(bf16[56,1536]{1,0:T(8,128)(2,1)S(1)} %get-tuple-element.36.r0_ref), channel_id=1, source_target_pairs={{0,32},{32,64},{64,96},{96,0},{1,33},{33,65},{65,97},{97,1},{2,34}... | collective-permute-start | bytes 516104 | tf_op jit(solution)/shard_map/ppermute | solution.py:356
  66.9 10.8 %collective-permute-start.5 = (bf16[56,1536]{1,0:T(8,128)(2,1)S(1)}, bf16[56,1536]{1,0:T(8,128)(2,1)S(1)}, u32[]{:S(2)}, u32[]{:S(2)}) collective-permute-start(bf16[56,1536]{1,0:T(8,128)(2,1)S(1)} %get-tuple-element.36.r0_ref), channel_id=1, source_target_pairs={{0,64},{32,96},{64,0},{96,32},{1,65},{33,97},{65,1},{97,33},{2,66}... | collective-permute-start | bytes 516104 | tf_op jit(solution)/shard_map/ppermute | solution.py:356
  69.8 7.9 %collective-permute-start.6 = (bf16[56,1536]{1,0:T(8,128)(2,1)S(1)}, bf16[56,1536]{1,0:T(8,128)(2,1)S(1)}, u32[]{:S(2)}, u32[]{:S(2)}) collective-permute-start(bf16[56,1536]{1,0:T(8,128)(2,1)S(1)} %get-tuple-element.36.r0_ref), channel_id=1, source_target_pairs={{0,96},{32,0},{64,32},{96,64},{1,97},{33,1},{65,33},{97,65},{2,98}... | collective-permute-start | bytes 516104 | tf_op jit(solution)/shard_map/ppermute | solution.py:356
  77.7 7.6 %copy-start.3 = (bf16[3072]{0:T(1024)(128)(2,1)S(1)}, bf16[3072]{0:T(1024)(128)(2,1)}, u32[]{:S(2)}) copy-start(bf16[3072]{0:T(1024)(128)(2,1)} %param.19) | copy-start | bytes 18436
  80.6 8.9 %collective-permute-start.7 = (bf16[56,1536]{1,0:T(8,128)(2,1)S(1)}, bf16[56,1536]{1,0:T(8,128)(2,1)S(1)}, u32[]{:S(2)}, u32[]{:S(2)}) collective-permute-start(bf16[56,1536]{1,0:T(8,128)(2,1)S(1)} %get-tuple-element.41), channel_id=1, source_target_pairs={{0,64},{32,96},{64,0},{96,32},{1,65},{33,97},{65,1},{97,33},{2,66}... | collective-permute-start | bytes 516104 | tf_op jit(solution)/shard_map/ppermute | solution.py:370
  83.3 8.0 %collective-permute-start.8 = (bf16[56,1536]{1,0:T(8,128)(2,1)S(1)}, bf16[56,1536]{1,0:T(8,128)(2,1)S(1)}, u32[]{:S(2)}, u32[]{:S(2)}) collective-permute-start(bf16[56,1536]{1,0:T(8,128)(2,1)S(1)} %get-tuple-element.42), channel_id=1, source_target_pairs={{0,96},{32,0},{64,32},{96,64},{1,97},{33,1},{65,33},{97,65},{2,98}... | collective-permute-start | bytes 516104 | tf_op jit(solution)/shard_map/ppermute | solution.py:370
  84.6 7.4 %collective-permute-start.9 = (bf16[56,1536]{1,0:T(8,128)(2,1)S(1)}, bf16[56,1536]{1,0:T(8,128)(2,1)S(1)}, u32[]{:S(2)}, u32[]{:S(2)}) collective-permute-start(bf16[56,1536]{1,0:T(8,128)(2,1)S(1)} %get-tuple-element.43), channel_id=1, source_target_pairs={{0,32},{32,64},{64,96},{96,0},{1,33},{33,65},{65,97},{97,1},{2,34}... | collective-permute-start | bytes 516104 | tf_op jit(solution)/shard_map/ppermute | solution.py:370

commit v6 on v5

--- a/solution.py
+++ b/solution.py
@@ -41,8 +41,8 @@
 
 
 def pack_kernel(
-    count_ref, kv_hbm, fresh_hbm, chosen_hbm, keep_hbm, send_hbm,
-    kv_ref, fresh_ref, chosen_ref, patched, queries, in_sems, out_sems,
+    count_ref, kv_hbm, fresh_hbm, chosen_hbm, q_hbm, keep_hbm, send_hbm,
+    kv_ref, fresh_ref, chosen_ref, patched, q_out, in_sems, out_sems,
 ):
     sources = [
         (fresh_hbm.at[0], fresh_ref.at[0]),
@@ -55,28 +55,17 @@
         copy.start()
     tokens = kv_ref.shape[0]
     slots = fresh_ref.shape[1]
+    copies[0].wait()
+    for dest in range(32):
+        z, x, core = dest // 8, dest // 2 % 4, dest % 2
+        group = x if core == 0 else 4 + z
+        q_out[dest, :slots, :] = fresh_ref[0, :, group * BLOCK : (group + 1) * BLOCK]
+        q_out[dest, slots:, :] = jnp.zeros((SLOT_PAD - slots, BLOCK), bf16)
+    outs = [pltpu.make_async_copy(q_out, q_hbm, out_sems.at[0])]
+    outs[0].start()
+
     core, ring_x, ring_z = (lax.axis_index(a) for a in ("core", "x", "z"))
     count = count_ref[0, 0]
-    half = 4 * BLOCK
-    outs = []
-
-    def send_out(source, first_row, rows, k, mine, other):
-        at_mine = pl.multiple_of(core * half + mine * BLOCK, BLOCK)
-        at_other = pl.multiple_of((1 - core) * half + other * BLOCK, BLOCK)
-        for at, target in ((at_other, send_hbm), (at_mine, keep_hbm)):
-            copy = pltpu.make_async_copy(
-                source.at[:, pl.ds(at, BLOCK)],
-                target.at[k, pl.ds(first_row, rows)],
-                out_sems.at[len(outs)],
-            )
-            copy.start()
-            outs.append(copy)
-
-    copies[0].wait()
-    queries[:slots, :] = fresh_ref[0]
-    queries[slots:, :] = jnp.zeros((SLOT_PAD - slots, queries.shape[1]), bf16)
-    for k in range(4):
-        send_out(queries, 2 * tokens, SLOT_PAD, k, k, k)
     for copy in copies[1:]:
         copy.wait()
     token_id = lax.broadcasted_iota(i32, (tokens, slots), 0)
@@ -86,28 +75,29 @@
     taken = jnp.sum(hot, axis=1, keepdims=True) > 0.5
     hot = hot.astype(bf16)
     old = jnp.swapaxes(kv_ref[...], 0, 1)
+    half = 4 * BLOCK
     for which in range(2):
         new = jnp.dot(hot, fresh_ref[1 + which], preferred_element_type=f32)
         patched[which] = jnp.where(taken, new, old[which].astype(f32)).astype(bf16)
         for k in range(4):
             mine = lax.rem(jnp.where(core == 0, ring_x, ring_z) + k, 4)
             other = lax.rem(jnp.where(core == 0, ring_z, ring_x) + k, 4)
-            send_out(patched.at[which], which * tokens, tokens, k, mine, other)
+            at_mine = pl.multiple_of(core * half + mine * BLOCK, BLOCK)
+            at_other = pl.multiple_of((1 - core) * half + other * BLOCK, BLOCK)
+            for at, target in ((at_other, send_hbm), (at_mine, keep_hbm)):
+                copy = pltpu.make_async_copy(
+                    patched.at[which, :, pl.ds(at, BLOCK)], target.at[k, which], out_sems.at[len(outs)]
+                )
+                copy.start()
+                outs.append(copy)
     for copy in outs:
         copy.wait()
 
 
-def stack_kernel(keep_ref, first_ref, *refs):
-    core = lax.axis_index("core")
-    rows = refs[0].shape[1]
-    for k, out_ref in enumerate(refs[:4]):
-        out_ref[0] = keep_ref[k, :rows]
-        out_ref[1] = first_ref[k, :rows]
-    q_ref = refs[4]
-    for chip in range(16):
-        group = jnp.where(core == 0, chip % 4, chip // 4)
-        q_ref[chip, core] = keep_ref[group, rows:]
-        q_ref[chip, 1 - core] = first_ref[group, rows:]
+def stack_kernel(keep_ref, first_ref, *out_refs):
+    for k, out_ref in enumerate(out_refs):
+        out_ref[0] = keep_ref[k]
+        out_ref[1] = first_ref[k]
 
 
 def gather_keys(sources, keys, values_t):
@@ -115,10 +105,10 @@
     at = 0
     for ref in sources:
         for core in range(2):
-            keys[at : at + rows, :] = ref[core, :rows, :]
+            keys[at : at + rows, :] = ref[core, 0]
             for h in range(HEADS_HERE):
                 cols = slice(h * HEAD_DIM, (h + 1) * HEAD_DIM)
-                values_t[h, :, at : at + rows] = ref[core, rows:, cols].T
+                values_t[h, :, at : at + rows] = ref[core, 1, :, cols].T
             at += rows
 
 
@@ -297,33 +287,27 @@
     slots, width = rows_in.shape[1], rows_in.shape[2]
     tokens = kv_cache.shape[1]
     fresh = jnp.swapaxes(fresh_qkv[0], 0, 1)
-    packed = shape((4, 2 * tokens + SLOT_PAD, BLOCK), bf16)
-    keep, send = pl.pallas_call(
+    q_blocks, keep, send = pl.pallas_call(
         pack_kernel,
-        out_shape=[packed] * 2,
+        out_shape=[shape((32, SLOT_PAD, BLOCK), bf16)] + [shape((4, 2, tokens, BLOCK), bf16)] * 2,
         in_specs=[pl.BlockSpec(memory_space=pltpu.SMEM)] + [pl.BlockSpec(memory_space=pltpu.HBM)] * 3,
-        out_specs=[pl.BlockSpec(memory_space=pltpu.HBM)] * 2,
+        out_specs=[pl.BlockSpec(memory_space=pltpu.HBM)] * 3,
         scratch_shapes=[
             pltpu.VMEM((tokens, 2, width), bf16),
             pltpu.VMEM((3, slots, width), bf16),
             pltpu.VMEM((1, slots), i32),
             pltpu.VMEM((2, tokens, width), bf16),
-            pltpu.VMEM((SLOT_PAD, width), bf16),
+            pltpu.VMEM((32, SLOT_PAD, BLOCK), bf16),
             pltpu.SemaphoreType.DMA((4,)),
-            pltpu.SemaphoreType.DMA((24,)),
+            pltpu.SemaphoreType.DMA((17,)),
         ],
         compiler_params=pltpu.CompilerParams(vmem_limit_bytes=61 * MB),
     )(counts, kv_cache[0], fresh, chosen)
+    q_all = lax.all_to_all(q_blocks, SEQ, 0, 0, tiled=True)
     swap = [(position(z, x, c), position(z, x, 1 - c)) for z in range(4) for x in range(4) for c in range(2)]
     first = lax.ppermute(send, SEQ, swap)
-    *stacked, q_blocks = call(
-        stack_kernel,
-        [shape((2, 2 * tokens, BLOCK), bf16)] * 4 + [shape((16, 2, SLOT_PAD, BLOCK), bf16)],
-        n_in=2,
-    )(keep, first)
+    stacked = call(stack_kernel, [shape((2, 2, tokens, BLOCK), bf16)] * 4, n_in=2)(keep, first)
     others = [lax.ppermute(stacked[k], SEQ, ring_pairs(k)) for k in (1, 2, 3)]
-    q_all = lax.all_to_all(q_blocks.reshape(16, 2 * SLOT_PAD, BLOCK), ("z", "x"), 0, 0, tiled=True)
-    q_all = q_all.reshape(32, SLOT_PAD, BLOCK)
 
     rows = 32 * SLOT_PAD
     scratch = [pltpu.VMEM((4 * tokens, BLOCK), bf16), pltpu.VMEM((HEADS_HERE, HEAD_DIM, 4 * tokens), bf16)]

time: 93.2 us -> 88.4 us (0.948)
  waiting for transfers between devices: 35.8 us -> 31.6 us
    ppermute x3, waiting for transfers between devices: 12.2 us -> 3.93 us  [body(): others = [lax.ppermute(stacked[k], SEQ, ring_pairs(k)) for k in (1, 2, 3)]]
    all_to_all x1, waiting for transfers between devices: 0.01 us -> 6.6 us  [body(): q_all = lax.all_to_all(q_blocks, SEQ, 0, 0, tiled=True)]
    ppermute x1, waiting for transfers between devices: 2.62 us -> 0.01 us  [body(): first = lax.ppermute(send, SEQ, swap)]
  transfers between devices with their start and end apart: 12 -> 12, of which waited for: 8 -> 8; matrix products, arithmetic and copies ran while one was open for 0% -> 0% of each run, Pallas kernels for 10% -> 12%
where the time goes in v6:
time: 88.4 us; the launch traced here: 88 us
  starting transfers between devices  32.1 us (36%)
  waiting for transfers between devices  31.6 us (36%)
  Pallas kernels  22.4 us (25%)
  local copies, waits for them, and re-layouts  1.16 us (1%)
    all_to_all x1, waiting for transfers between devices, body(): parts = lax.all_to_all(partial, SEQ, 0, 0, tiled=True)  14.2 us
    all_to_all x1, starting transfers between devices, body(): q_all = lax.all_to_all(q_blocks, SEQ, 0, 0, tiled=True)  8.34 us
    all_to_all x1, starting transfers between devices, body(): parts = lax.all_to_all(partial, SEQ, 0, 0, tiled=True)  7.12 us
    pallas_call x2, Pallas kernels, load(): call(load_kernel, [jax.ShapeDtypeStruct(v.shape, bf16) for v in arrays],...  6.69 us
    ppermute x3, waiting for transfers between devices, body(): back = [lax.ppermute(terms[k], 'y', turn(-k)) for k in (2, 1, 3)]  6.68 us
    all_to_all x1, waiting for transfers between devices, body(): q_all = lax.all_to_all(q_blocks, SEQ, 0, 0, tiled=True)  6.6 us
    ppermute x3, starting transfers between devices, body(): others = [lax.ppermute(stacked[k], SEQ, ring_pairs(k)) for k in (1, 2, 3)]  5.93 us
    ppermute x3, starting transfers between devices, body(): far, near, last = (lax.ppermute(normed, 'y', turn(k)) for k in (2, 1, 3))  5.9 us
  transfers between devices with their start and end apart: 12, of which 8 were waited for; matrix products, arithmetic and copies ran while one was open for 0% of the time, Pallas kernels for 12%

profile of v6, /device:TPU:0, one launch (start us, length us, event | category | flops | bytes accessed | tf_op | source)
XLA Modules:
  0.0 88.0 jit_solution(16476581367245043020)
XLA Ops:
  0.7 3.6 %shard_map.100 = (bf16[32,32,384]{2,1,0:T(8,128)(2,1)}, bf16[4,2,128,384]{3,2,1,0:T(8,128)(2,1)}, bf16[4,2,128,384]{3,2,1,0:T(8,128)(2,1)}) custom-call(s32[1,1]{1,0:T(1,128)S(6)} %copy.11.count_ref, bf16[128,2,3072]{2,1,0:T(2,128)(2,1)} %bitcast.4, bf16[3,28,3072]{2,1,0:T(8,128)(2,1)} %bitcast.5, s32[1,28]{1,0:T(1,128)} %chosen_hbm.1), custom_call_target="tpu_custom_call" | custom-call | tf_op jit(solution)/shard_map/pallas_call | solution.py:290
  4.3 0.1 collective-permute-start
  4.4 8.3 %all-to-all-start = ((bf16[32,32,384]{2,1,0:T(8,128)(2,1)}), bf16[32,32,384]{2,1,0:T(8,128)(2,1)S(1)}, u32[]{:S(2)}, u32[]{:S(2)}) async-start(bf16[32,32,384]{2,1,0:T(8,128)(2,1)} %get-tuple-element.25), calls=%async_computation | async-start | bytes 1572864 | tf_op jit(solution)/shard_map/all_to_all | solution.py:306
  12.7 0.0 collective-permute-done.first_ref
  12.7 1.1 %copy-done = bf16[4,2,128,384]{3,2,1,0:T(8,128)(2,1)S(1)} copy-done((bf16[4,2,128,384]{3,2,1,0:T(8,128)(2,1)S(1)}, bf16[4,2,128,384]{3,2,1,0:T(8,128)(2,1)}, u32[]{:S(2)}) %copy-start) | copy-done | bytes 786456
  13.9 0.9 %shard_map.101 = (bf16[2,2,128,384]{3,2,1,0:T(8,128)(2,1)S(1)}, bf16[2,2,128,384]{3,2,1,0:T(8,128)(2,1)}, bf16[2,2,128,384]{3,2,1,0:T(8,128)(2,1)S(1)}, bf16[2,2,128,384]{3,2,1,0:T(8,128)(2,1)S(1)}) custom-call(bf16[4,2,128,384]{3,2,1,0:T(8,128)(2,1)S(1)} %copy-done, bf16[4,2,128,384]{3,2,1,0:T(8,128)(2,1)S(1)} %collective-permute-done.first_ref), custom_call_target="tpu_custom_call" | custom-call | bytes 3300000 | tf_op jit(solution)/shard_map/pallas_call | solution.py:309
  14.8 1.8 %collective-permute-start.3 = (bf16[2,2,128,384]{3,2,1,0:T(8,128)(2,1)}, bf16[2,2,128,384]{3,2,1,0:T(8,128)(2,1)S(1)}, u32[]{:S(2)}, u32[]{:S(2)}) collective-permute-start(bf16[2,2,128,384]{3,2,1,0:T(8,128)(2,1)} %get-tuple-element.31), channel_id=1, source_target_pairs={{0,2},{1,9},{2,4},{3,11},{4,6},{5,13},{6,0},{7,15},{8,10},{9,17},{... | collective-permute-start | bytes 1179656 | tf_op jit(solution)/shard_map/ppermute | solution.py:310
  16.5 2.7 %collective-permute-start.1 = (bf16[2,2,128,384]{3,2,1,0:T(8,128)(2,1)S(1)}, bf16[2,2,128,384]{3,2,1,0:T(8,128)(2,1)S(1)}, u32[]{:S(2)}, u32[]{:S(2)}) collective-permute-start(bf16[2,2,128,384]{3,2,1,0:T(8,128)(2,1)S(1)} %get-tuple-element.28), channel_id=1, source_target_pairs={{0,4},{1,17},{2,6},{3,19},{4,0},{5,21},{6,2},{7,23},{8,12},{9,25},... | collective-permute-start | bytes 1179656 | tf_op jit(solution)/shard_map/ppermute | solution.py:310
  19.2 1.5 %collective-permute-start.2 = (bf16[2,2,128,384]{3,2,1,0:T(8,128)(2,1)S(1)}, bf16[2,2,128,384]{3,2,1,0:T(8,128)(2,1)S(1)}, u32[]{:S(2)}, u32[]{:S(2)}) collective-permute-start(bf16[2,2,128,384]{3,2,1,0:T(8,128)(2,1)S(1)} %get-tuple-element.29), channel_id=1, source_target_pairs={{0,6},{1,25},{2,0},{3,27},{4,2},{5,29},{6,4},{7,31},{8,14},{9,1},{... | collective-permute-start | bytes 1179656 | tf_op jit(solution)/shard_map/ppermute | solution.py:310
  20.7 6.6 %all-to-all-done.q_ref = bf16[32,32,384]{2,1,0:T(8,128)(2,1)S(1)} async-done(((bf16[32,32,384]{2,1,0:T(8,128)(2,1)}), bf16[32,32,384]{2,1,0:T(8,128)(2,1)S(1)}, u32[]{:S(2)}, u32[]{:S(2)}) %all-to-all-start) | async-done | bytes 786464 | tf_op jit(solution)/shard_map/all_to_all | solution.py:306
  27.3 2.2 %collective-permute-done.3.r1_ref = bf16[2,2,128,384]{3,2,1,0:T(8,128)(2,1)S(1)} collective-permute-done((bf16[2,2,128,384]{3,2,1,0:T(8,128)(2,1)}, bf16[2,2,128,384]{3,2,1,0:T(8,128)(2,1)S(1)}, u32[]{:S(2)}, u32[]{:S(2)}) %collective-permute-start.3) | collective-permute-done | bytes 393248 | tf_op jit(solution)/shard_map/ppermute | solution.py:310
  29.5 2.7 %shard_map.102 = (f32[3,128,1024]{2,1,0:T(8,128)S(1)}, f32[8,1024]{1,0:T(8,128)S(1)}) custom-call(bf16[32,32,384]{2,1,0:T(8,128)(2,1)S(1)} %all-to-all-done.q_ref, bf16[2,2,128,384]{3,2,1,0:T(8,128)(2,1)S(1)} %get-tuple-element.30.r0_ref, bf16[2,2,128,384]{3,2,1,0:T(8,128)(2,1)S(1)} %collective-permute-done.3.r1_ref), custom_call_target="tpu_custom_call" | custom-call | bytes 9240000 | tf_op jit(solution)/shard_map/pallas_call | solution.py:314
  32.2 1.8 %collective-permute-done.1.r2_ref = bf16[2,2,128,384]{3,2,1,0:T(8,128)(2,1)S(1)} collective-permute-done((bf16[2,2,128,384]{3,2,1,0:T(8,128)(2,1)S(1)}, bf16[2,2,128,384]{3,2,1,0:T(8,128)(2,1)S(1)}, u32[]{:S(2)}, u32[]{:S(2)}) %collective-permute-start.1) | collective-permute-done | bytes 393248 | tf_op jit(solution)/shard_map/ppermute | solution.py:310
  34.0 3.7 %shard_map.103.after_ref = bf16[32,32,384]{2,1,0:T(8,128)(2,1)} custom-call(bf16[32,32,384]{2,1,0:T(8,128)(2,1)S(1)} %all-to-all-done.q_ref, bf16[2,2,128,384]{3,2,1,0:T(8,128)(2,1)S(1)} %collective-permute-done.1.r2_ref, bf16[2,2,128,384]{3,2,1,0:T(8,128)(2,1)S(1)} %collective-permute-done.2.r3_ref, f32[3,128,1024]{2,1,0:T(8,128)S(1)} %get-tuple-element.32.mixed_ref, ...), custom_call_target="tpu_custom_call" | custom-call | bytes 9900000 | tf_op jit(solution)/shard_map/pallas_call | solution.py:322
  37.6 7.1 %all-to-all-start.1 = ((bf16[32,32,384]{2,1,0:T(8,128)(2,1)}), bf16[32,32,384]{2,1,0:T(8,128)(2,1)S(1)}, u32[]{:S(2)}, u32[]{:S(2)}) async-start(bf16[32,32,384]{2,1,0:T(8,128)(2,1)} %shard_map.103.after_ref), calls=%async_computation.1 | async-start | bytes 1572864 | tf_op jit(solution)/shard_map/all_to_all | solution.py:330
  44.8 0.3 shard_map.104
  45.1 14.2 %all-to-all-done.1.parts_ref = bf16[32,32,384]{2,1,0:T(8,128)(2,1)S(1)} async-done(((bf16[32,32,384]{2,1,0:T(8,128)(2,1)}), bf16[32,32,384]{2,1,0:T(8,128)(2,1)S(1)}, u32[]{:S(2)}, u32[]{:S(2)}) %all-to-all-start.1) | async-done | bytes 786464 | tf_op jit(solution)/shard_map/all_to_all | solution.py:330
  59.3 1.1 %shard_map.105 = (f32[28,3072]{1,0:T(8,128)S(1)}, bf16[56,1536]{1,0:T(8,128)(2,1)S(1)}, bf16[16,128]{1,0:T(8,128)(2,1)S(1)}) custom-call(bf16[32,32,384]{2,1,0:T(8,128)(2,1)S(1)} %all-to-all-done.1.parts_ref, bf16[1,28,3072]{2,1,0:T(8,128)(2,1)S(1)} %get-tuple-element.34.rows_ref, bf16[1,4,3072]{2,1,0:T(4,128)(2,1)S(1)} %get-tuple-element.35.mod_ref), custom_call_target="tpu_custom_call" | custom-call | bytes 5280000 | tf_op jit(solution)/shard_map/pallas_call | solution.py:332
  60.4 1.6 %collective-permute-start.4 = (bf16[56,1536]{1,0:T(8,128)(2,1)S(1)}, bf16[56,1536]{1,0:T(8,128)(2,1)S(1)}, u32[]{:S(2)}, u32[]{:S(2)}) collective-permute-start(bf16[56,1536]{1,0:T(8,128)(2,1)S(1)} %get-tuple-element.36.r0_ref), channel_id=1, source_target_pairs={{0,32},{32,64},{64,96},{96,0},{1,33},{33,65},{65,97},{97,1},{2,34}... | collective-permute-start | bytes 516104 | tf_op jit(solution)/shard_map/ppermute | solution.py:340
  62.1 2.9 %collective-permute-start.5 = (bf16[56,1536]{1,0:T(8,128)(2,1)S(1)}, bf16[56,1536]{1,0:T(8,128)(2,1)S(1)}, u32[]{:S(2)}, u32[]{:S(2)}) collective-permute-start(bf16[56,1536]{1,0:T(8,128)(2,1)S(1)} %get-tuple-element.36.r0_ref), channel_id=1, source_target_pairs={{0,64},{32,96},{64,0},{96,32},{1,65},{33,97},{65,1},{97,33},{2,66}... | collective-permute-start | bytes 516104 | tf_op jit(solution)/shard_map/ppermute | solution.py:340
  65.0 1.3 %collective-permute-start.6 = (bf16[56,1536]{1,0:T(8,128)(2,1)S(1)}, bf16[56,1536]{1,0:T(8,128)(2,1)S(1)}, u32[]{:S(2)}, u32[]{:S(2)}) collective-permute-start(bf16[56,1536]{1,0:T(8,128)(2,1)S(1)} %get-tuple-element.36.r0_ref), channel_id=1, source_target_pairs={{0,96},{32,0},{64,32},{96,64},{1,97},{33,1},{65,33},{97,65},{2,98}... | collective-permute-start | bytes 516104 | tf_op jit(solution)/shard_map/ppermute | solution.py:340
  66.4 6.4 %shard_map.106 = (bf16[3072,1536]{1,0:T(8,128)(2,1)S(1)}, bf16[1536,3072]{1,0:T(8,128)(2,1)S(1)}) custom-call(bf16[16,128]{1,0:T(8,128)(2,1)S(1)} %get-tuple-element.37.after_ref, bf16[3072,1536]{1,0:T(8,128)(2,1)} %refs_0_.3, bf16[1536,3072]{1,0:T(8,128)(2,1)} %refs_1_.3), custom_call_target="tpu_custom_call" | custom-call | bytes 11880000 | tf_op jit(solution)/shard_map/pallas_call | solution.py:225
  72.8 0.1 collective-permute-done.5.r2_ref
  72.9 0.0 collective-permute-done.6.r3_ref
  72.9 2.9 %shard_map.107 = (bf16[56,1536]{1,0:T(8,128)(2,1)S(1)}, bf16[56,1536]{1,0:T(8,128)(2,1)S(1)}, bf16[56,1536]{1,0:T(8,128)(2,1)S(1)}, bf16[56,1536]{1,0:T(8,128)(2,1)S(1)}) custom-call(bf16[56,1536]{1,0:T(8,128)(2,1)S(1)} %get-tuple-element.36.r0_ref, bf16[56,1536]{1,0:T(8,128)(2,1)S(1)} %collective-permute-done.4.r1_ref, ...), custom_call_target="tpu_custom_call" | custom-call | bytes 12210000 | tf_op jit(solution)/shard_map/pallas_call | solution.py:343
  75.8 2.7 %collective-permute-start.7 = (bf16[56,1536]{1,0:T(8,128)(2,1)S(1)}, bf16[56,1536]{1,0:T(8,128)(2,1)S(1)}, u32[]{:S(2)}, u32[]{:S(2)}) collective-permute-start(bf16[56,1536]{1,0:T(8,128)(2,1)S(1)} %get-tuple-element.41), channel_id=1, source_target_pairs={{0,64},{32,96},{64,0},{96,32},{1,65},{33,97},{65,1},{97,33},{2,66}... | collective-permute-start | bytes 516104 | tf_op jit(solution)/shard_map/ppermute | solution.py:354
  78.4 1.3 %collective-permute-start.8 = (bf16[56,1536]{1,0:T(8,128)(2,1)S(1)}, bf16[56,1536]{1,0:T(8,128)(2,1)S(1)}, u32[]{:S(2)}, u32[]{:S(2)}) collective-permute-start(bf16[56,1536]{1,0:T(8,128)(2,1)S(1)} %get-tuple-element.42), channel_id=1, source_target_pairs={{0,96},{32,0},{64,32},{96,64},{1,97},{33,1},{65,33},{97,65},{2,98}... | collective-permute-start | bytes 516104 | tf_op jit(solution)/shard_map/ppermute | solution.py:354
  79.7 0.7 collective-permute-start.9
  80.5 4.2 %collective-permute-done.7.t1_ref = bf16[56,1536]{1,0:T(8,128)(2,1)S(1)} collective-permute-done((bf16[56,1536]{1,0:T(8,128)(2,1)S(1)}, bf16[56,1536]{1,0:T(8,128)(2,1)S(1)}, u32[]{:S(2)}, u32[]{:S(2)}) %collective-permute-start.7) | collective-permute-done | bytes 172064 | tf_op jit(solution)/shard_map/ppermute | solution.py:354
  84.7 1.7 %collective-permute-done.8.t2_ref = bf16[56,1536]{1,0:T(8,128)(2,1)S(1)} collective-permute-done((bf16[56,1536]{1,0:T(8,128)(2,1)S(1)}, bf16[56,1536]{1,0:T(8,128)(2,1)S(1)}, u32[]{:S(2)}, u32[]{:S(2)}) %collective-permute-start.8) | collective-permute-done | bytes 172064 | tf_op jit(solution)/shard_map/ppermute | solution.py:354
  86.4 0.8 collective-permute-done.9.t3_ref
  87.1 0.9 shard_map.108
  (13 shorter events, 0.0 us)
Async XLA Ops:
  0.0 44.8 %copy-start.1 = (bf16[1,28,3072]{2,1,0:T(8,128)(2,1)S(1)}, bf16[1,28,3072]{2,1,0:T(8,128)(2,1)}, u32[]{:S(2)}) copy-start(bf16[1,28,3072]{2,1,0:T(8,128)(2,1)} %refs_0_.2) | copy-start | bytes 516100
  0.0 44.8 %copy-start.2 = (bf16[1,4,3072]{2,1,0:T(4,128)(2,1)S(1)}, bf16[1,4,3072]{2,1,0:T(4,128)(2,1)}, u32[]{:S(2)}) copy-start(bf16[1,4,3072]{2,1,0:T(4,128)(2,1)} %mod_ref.1) | copy-start | bytes 73732
  0.0 66.3 %copy-start.4 = (bf16[1536]{0:T(1024)(128)(2,1)S(1)}, bf16[1536]{0:T(1024)(128)(2,1)}, u32[]{:S(2)}) copy-start(bf16[1536]{0:T(1024)(128)(2,1)} %param.17) | copy-start | bytes 9220
  4.3 8.4 %collective-permute-start = (bf16[4,2,128,384]{3,2,1,0:T(8,128)(2,1)}, bf16[4,2,128,384]{3,2,1,0:T(8,128)(2,1)S(1)}, u32[]{:S(2)}, u32[]{:S(2)}) collective-permute-start(bf16[4,2,128,384]{3,2,1,0:T(8,128)(2,1)} %get-tuple-element.27), channel_id=1, source_target_pairs={{0,1},{1,0},{2,3},{3,2},{4,5},{5,4},{6,7},{7,6},{8,9},{9,8},{10,11... | collective-permute-start | bytes 2359304 | tf_op jit(solution)/shard_map/ppermute | solution.py:308
  4.4 22.9 %all-to-all-start = ((bf16[32,32,384]{2,1,0:T(8,128)(2,1)}), bf16[32,32,384]{2,1,0:T(8,128)(2,1)S(1)}, u32[]{:S(2)}, u32[]{:S(2)}) async-start(bf16[32,32,384]{2,1,0:T(8,128)(2,1)} %get-tuple-element.25), calls=%async_computation | async-start | bytes 1572864 | tf_op jit(solution)/shard_map/all_to_all | solution.py:306
  12.7 1.1 %copy-start = (bf16[4,2,128,384]{3,2,1,0:T(8,128)(2,1)S(1)}, bf16[4,2,128,384]{3,2,1,0:T(8,128)(2,1)}, u32[]{:S(2)}) copy-start(bf16[4,2,128,384]{3,2,1,0:T(8,128)(2,1)} %get-tuple-element.26.keep_ref) | copy-start | bytes 2359300
  14.8 14.7 %collective-permute-start.3 = (bf16[2,2,128,384]{3,2,1,0:T(8,128)(2,1)}, bf16[2,2,128,384]{3,2,1,0:T(8,128)(2,1)S(1)}, u32[]{:S(2)}, u32[]{:S(2)}) collective-permute-start(bf16[2,2,128,384]{3,2,1,0:T(8,128)(2,1)} %get-tuple-element.31), channel_id=1, source_target_pairs={{0,2},{1,9},{2,4},{3,11},{4,6},{5,13},{6,0},{7,15},{8,10},{9,17},{... | collective-permute-start | bytes 1179656 | tf_op jit(solution)/shard_map/ppermute | solution.py:310
  16.5 17.4 %collective-permute-start.1 = (bf16[2,2,128,384]{3,2,1,0:T(8,128)(2,1)S(1)}, bf16[2,2,128,384]{3,2,1,0:T(8,128)(2,1)S(1)}, u32[]{:S(2)}, u32[]{:S(2)}) collective-permute-start(bf16[2,2,128,384]{3,2,1,0:T(8,128)(2,1)S(1)} %get-tuple-element.28), channel_id=1, source_target_pairs={{0,4},{1,17},{2,6},{3,19},{4,0},{5,21},{6,2},{7,23},{8,12},{9,25},... | collective-permute-start | bytes 1179656 | tf_op jit(solution)/shard_map/ppermute | solution.py:310
  19.2 14.7 %collective-permute-start.2 = (bf16[2,2,128,384]{3,2,1,0:T(8,128)(2,1)S(1)}, bf16[2,2,128,384]{3,2,1,0:T(8,128)(2,1)S(1)}, u32[]{:S(2)}, u32[]{:S(2)}) collective-permute-start(bf16[2,2,128,384]{3,2,1,0:T(8,128)(2,1)S(1)} %get-tuple-element.29), channel_id=1, source_target_pairs={{0,6},{1,25},{2,0},{3,27},{4,2},{5,29},{6,4},{7,31},{8,14},{9,1},{... | collective-permute-start | bytes 1179656 | tf_op jit(solution)/shard_map/ppermute | solution.py:310
  37.6 21.7 %all-to-all-start.1 = ((bf16[32,32,384]{2,1,0:T(8,128)(2,1)}), bf16[32,32,384]{2,1,0:T(8,128)(2,1)S(1)}, u32[]{:S(2)}, u32[]{:S(2)}) async-start(bf16[32,32,384]{2,1,0:T(8,128)(2,1)} %shard_map.103.after_ref), calls=%async_computation.1 | async-start | bytes 1572864 | tf_op jit(solution)/shard_map/all_to_all | solution.py:330
  60.4 12.3 %collective-permute-start.4 = (bf16[56,1536]{1,0:T(8,128)(2,1)S(1)}, bf16[56,1536]{1,0:T(8,128)(2,1)S(1)}, u32[]{:S(2)}, u32[]{:S(2)}) collective-permute-start(bf16[56,1536]{1,0:T(8,128)(2,1)S(1)} %get-tuple-element.36.r0_ref), channel_id=1, source_target_pairs={{0,32},{32,64},{64,96},{96,0},{1,33},{33,65},{65,97},{97,1},{2,34}... | collective-permute-start | bytes 516104 | tf_op jit(solution)/shard_map/ppermute | solution.py:340
  62.1 10.8 %collective-permute-start.5 = (bf16[56,1536]{1,0:T(8,128)(2,1)S(1)}, bf16[56,1536]{1,0:T(8,128)(2,1)S(1)}, u32[]{:S(2)}, u32[]{:S(2)}) collective-permute-start(bf16[56,1536]{1,0:T(8,128)(2,1)S(1)} %get-tuple-element.36.r0_ref), channel_id=1, source_target_pairs={{0,64},{32,96},{64,0},{96,32},{1,65},{33,97},{65,1},{97,33},{2,66}... | collective-permute-start | bytes 516104 | tf_op jit(solution)/shard_map/ppermute | solution.py:340
  65.0 7.9 %collective-permute-start.6 = (bf16[56,1536]{1,0:T(8,128)(2,1)S(1)}, bf16[56,1536]{1,0:T(8,128)(2,1)S(1)}, u32[]{:S(2)}, u32[]{:S(2)}) collective-permute-start(bf16[56,1536]{1,0:T(8,128)(2,1)S(1)} %get-tuple-element.36.r0_ref), channel_id=1, source_target_pairs={{0,96},{32,0},{64,32},{96,64},{1,97},{33,1},{65,33},{97,65},{2,98}... | collective-permute-start | bytes 516104 | tf_op jit(solution)/shard_map/ppermute | solution.py:340
  72.9 7.6 %copy-start.3 = (bf16[3072]{0:T(1024)(128)(2,1)S(1)}, bf16[3072]{0:T(1024)(128)(2,1)}, u32[]{:S(2)}) copy-start(bf16[3072]{0:T(1024)(128)(2,1)} %param.19) | copy-start | bytes 18436
  75.8 8.9 %collective-permute-start.7 = (bf16[56,1536]{1,0:T(8,128)(2,1)S(1)}, bf16[56,1536]{1,0:T(8,128)(2,1)S(1)}, u32[]{:S(2)}, u32[]{:S(2)}) collective-permute-start(bf16[56,1536]{1,0:T(8,128)(2,1)S(1)} %get-tuple-element.41), channel_id=1, source_target_pairs={{0,64},{32,96},{64,0},{96,32},{1,65},{33,97},{65,1},{97,33},{2,66}... | collective-permute-start | bytes 516104 | tf_op jit(solution)/shard_map/ppermute | solution.py:354
  78.4 7.9 %collective-permute-start.8 = (bf16[56,1536]{1,0:T(8,128)(2,1)S(1)}, bf16[56,1536]{1,0:T(8,128)(2,1)S(1)}, u32[]{:S(2)}, u32[]{:S(2)}) collective-permute-start(bf16[56,1536]{1,0:T(8,128)(2,1)S(1)} %get-tuple-element.42), channel_id=1, source_target_pairs={{0,96},{32,0},{64,32},{96,64},{1,97},{33,1},{65,33},{97,65},{2,98}... | collective-permute-start | bytes 516104 | tf_op jit(solution)/shard_map/ppermute | solution.py:354
  79.7 7.4 %collective-permute-start.9 = (bf16[56,1536]{1,0:T(8,128)(2,1)S(1)}, bf16[56,1536]{1,0:T(8,128)(2,1)S(1)}, u32[]{:S(2)}, u32[]{:S(2)}) collective-permute-start(bf16[56,1536]{1,0:T(8,128)(2,1)S(1)} %get-tuple-element.43), channel_id=1, source_target_pairs={{0,32},{32,64},{64,96},{96,0},{1,33},{33,65},{65,97},{97,1},{2,34}... | collective-permute-start | bytes 516104 | tf_op jit(solution)/shard_map/ppermute | solution.py:354

commit v7 on v6

--- a/solution.py
+++ b/solution.py
@@ -122,8 +122,8 @@
 SCALE = LOG2E * HEAD_DIM**-0.5
 
 
-def attention_first_kernel(q_ref, r0_ref, r1_ref, mixed_ref, stats_ref, keys, values_t):
-    gather_keys((r0_ref, r1_ref), keys, values_t)
+def attention_first_kernel(q_ref, r0_ref, mixed_ref, stats_ref, keys, values_t):
+    gather_keys((r0_ref,), keys, values_t)
     q_all = q_ref[...].reshape(-1, BLOCK)
     for h in range(HEADS_HERE):
         scores = head_scores(q_all, keys, h)
@@ -134,8 +134,10 @@
         mixed_ref[h] = jnp.dot(values_t[h], weights.astype(bf16), preferred_element_type=f32)
 
 
-def attention_second_kernel(q_ref, r2_ref, r3_ref, mixed_ref, stats_ref, out_ref, keys, values_t):
-    gather_keys((r2_ref, r3_ref), keys, values_t)
+def attention_second_kernel(
+    q_ref, r1_ref, r2_ref, r3_ref, mixed_ref, stats_ref, after_ref, out_ref, keys, values_t
+):
+    gather_keys((r1_ref, r2_ref, r3_ref), keys, values_t)
     q_all = q_ref[...].reshape(-1, BLOCK)
     for h in range(HEADS_HERE):
         cols = slice(h * HEAD_DIM, (h + 1) * HEAD_DIM)
@@ -309,26 +311,28 @@
     stacked = call(stack_kernel, [shape((2, 2, tokens, BLOCK), bf16)] * 4, n_in=2)(keep, first)
     others = [lax.ppermute(stacked[k], SEQ, ring_pairs(k)) for k in (1, 2, 3)]
 
-    rows = 32 * SLOT_PAD
-    scratch = [pltpu.VMEM((4 * tokens, BLOCK), bf16), pltpu.VMEM((HEADS_HERE, HEAD_DIM, 4 * tokens), bf16)]
+
+    def key_scratch(count):
+        return [pltpu.VMEM((count, BLOCK), bf16), pltpu.VMEM((HEADS_HERE, HEAD_DIM, count), bf16)]
+
     mixed, stats = call(
         attention_first_kernel,
-        [shape((HEADS_HERE, HEAD_DIM, rows), f32), shape((8, rows), f32)],
-        scratch=scratch,
-        n_in=3,
+        [shape((HEADS_HERE, HEAD_DIM, 32 * SLOT_PAD), f32), shape((8, 32 * SLOT_PAD), f32)],
+        scratch=key_scratch(2 * tokens),
+        n_in=2,
         limit=24,
-        us=2.8,
-    )(q_all, stacked[0], others[0])
+        us=1.6,
+    )(q_all, stacked[0])
+    rows, mod = load(stats, [rows_in, modulation], 16)
     partial = call(
         attention_second_kernel,
         shape((32, SLOT_PAD, BLOCK), bf16),
-        scratch=scratch,
-        n_in=5,
+        scratch=key_scratch(6 * tokens),
+        n_in=7,
         limit=24,
-        us=3.0,
-    )(q_all, others[1], others[2], mixed, stats)
+        us=4.6,
+    )(q_all, *others, mixed, stats, mod)
     parts = lax.all_to_all(partial, SEQ, 0, 0, tiled=True)
-    rows, mod = load(partial, [rows_in, modulation], 16)
     hidden, normed, mark = call(
         combine_kernel,
         [shape((slots, width), f32), shape((2 * slots, width // 2), bf16), shape((16, 128), bf16)],

time: 88.4 us -> 86.5 us (0.979)
  blocking collectives: 0 us -> 19.7 us
  waiting for transfers between devices: 31.6 us -> 17.1 us
  starting transfers between devices: 32.1 us -> 25 us
  Pallas kernels: 22.4 us -> 20.6 us
  local copies, waits for them, and re-layouts: 1.16 us -> 2.81 us
    all_to_all x0 -> x1, blocking collectives: none -> 19.7 us  [body(): parts = lax.all_to_all(partial, SEQ, 0, 0, tiled=True)]
    all_to_all x1 -> x0, waiting for transfers between devices: 14.2 us -> none  [body(): parts = lax.all_to_all(partial, SEQ, 0, 0, tiled=True)]
    all_to_all x1 -> x0, starting transfers between devices: 7.12 us -> none  [body(): parts = lax.all_to_all(partial, SEQ, 0, 0, tiled=True)]
    unnamed x10 -> x12, local copies, waits for them, and re-layouts: 1.14 us -> 2.8 us
    pallas_call x1, Pallas kernels: 2.74 us -> 1.68 us  [body(): call(attention_first_kernel, [shape((HEADS_HERE, HEAD_DIM, 32 * SLOT_PAD)...]
    ppermute x3, waiting for transfers between devices: 3.93 us -> 3.03 us  [body(): others = [lax.ppermute(stacked[k], SEQ, ring_pairs(k)) for k in (1, 2, 3)]]
  transfers between devices with their start and end apart: 12 -> 11, of which waited for: 8 -> 6; matrix products, arithmetic and copies ran while one was open for 0% -> 0% of each run, Pallas kernels for 12% -> 10%
where the time goes in v7:
time: 86.5 us; the launch traced here: 86.1 us
  starting transfers between devices  25 us (29%)
  Pallas kernels  20.6 us (24%)
  blocking collectives  19.7 us (23%)
  waiting for transfers between devices  17.1 us (20%)
  local copies, waits for them, and re-layouts  2.81 us (3%)
    all_to_all x1, blocking collectives, body(): parts = lax.all_to_all(partial, SEQ, 0, 0, tiled=True)  19.7 us
    all_to_all x1, starting transfers between devices, body(): q_all = lax.all_to_all(q_blocks, SEQ, 0, 0, tiled=True)  8.35 us
    all_to_all x1, waiting for transfers between devices, body(): q_all = lax.all_to_all(q_blocks, SEQ, 0, 0, tiled=True)  7.29 us
    ppermute x3, waiting for transfers between devices, body(): back = [lax.ppermute(terms[k], 'y', turn(-k)) for k in (2, 1, 3)]  6.69 us
    pallas_call x2, Pallas kernels, load(): call(load_kernel, [jax.ShapeDtypeStruct(v.shape, bf16) for v in arrays],...  6.66 us
    ppermute x3, starting transfers between devices, body(): others = [lax.ppermute(stacked[k], SEQ, ring_pairs(k)) for k in (1, 2, 3)]  6 us
    ppermute x3, starting transfers between devices, body(): far, near, last = (lax.ppermute(normed, 'y', turn(k)) for k in (2, 1, 3))  5.9 us
    ppermute x3, starting transfers between devices, body(): back = [lax.ppermute(terms[k], 'y', turn(-k)) for k in (2, 1, 3)]  4.67 us
  transfers between devices with their start and end apart: 11, of which 6 were waited for; matrix products, arithmetic and copies ran while one was open for 0% of the time, Pallas kernels for 10%

profile of v7, /device:TPU:0, one launch (start us, length us, event | category | flops | bytes accessed | tf_op | source)
XLA Modules:
  0.0 86.1 jit_solution(6631758814560181431)
XLA Ops:
  0.7 3.6 %shard_map.100 = (bf16[32,32,384]{2,1,0:T(8,128)(2,1)}, bf16[4,2,128,384]{3,2,1,0:T(8,128)(2,1)}, bf16[4,2,128,384]{3,2,1,0:T(8,128)(2,1)}) custom-call(s32[1,1]{1,0:T(1,128)S(6)} %copy.11.count_ref, bf16[128,2,3072]{2,1,0:T(2,128)(2,1)} %bitcast.4, bf16[3,28,3072]{2,1,0:T(8,128)(2,1)} %bitcast.5, s32[1,28]{1,0:T(1,128)} %chosen_hbm.1), custom_call_target="tpu_custom_call" | custom-call | tf_op jit(solution)/shard_map/pallas_call | solution.py:292
  4.2 0.1 collective-permute-start
  4.3 8.3 %all-to-all-start = ((bf16[32,32,384]{2,1,0:T(8,128)(2,1)}), bf16[32,32,384]{2,1,0:T(8,128)(2,1)S(1)}, u32[]{:S(2)}, u32[]{:S(2)}) async-start(bf16[32,32,384]{2,1,0:T(8,128)(2,1)} %get-tuple-element.25), calls=%async_computation | async-start | bytes 1572864 | tf_op jit(solution)/shard_map/all_to_all | solution.py:308
  12.7 0.0 collective-permute-done.first_ref
  12.7 1.1 %copy-done = bf16[4,2,128,384]{3,2,1,0:T(8,128)(2,1)S(1)} copy-done((bf16[4,2,128,384]{3,2,1,0:T(8,128)(2,1)S(1)}, bf16[4,2,128,384]{3,2,1,0:T(8,128)(2,1)}, u32[]{:S(2)}) %copy-start) | copy-done | bytes 786456
  13.8 0.1 shard_map.101
  14.0 1.9 %collective-permute-start.1 = (bf16[2,2,128,384]{3,2,1,0:T(8,128)(2,1)S(1)}, bf16[2,2,128,384]{3,2,1,0:T(8,128)(2,1)S(1)}, u32[]{:S(2)}, u32[]{:S(2)}) collective-permute-start(bf16[2,2,128,384]{3,2,1,0:T(8,128)(2,1)S(1)} %get-tuple-element.28), channel_id=1, source_target_pairs={{0,2},{1,9},{2,4},{3,11},{4,6},{5,13},{6,0},{7,15},{8,10},{9,17},{... | collective-permute-start | bytes 1179656 | tf_op jit(solution)/shard_map/ppermute | solution.py:312
  15.8 2.7 %collective-permute-start.2 = (bf16[2,2,128,384]{3,2,1,0:T(8,128)(2,1)S(1)}, bf16[2,2,128,384]{3,2,1,0:T(8,128)(2,1)S(1)}, u32[]{:S(2)}, u32[]{:S(2)}) collective-permute-start(bf16[2,2,128,384]{3,2,1,0:T(8,128)(2,1)S(1)} %get-tuple-element.29), channel_id=1, source_target_pairs={{0,4},{1,17},{2,6},{3,19},{4,0},{5,21},{6,2},{7,23},{8,12},{9,25},... | collective-permute-start | bytes 1179656 | tf_op jit(solution)/shard_map/ppermute | solution.py:312
  18.5 1.5 %collective-permute-start.3 = (bf16[2,2,128,384]{3,2,1,0:T(8,128)(2,1)S(1)}, bf16[2,2,128,384]{3,2,1,0:T(8,128)(2,1)S(1)}, u32[]{:S(2)}, u32[]{:S(2)}) collective-permute-start(bf16[2,2,128,384]{3,2,1,0:T(8,128)(2,1)S(1)} %get-tuple-element.30), channel_id=1, source_target_pairs={{0,6},{1,25},{2,0},{3,27},{4,2},{5,29},{6,4},{7,31},{8,14},{9,1},{... | collective-permute-start | bytes 1179656 | tf_op jit(solution)/shard_map/ppermute | solution.py:312
  20.0 7.3 %all-to-all-done.q_ref = bf16[32,32,384]{2,1,0:T(8,128)(2,1)S(1)} async-done(((bf16[32,32,384]{2,1,0:T(8,128)(2,1)}), bf16[32,32,384]{2,1,0:T(8,128)(2,1)S(1)}, u32[]{:S(2)}, u32[]{:S(2)}) %all-to-all-start) | async-done | bytes 786464 | tf_op jit(solution)/shard_map/all_to_all | solution.py:308
  27.3 1.7 %shard_map.102 = (f32[3,128,1024]{2,1,0:T(8,128)S(1)}, f32[8,1024]{1,0:T(8,128)S(1)}) custom-call(bf16[32,32,384]{2,1,0:T(8,128)(2,1)S(1)} %all-to-all-done.q_ref, bf16[2,2,128,384]{3,2,1,0:T(8,128)(2,1)S(1)} %get-tuple-element.31.r0_ref), custom_call_target="tpu_custom_call" | custom-call | bytes 5280000 | tf_op jit(solution)/shard_map/pallas_call | solution.py:318
  28.9 0.0 copy-start.1
  29.0 0.9 %copy-done.1 = bf16[1,28,3072]{2,1,0:T(8,128)(2,1)S(1)} copy-done((bf16[1,28,3072]{2,1,0:T(8,128)(2,1)S(1)}, bf16[1,28,3072]{2,1,0:T(8,128)(2,1)}, u32[]{:S(2)}) %copy-start.1) | copy-done | bytes 172056
  29.9 0.7 copy-done.2
  30.6 0.3 shard_map.103
  30.9 3.0 %collective-permute-done.2.r2_ref = bf16[2,2,128,384]{3,2,1,0:T(8,128)(2,1)S(1)} collective-permute-done((bf16[2,2,128,384]{3,2,1,0:T(8,128)(2,1)S(1)}, bf16[2,2,128,384]{3,2,1,0:T(8,128)(2,1)S(1)}, u32[]{:S(2)}, u32[]{:S(2)}) %collective-permute-start.2) | collective-permute-done | bytes 393248 | tf_op jit(solution)/shard_map/ppermute | solution.py:312
  33.9 3.7 %shard_map.104 = bf16[32,32,384]{2,1,0:T(8,128)(2,1)S(1)} custom-call(bf16[32,32,384]{2,1,0:T(8,128)(2,1)S(1)} %all-to-all-done.q_ref, bf16[2,2,128,384]{3,2,1,0:T(8,128)(2,1)S(1)} %collective-permute-done.1.r1_ref, bf16[2,2,128,384]{3,2,1,0:T(8,128)(2,1)S(1)} %collective-permute-done.2.r2_ref, bf16[2,2,128,384]{3,2,1,0:T(8,128)(2,1)S(1)} %collective-permute-done.3.r3_ref, ...), custom_call_target="tpu_custom_call" | custom-call | bytes 15179999 | tf_op jit(solution)/shard_map/pallas_call | solution.py:327
  37.7 19.7 %all_to_all.10.parts_ref = bf16[32,32,384]{2,1,0:T(8,128)(2,1)S(1)} all-to-all(bf16[32,32,384]{2,1,0:T(8,128)(2,1)S(1)} %shard_map.104), channel_id=1, replica_groups=mesh['y'=4,'z'=4,'x'=4,'core'=2] {'z','x','core'}, dimensions={0} | all-to-all | bytes 1572864 | tf_op jit(solution)/shard_map/all_to_all | solution.py:335
  57.3 1.1 %shard_map.105 = (f32[28,3072]{1,0:T(8,128)S(1)}, bf16[56,1536]{1,0:T(8,128)(2,1)S(1)}, bf16[16,128]{1,0:T(8,128)(2,1)S(1)}) custom-call(bf16[32,32,384]{2,1,0:T(8,128)(2,1)S(1)} %all_to_all.10.parts_ref, bf16[1,28,3072]{2,1,0:T(8,128)(2,1)S(1)} %get-tuple-element.35.rows_ref, bf16[1,4,3072]{2,1,0:T(4,128)(2,1)S(1)} %get-tuple-element.34.after_ref.mod_ref), custom_call_target="tpu_custom_call" | custom-call | bytes 5280000 | tf_op jit(solution)/shard_map/pallas_call | solution.py:336
  58.5 1.7 %collective-permute-start.4 = (bf16[56,1536]{1,0:T(8,128)(2,1)S(1)}, bf16[56,1536]{1,0:T(8,128)(2,1)S(1)}, u32[]{:S(2)}, u32[]{:S(2)}) collective-permute-start(bf16[56,1536]{1,0:T(8,128)(2,1)S(1)} %get-tuple-element.36.r0_ref), channel_id=1, source_target_pairs={{0,32},{32,64},{64,96},{96,0},{1,33},{33,65},{65,97},{97,1},{2,34}... | collective-permute-start | bytes 516104 | tf_op jit(solution)/shard_map/ppermute | solution.py:344
  60.1 2.9 %collective-permute-start.5 = (bf16[56,1536]{1,0:T(8,128)(2,1)S(1)}, bf16[56,1536]{1,0:T(8,128)(2,1)S(1)}, u32[]{:S(2)}, u32[]{:S(2)}) collective-permute-start(bf16[56,1536]{1,0:T(8,128)(2,1)S(1)} %get-tuple-element.36.r0_ref), channel_id=1, source_target_pairs={{0,64},{32,96},{64,0},{96,32},{1,65},{33,97},{65,1},{97,33},{2,66}... | collective-permute-start | bytes 516104 | tf_op jit(solution)/shard_map/ppermute | solution.py:344
  63.0 1.3 %collective-permute-start.6 = (bf16[56,1536]{1,0:T(8,128)(2,1)S(1)}, bf16[56,1536]{1,0:T(8,128)(2,1)S(1)}, u32[]{:S(2)}, u32[]{:S(2)}) collective-permute-start(bf16[56,1536]{1,0:T(8,128)(2,1)S(1)} %get-tuple-element.36.r0_ref), channel_id=1, source_target_pairs={{0,96},{32,0},{64,32},{96,64},{1,97},{33,1},{65,33},{97,65},{2,98}... | collective-permute-start | bytes 516104 | tf_op jit(solution)/shard_map/ppermute | solution.py:344
  64.4 6.4 %shard_map.106 = (bf16[3072,1536]{1,0:T(8,128)(2,1)S(1)}, bf16[1536,3072]{1,0:T(8,128)(2,1)S(1)}) custom-call(bf16[16,128]{1,0:T(8,128)(2,1)S(1)} %get-tuple-element.37.after_ref, bf16[3072,1536]{1,0:T(8,128)(2,1)} %refs_0_.3, bf16[1536,3072]{1,0:T(8,128)(2,1)} %refs_1_.3), custom_call_target="tpu_custom_call" | custom-call | bytes 11880000 | tf_op jit(solution)/shard_map/pallas_call | solution.py:227
  70.8 0.1 collective-permute-done.5.r2_ref
  70.9 2.9 %shard_map.107 = (bf16[56,1536]{1,0:T(8,128)(2,1)S(1)}, bf16[56,1536]{1,0:T(8,128)(2,1)S(1)}, bf16[56,1536]{1,0:T(8,128)(2,1)S(1)}, bf16[56,1536]{1,0:T(8,128)(2,1)S(1)}) custom-call(bf16[56,1536]{1,0:T(8,128)(2,1)S(1)} %get-tuple-element.36.r0_ref, bf16[56,1536]{1,0:T(8,128)(2,1)S(1)} %collective-permute-done.4.r1_ref, ...), custom_call_target="tpu_custom_call" | custom-call | bytes 12210000 | tf_op jit(solution)/shard_map/pallas_call | solution.py:347
  73.8 2.6 %collective-permute-start.7 = (bf16[56,1536]{1,0:T(8,128)(2,1)S(1)}, bf16[56,1536]{1,0:T(8,128)(2,1)S(1)}, u32[]{:S(2)}, u32[]{:S(2)}) collective-permute-start(bf16[56,1536]{1,0:T(8,128)(2,1)S(1)} %get-tuple-element.41), channel_id=1, source_target_pairs={{0,64},{32,96},{64,0},{96,32},{1,65},{33,97},{65,1},{97,33},{2,66}... | collective-permute-start | bytes 516104 | tf_op jit(solution)/shard_map/ppermute | solution.py:358
  76.5 1.3 %collective-permute-start.8 = (bf16[56,1536]{1,0:T(8,128)(2,1)S(1)}, bf16[56,1536]{1,0:T(8,128)(2,1)S(1)}, u32[]{:S(2)}, u32[]{:S(2)}) collective-permute-start(bf16[56,1536]{1,0:T(8,128)(2,1)S(1)} %get-tuple-element.42), channel_id=1, source_target_pairs={{0,96},{32,0},{64,32},{96,64},{1,97},{33,1},{65,33},{97,65},{2,98}... | collective-permute-start | bytes 516104 | tf_op jit(solution)/shard_map/ppermute | solution.py:358
  77.8 0.7 collective-permute-start.9
  78.5 4.2 %collective-permute-done.7.t1_ref = bf16[56,1536]{1,0:T(8,128)(2,1)S(1)} collective-permute-done((bf16[56,1536]{1,0:T(8,128)(2,1)S(1)}, bf16[56,1536]{1,0:T(8,128)(2,1)S(1)}, u32[]{:S(2)}, u32[]{:S(2)}) %collective-permute-start.7) | collective-permute-done | bytes 172064 | tf_op jit(solution)/shard_map/ppermute | solution.py:358
  82.7 1.7 %collective-permute-done.8.t2_ref = bf16[56,1536]{1,0:T(8,128)(2,1)S(1)} collective-permute-done((bf16[56,1536]{1,0:T(8,128)(2,1)S(1)}, bf16[56,1536]{1,0:T(8,128)(2,1)S(1)}, u32[]{:S(2)}, u32[]{:S(2)}) %collective-permute-start.8) | collective-permute-done | bytes 172064 | tf_op jit(solution)/shard_map/ppermute | solution.py:358
  84.4 0.8 collective-permute-done.9.t3_ref
  85.2 0.9 shard_map.108
  (14 shorter events, 0.0 us)
Async XLA Ops:
  0.0 64.4 %copy-start.5 = (bf16[1536]{0:T(1024)(128)(2,1)S(1)}, bf16[1536]{0:T(1024)(128)(2,1)}, u32[]{:S(2)}) copy-start(bf16[1536]{0:T(1024)(128)(2,1)} %param.17) | copy-start | bytes 9220
  4.2 8.5 %collective-permute-start = (bf16[4,2,128,384]{3,2,1,0:T(8,128)(2,1)}, bf16[4,2,128,384]{3,2,1,0:T(8,128)(2,1)S(1)}, u32[]{:S(2)}, u32[]{:S(2)}) collective-permute-start(bf16[4,2,128,384]{3,2,1,0:T(8,128)(2,1)} %get-tuple-element.27), channel_id=1, source_target_pairs={{0,1},{1,0},{2,3},{3,2},{4,5},{5,4},{6,7},{7,6},{8,9},{9,8},{10,11... | collective-permute-start | bytes 2359304 | tf_op jit(solution)/shard_map/ppermute | solution.py:310
  4.3 22.9 %all-to-all-start = ((bf16[32,32,384]{2,1,0:T(8,128)(2,1)}), bf16[32,32,384]{2,1,0:T(8,128)(2,1)S(1)}, u32[]{:S(2)}, u32[]{:S(2)}) async-start(bf16[32,32,384]{2,1,0:T(8,128)(2,1)} %get-tuple-element.25), calls=%async_computation | async-start | bytes 1572864 | tf_op jit(solution)/shard_map/all_to_all | solution.py:308
  12.7 1.1 %copy-start = (bf16[4,2,128,384]{3,2,1,0:T(8,128)(2,1)S(1)}, bf16[4,2,128,384]{3,2,1,0:T(8,128)(2,1)}, u32[]{:S(2)}) copy-start(bf16[4,2,128,384]{3,2,1,0:T(8,128)(2,1)} %get-tuple-element.26.keep_ref) | copy-start | bytes 2359300
  14.0 16.9 %collective-permute-start.1 = (bf16[2,2,128,384]{3,2,1,0:T(8,128)(2,1)S(1)}, bf16[2,2,128,384]{3,2,1,0:T(8,128)(2,1)S(1)}, u32[]{:S(2)}, u32[]{:S(2)}) collective-permute-start(bf16[2,2,128,384]{3,2,1,0:T(8,128)(2,1)S(1)} %get-tuple-element.28), channel_id=1, source_target_pairs={{0,2},{1,9},{2,4},{3,11},{4,6},{5,13},{6,0},{7,15},{8,10},{9,17},{... | collective-permute-start | bytes 1179656 | tf_op jit(solution)/shard_map/ppermute | solution.py:312
  15.8 18.1 %collective-permute-start.2 = (bf16[2,2,128,384]{3,2,1,0:T(8,128)(2,1)S(1)}, bf16[2,2,128,384]{3,2,1,0:T(8,128)(2,1)S(1)}, u32[]{:S(2)}, u32[]{:S(2)}) collective-permute-start(bf16[2,2,128,384]{3,2,1,0:T(8,128)(2,1)S(1)} %get-tuple-element.29), channel_id=1, source_target_pairs={{0,4},{1,17},{2,6},{3,19},{4,0},{5,21},{6,2},{7,23},{8,12},{9,25},... | collective-permute-start | bytes 1179656 | tf_op jit(solution)/shard_map/ppermute | solution.py:312
  18.5 15.4 %collective-permute-start.3 = (bf16[2,2,128,384]{3,2,1,0:T(8,128)(2,1)S(1)}, bf16[2,2,128,384]{3,2,1,0:T(8,128)(2,1)S(1)}, u32[]{:S(2)}, u32[]{:S(2)}) collective-permute-start(bf16[2,2,128,384]{3,2,1,0:T(8,128)(2,1)S(1)} %get-tuple-element.30), channel_id=1, source_target_pairs={{0,6},{1,25},{2,0},{3,27},{4,2},{5,29},{6,4},{7,31},{8,14},{9,1},{... | collective-permute-start | bytes 1179656 | tf_op jit(solution)/shard_map/ppermute | solution.py:312
  28.9 0.9 %copy-start.1 = (bf16[1,28,3072]{2,1,0:T(8,128)(2,1)S(1)}, bf16[1,28,3072]{2,1,0:T(8,128)(2,1)}, u32[]{:S(2)}) copy-start(bf16[1,28,3072]{2,1,0:T(8,128)(2,1)} %refs_0_.2) | copy-start | bytes 516100
  29.9 0.7 copy-start.2
  58.5 12.3 %collective-permute-start.4 = (bf16[56,1536]{1,0:T(8,128)(2,1)S(1)}, bf16[56,1536]{1,0:T(8,128)(2,1)S(1)}, u32[]{:S(2)}, u32[]{:S(2)}) collective-permute-start(bf16[56,1536]{1,0:T(8,128)(2,1)S(1)} %get-tuple-element.36.r0_ref), channel_id=1, source_target_pairs={{0,32},{32,64},{64,96},{96,0},{1,33},{33,65},{65,97},{97,1},{2,34}... | collective-permute-start | bytes 516104 | tf_op jit(solution)/shard_map/ppermute | solution.py:344
  60.1 10.8 %collective-permute-start.5 = (bf16[56,1536]{1,0:T(8,128)(2,1)S(1)}, bf16[56,1536]{1,0:T(8,128)(2,1)S(1)}, u32[]{:S(2)}, u32[]{:S(2)}) collective-permute-start(bf16[56,1536]{1,0:T(8,128)(2,1)S(1)} %get-tuple-element.36.r0_ref), channel_id=1, source_target_pairs={{0,64},{32,96},{64,0},{96,32},{1,65},{33,97},{65,1},{97,33},{2,66}... | collective-permute-start | bytes 516104 | tf_op jit(solution)/shard_map/ppermute | solution.py:344
  63.0 7.9 %collective-permute-start.6 = (bf16[56,1536]{1,0:T(8,128)(2,1)S(1)}, bf16[56,1536]{1,0:T(8,128)(2,1)S(1)}, u32[]{:S(2)}, u32[]{:S(2)}) collective-permute-start(bf16[56,1536]{1,0:T(8,128)(2,1)S(1)} %get-tuple-element.36.r0_ref), channel_id=1, source_target_pairs={{0,96},{32,0},{64,32},{96,64},{1,97},{33,1},{65,33},{97,65},{2,98}... | collective-permute-start | bytes 516104 | tf_op jit(solution)/shard_map/ppermute | solution.py:344
  70.9 7.6 %copy-start.4 = (bf16[3072]{0:T(1024)(128)(2,1)S(1)}, bf16[3072]{0:T(1024)(128)(2,1)}, u32[]{:S(2)}) copy-start(bf16[3072]{0:T(1024)(128)(2,1)} %param.19) | copy-start | bytes 18436
  70.9 14.3 %copy-start.3 = (bf16[1,4,3072]{2,1,0:T(4,128)(2,1)S(1)}, bf16[1,4,3072]{2,1,0:T(4,128)(2,1)}, u32[]{:S(2)}) copy-start(bf16[1,4,3072]{2,1,0:T(4,128)(2,1)} %mod_ref.1) | copy-start | bytes 73732
  73.8 8.9 %collective-permute-start.7 = (bf16[56,1536]{1,0:T(8,128)(2,1)S(1)}, bf16[56,1536]{1,0:T(8,128)(2,1)S(1)}, u32[]{:S(2)}, u32[]{:S(2)}) collective-permute-start(bf16[56,1536]{1,0:T(8,128)(2,1)S(1)} %get-tuple-element.41), channel_id=1, source_target_pairs={{0,64},{32,96},{64,0},{96,32},{1,65},{33,97},{65,1},{97,33},{2,66}... | collective-permute-start | bytes 516104 | tf_op jit(solution)/shard_map/ppermute | solution.py:358
  76.5 8.0 %collective-permute-start.8 = (bf16[56,1536]{1,0:T(8,128)(2,1)S(1)}, bf16[56,1536]{1,0:T(8,128)(2,1)S(1)}, u32[]{:S(2)}, u32[]{:S(2)}) collective-permute-start(bf16[56,1536]{1,0:T(8,128)(2,1)S(1)} %get-tuple-element.42), channel_id=1, source_target_pairs={{0,96},{32,0},{64,32},{96,64},{1,97},{33,1},{65,33},{97,65},{2,98}... | collective-permute-start | bytes 516104 | tf_op jit(solution)/shard_map/ppermute | solution.py:358
  77.8 7.4 %collective-permute-start.9 = (bf16[56,1536]{1,0:T(8,128)(2,1)S(1)}, bf16[56,1536]{1,0:T(8,128)(2,1)S(1)}, u32[]{:S(2)}, u32[]{:S(2)}) collective-permute-start(bf16[56,1536]{1,0:T(8,128)(2,1)S(1)} %get-tuple-element.43), channel_id=1, source_target_pairs={{0,32},{32,64},{64,96},{96,0},{1,33},{33,65},{65,97},{97,1},{2,34}... | collective-permute-start | bytes 516104 | tf_op jit(solution)/shard_map/ppermute | solution.py:358

commit v8 on v7

--- a/solution.py
+++ b/solution.py
@@ -46,9 +46,10 @@
 ):
     sources = [
         (fresh_hbm.at[0], fresh_ref.at[0]),
-        (kv_hbm, kv_ref),
         (fresh_hbm.at[1:3], fresh_ref.at[1:3]),
         (chosen_hbm, chosen_ref),
+        (kv_hbm.at[0:64], kv_ref.at[0:64]),
+        (kv_hbm.at[64:128], kv_ref.at[64:128]),
     ]
     copies = [pltpu.make_async_copy(src, dst, in_sems.at[i]) for i, (src, dst) in enumerate(sources)]
     for copy in copies:
@@ -66,36 +67,42 @@
 
     core, ring_x, ring_z = (lax.axis_index(a) for a in ("core", "x", "z"))
     count = count_ref[0, 0]
-    for copy in copies[1:]:
-        copy.wait()
+    copies[1].wait()
+    copies[2].wait()
     token_id = lax.broadcasted_iota(i32, (tokens, slots), 0)
     slot_id = lax.broadcasted_iota(i32, (tokens, slots), 1)
     hit = (token_id == chosen_ref[...]) & (slot_id < count)
     hot = jnp.where(hit, 1.0, 0.0)
     taken = jnp.sum(hot, axis=1, keepdims=True) > 0.5
     hot = hot.astype(bf16)
-    old = jnp.swapaxes(kv_ref[...], 0, 1)
     half = 4 * BLOCK
-    for which in range(2):
-        new = jnp.dot(hot, fresh_ref[1 + which], preferred_element_type=f32)
-        patched[which] = jnp.where(taken, new, old[which].astype(f32)).astype(bf16)
-        for k in range(4):
-            mine = lax.rem(jnp.where(core == 0, ring_x, ring_z) + k, 4)
-            other = lax.rem(jnp.where(core == 0, ring_z, ring_x) + k, 4)
-            at_mine = pl.multiple_of(core * half + mine * BLOCK, BLOCK)
-            at_other = pl.multiple_of((1 - core) * half + other * BLOCK, BLOCK)
-            for at, target in ((at_other, send_hbm), (at_mine, keep_hbm)):
-                copy = pltpu.make_async_copy(
-                    patched.at[which, :, pl.ds(at, BLOCK)], target.at[k, which], out_sems.at[len(outs)]
-                )
-                copy.start()
-                outs.append(copy)
+    part = tokens // 2
+    for step in range(2):
+        here = slice(step * part, (step + 1) * part)
+        copies[3 + step].wait()
+        old = jnp.swapaxes(kv_ref[here], 0, 1)
+        for which in range(2):
+            new = jnp.dot(hot[here], fresh_ref[1 + which], preferred_element_type=f32)
+            patched[which, here] = jnp.where(taken[here], new, old[which].astype(f32)).astype(bf16)
+            for k in range(4):
+                mine = lax.rem(jnp.where(core == 0, ring_x, ring_z) + k, 4)
+                other = lax.rem(jnp.where(core == 0, ring_z, ring_x) + k, 4)
+                at_mine = pl.multiple_of(core * half + mine * BLOCK, BLOCK)
+                at_other = pl.multiple_of((1 - core) * half + other * BLOCK, BLOCK)
+                for at, target in ((at_other, send_hbm), (at_mine, keep_hbm)):
+                    copy = pltpu.make_async_copy(
+                        patched.at[which, here, pl.ds(at, BLOCK)],
+                        target.at[k, which, here],
+                        out_sems.at[len(outs)],
+                    )
+                    copy.start()
+                    outs.append(copy)
     for copy in outs:
         copy.wait()
 
 
 def stack_kernel(keep_ref, first_ref, *out_refs):
-    for k, out_ref in enumerate(out_refs):
+    for k, out_ref in enumerate(out_refs, 1):
         out_ref[0] = keep_ref[k]
         out_ref[1] = first_ref[k]
 
@@ -104,12 +111,11 @@
     rows = 128
     at = 0
     for ref in sources:
-        for core in range(2):
-            keys[at : at + rows, :] = ref[core, 0]
-            for h in range(HEADS_HERE):
-                cols = slice(h * HEAD_DIM, (h + 1) * HEAD_DIM)
-                values_t[h, :, at : at + rows] = ref[core, 1, :, cols].T
-            at += rows
+        keys[at : at + rows, :] = ref[0]
+        for h in range(HEADS_HERE):
+            cols = slice(h * HEAD_DIM, (h + 1) * HEAD_DIM)
+            values_t[h, :, at : at + rows] = ref[1, :, cols].T
+        at += rows
 
 
 def head_scores(q_all, keys, h):
@@ -122,8 +128,8 @@
 SCALE = LOG2E * HEAD_DIM**-0.5
 
 
-def attention_first_kernel(q_ref, r0_ref, mixed_ref, stats_ref, keys, values_t):
-    gather_keys((r0_ref,), keys, values_t)
+def attention_first_kernel(q_ref, keep_ref, first_ref, mixed_ref, stats_ref, keys, values_t):
+    gather_keys((keep_ref.at[0], first_ref.at[0]), keys, values_t)
     q_all = q_ref[...].reshape(-1, BLOCK)
     for h in range(HEADS_HERE):
         scores = head_scores(q_all, keys, h)
@@ -137,7 +143,8 @@
 def attention_second_kernel(
     q_ref, r1_ref, r2_ref, r3_ref, mixed_ref, stats_ref, after_ref, out_ref, keys, values_t
 ):
-    gather_keys((r1_ref, r2_ref, r3_ref), keys, values_t)
+    sources = [ref.at[core] for ref in (r1_ref, r2_ref, r3_ref) for core in range(2)]
+    gather_keys(sources, keys, values_t)
     q_all = q_ref[...].reshape(-1, BLOCK)
     for h in range(HEADS_HERE):
         cols = slice(h * HEAD_DIM, (h + 1) * HEAD_DIM)
@@ -300,16 +307,16 @@
             pltpu.VMEM((1, slots), i32),
             pltpu.VMEM((2, tokens, width), bf16),
             pltpu.VMEM((32, SLOT_PAD, BLOCK), bf16),
-            pltpu.SemaphoreType.DMA((4,)),
-            pltpu.SemaphoreType.DMA((17,)),
+            pltpu.SemaphoreType.DMA((5,)),
+            pltpu.SemaphoreType.DMA((33,)),
         ],
         compiler_params=pltpu.CompilerParams(vmem_limit_bytes=61 * MB),
     )(counts, kv_cache[0], fresh, chosen)
     q_all = lax.all_to_all(q_blocks, SEQ, 0, 0, tiled=True)
     swap = [(position(z, x, c), position(z, x, 1 - c)) for z in range(4) for x in range(4) for c in range(2)]
     first = lax.ppermute(send, SEQ, swap)
-    stacked = call(stack_kernel, [shape((2, 2, tokens, BLOCK), bf16)] * 4, n_in=2)(keep, first)
-    others = [lax.ppermute(stacked[k], SEQ, ring_pairs(k)) for k in (1, 2, 3)]
+    stacked = call(stack_kernel, [shape((2, 2, tokens, BLOCK), bf16)] * 3, n_in=2)(keep, first)
+    others = [lax.ppermute(stacked[k - 1], SEQ, ring_pairs(k)) for k in (1, 2, 3)]
 
 
     def key_scratch(count):
@@ -319,10 +326,10 @@
         attention_first_kernel,
         [shape((HEADS_HERE, HEAD_DIM, 32 * SLOT_PAD), f32), shape((8, 32 * SLOT_PAD), f32)],
         scratch=key_scratch(2 * tokens),
-        n_in=2,
+        n_in=3,
         limit=24,
         us=1.6,
-    )(q_all, stacked[0])
+    )(q_all, keep, first)
     rows, mod = load(stats, [rows_in, modulation], 16)
     partial = call(
         attention_second_kernel,

time: 86.5 us -> 86.3 us (level)
  waiting for transfers between devices: 17.1 us -> 15.3 us
  local copies, waits for them, and re-layouts: 2.81 us -> 3.94 us
    ppermute x3, waiting for transfers between devices: 3.03 us -> 1.89 us  [body(): lax.ppermute(stacked[k - 1], SEQ, ring_pairs(k))]
    unnamed x12 -> x14, local copies, waits for them, and re-layouts: 2.8 us -> 3.93 us
  transfers between devices with their start and end apart: 11 -> 11, of which waited for: 6 -> 6; matrix products, arithmetic and copies ran while one was open for 0% -> 0% of each run, Pallas kernels for 10% -> 11%
where the time goes in v8:
time: 86.3 us; the launch traced here: 85.8 us
  starting transfers between devices  24.9 us (29%)
  Pallas kernels  21.2 us (25%)
  blocking collectives  19.7 us (23%)
  waiting for transfers between devices  15.3 us (18%)
  local copies, waits for them, and re-layouts  3.94 us (5%)
    all_to_all x1, blocking collectives, body(): parts = lax.all_to_all(partial, SEQ, 0, 0, tiled=True)  19.7 us
    all_to_all x1, starting transfers between devices, body(): q_all = lax.all_to_all(q_blocks, SEQ, 0, 0, tiled=True)  8.36 us
    ppermute x3, waiting for transfers between devices, body(): back = [lax.ppermute(terms[k], 'y', turn(-k)) for k in (2, 1, 3)]  6.67 us
    pallas_call x2, Pallas kernels, load(): call(load_kernel, [jax.ShapeDtypeStruct(v.shape, bf16) for v in arrays],...  6.66 us
    all_to_all x1, waiting for transfers between devices, body(): q_all = lax.all_to_all(q_blocks, SEQ, 0, 0, tiled=True)  6.61 us
    ppermute x3, starting transfers between devices, body(): lax.ppermute(stacked[k - 1], SEQ, ring_pairs(k))  5.93 us
    ppermute x3, starting transfers between devices, body(): far, near, last = (lax.ppermute(normed, 'y', turn(k)) for k in (2, 1, 3))  5.86 us
    ppermute x3, starting transfers between devices, body(): back = [lax.ppermute(terms[k], 'y', turn(-k)) for k in (2, 1, 3)]  4.69 us
  transfers between devices with their start and end apart: 11, of which 6 were waited for; matrix products, arithmetic and copies ran while one was open for 0% of the time, Pallas kernels for 11%

profile of v8, /device:TPU:0, one launch (start us, length us, event | category | flops | bytes accessed | tf_op | source)
XLA Modules:
  0.0 85.8 jit_solution(13651750071495608326)
XLA Ops:
  0.7 3.4 %shard_map.100 = (bf16[32,32,384]{2,1,0:T(8,128)(2,1)}, bf16[4,2,128,384]{3,2,1,0:T(8,128)(2,1)}, bf16[4,2,128,384]{3,2,1,0:T(8,128)(2,1)}) custom-call(s32[1,1]{1,0:T(1,128)S(6)} %copy.11.count_ref, bf16[128,2,3072]{2,1,0:T(2,128)(2,1)} %bitcast.4, bf16[3,28,3072]{2,1,0:T(8,128)(2,1)} %bitcast.5, s32[1,28]{1,0:T(1,128)} %chosen_hbm.1), custom_call_target="tpu_custom_call" | custom-call | tf_op jit(solution)/shard_map/pallas_call | solution.py:299
  4.1 0.1 collective-permute-start
  4.2 8.4 %all-to-all-start = ((bf16[32,32,384]{2,1,0:T(8,128)(2,1)}), bf16[32,32,384]{2,1,0:T(8,128)(2,1)S(1)}, u32[]{:S(2)}, u32[]{:S(2)}) async-start(bf16[32,32,384]{2,1,0:T(8,128)(2,1)} %get-tuple-element.24), calls=%async_computation | async-start | bytes 1572864 | tf_op jit(solution)/shard_map/all_to_all | solution.py:315
  12.5 1.1 %copy-done = bf16[4,2,128,384]{3,2,1,0:T(8,128)(2,1)S(1)} copy-done((bf16[4,2,128,384]{3,2,1,0:T(8,128)(2,1)S(1)}, bf16[4,2,128,384]{3,2,1,0:T(8,128)(2,1)}, u32[]{:S(2)}) %copy-start) | copy-done | bytes 786456
  13.7 0.9 %shard_map.101 = (bf16[2,2,128,384]{3,2,1,0:T(8,128)(2,1)}, bf16[2,2,128,384]{3,2,1,0:T(8,128)(2,1)S(1)}, bf16[2,2,128,384]{3,2,1,0:T(8,128)(2,1)S(1)}) custom-call(bf16[4,2,128,384]{3,2,1,0:T(8,128)(2,1)S(1)} %copy-done, bf16[4,2,128,384]{3,2,1,0:T(8,128)(2,1)S(1)} %collective-permute-done.first_ref), custom_call_target="tpu_custom_call" | custom-call | bytes 3300000 | tf_op jit(solution)/shard_map/pallas_call | solution.py:318
  14.6 1.8 %collective-permute-start.1 = (bf16[2,2,128,384]{3,2,1,0:T(8,128)(2,1)}, bf16[2,2,128,384]{3,2,1,0:T(8,128)(2,1)S(1)}, u32[]{:S(2)}, u32[]{:S(2)}) collective-permute-start(bf16[2,2,128,384]{3,2,1,0:T(8,128)(2,1)} %get-tuple-element.27), channel_id=1, source_target_pairs={{0,2},{1,9},{2,4},{3,11},{4,6},{5,13},{6,0},{7,15},{8,10},{9,17},{... | collective-permute-start | bytes 1179656 | tf_op jit(solution)/shard_map/ppermute | solution.py:319
  16.3 2.7 %collective-permute-start.2 = (bf16[2,2,128,384]{3,2,1,0:T(8,128)(2,1)S(1)}, bf16[2,2,128,384]{3,2,1,0:T(8,128)(2,1)S(1)}, u32[]{:S(2)}, u32[]{:S(2)}) collective-permute-start(bf16[2,2,128,384]{3,2,1,0:T(8,128)(2,1)S(1)} %get-tuple-element.28), channel_id=1, source_target_pairs={{0,4},{1,17},{2,6},{3,19},{4,0},{5,21},{6,2},{7,23},{8,12},{9,25},... | collective-permute-start | bytes 1179656 | tf_op jit(solution)/shard_map/ppermute | solution.py:319
  19.0 1.5 %collective-permute-start.3 = (bf16[2,2,128,384]{3,2,1,0:T(8,128)(2,1)S(1)}, bf16[2,2,128,384]{3,2,1,0:T(8,128)(2,1)S(1)}, u32[]{:S(2)}, u32[]{:S(2)}) collective-permute-start(bf16[2,2,128,384]{3,2,1,0:T(8,128)(2,1)S(1)} %get-tuple-element.29), channel_id=1, source_target_pairs={{0,6},{1,25},{2,0},{3,27},{4,2},{5,29},{6,4},{7,31},{8,14},{9,1},{... | collective-permute-start | bytes 1179656 | tf_op jit(solution)/shard_map/ppermute | solution.py:319
  20.5 6.6 %all-to-all-done.q_ref = bf16[32,32,384]{2,1,0:T(8,128)(2,1)S(1)} async-done(((bf16[32,32,384]{2,1,0:T(8,128)(2,1)}), bf16[32,32,384]{2,1,0:T(8,128)(2,1)S(1)}, u32[]{:S(2)}, u32[]{:S(2)}) %all-to-all-start) | async-done | bytes 786464 | tf_op jit(solution)/shard_map/all_to_all | solution.py:315
  27.1 1.1 %copy-done.1 = bf16[4,2,128,384]{3,2,1,0:T(8,128)(2,1)S(1)} copy-done((bf16[4,2,128,384]{3,2,1,0:T(8,128)(2,1)S(1)}, bf16[4,2,128,384]{3,2,1,0:T(8,128)(2,1)}, u32[]{:S(2)}) %copy-start.1) | copy-done | bytes 786456
  28.2 1.7 %shard_map.102 = (f32[3,128,1024]{2,1,0:T(8,128)S(1)}, f32[8,1024]{1,0:T(8,128)S(1)}) custom-call(bf16[32,32,384]{2,1,0:T(8,128)(2,1)S(1)} %all-to-all-done.q_ref, bf16[4,2,128,384]{3,2,1,0:T(8,128)(2,1)S(1)} %copy-done.1, bf16[4,2,128,384]{3,2,1,0:T(8,128)(2,1)S(1)} %collective-permute-done.first_ref), custom_call_target="tpu_custom_call" | custom-call | bytes 5280000 | tf_op jit(solution)/shard_map/pallas_call | solution.py:325
  29.9 0.0 copy-start.2
  29.9 0.9 %copy-done.2 = bf16[1,28,3072]{2,1,0:T(8,128)(2,1)S(1)} copy-done((bf16[1,28,3072]{2,1,0:T(8,128)(2,1)S(1)}, bf16[1,28,3072]{2,1,0:T(8,128)(2,1)}, u32[]{:S(2)}) %copy-start.2) | copy-done | bytes 172056
  30.9 0.7 copy-done.3
  31.6 0.3 shard_map.103
  31.9 1.9 %collective-permute-done.2.r2_ref = bf16[2,2,128,384]{3,2,1,0:T(8,128)(2,1)S(1)} collective-permute-done((bf16[2,2,128,384]{3,2,1,0:T(8,128)(2,1)S(1)}, bf16[2,2,128,384]{3,2,1,0:T(8,128)(2,1)S(1)}, u32[]{:S(2)}, u32[]{:S(2)}) %collective-permute-start.2) | collective-permute-done | bytes 393248 | tf_op jit(solution)/shard_map/ppermute | solution.py:319
  33.8 3.7 %shard_map.104 = bf16[32,32,384]{2,1,0:T(8,128)(2,1)S(1)} custom-call(bf16[32,32,384]{2,1,0:T(8,128)(2,1)S(1)} %all-to-all-done.q_ref, bf16[2,2,128,384]{3,2,1,0:T(8,128)(2,1)S(1)} %collective-permute-done.1.r1_ref, bf16[2,2,128,384]{3,2,1,0:T(8,128)(2,1)S(1)} %collective-permute-done.2.r2_ref, bf16[2,2,128,384]{3,2,1,0:T(8,128)(2,1)S(1)} %collective-permute-done.3.r3_ref, ...), custom_call_target="tpu_custom_call" | custom-call | bytes 15179999 | tf_op jit(solution)/shard_map/pallas_call | solution.py:334
  37.5 19.7 %all_to_all.10.parts_ref = bf16[32,32,384]{2,1,0:T(8,128)(2,1)S(1)} all-to-all(bf16[32,32,384]{2,1,0:T(8,128)(2,1)S(1)} %shard_map.104), channel_id=1, replica_groups=mesh['y'=4,'z'=4,'x'=4,'core'=2] {'z','x','core'}, dimensions={0} | all-to-all | bytes 1572864 | tf_op jit(solution)/shard_map/all_to_all | solution.py:342
  57.2 1.1 %shard_map.105 = (f32[28,3072]{1,0:T(8,128)S(1)}, bf16[56,1536]{1,0:T(8,128)(2,1)S(1)}, bf16[16,128]{1,0:T(8,128)(2,1)S(1)}) custom-call(bf16[32,32,384]{2,1,0:T(8,128)(2,1)S(1)} %all_to_all.10.parts_ref, bf16[1,28,3072]{2,1,0:T(8,128)(2,1)S(1)} %get-tuple-element.33.rows_ref, bf16[1,4,3072]{2,1,0:T(4,128)(2,1)S(1)} %get-tuple-element.32.after_ref.mod_ref), custom_call_target="tpu_custom_call" | custom-call | bytes 5280000 | tf_op jit(solution)/shard_map/pallas_call | solution.py:343
  58.3 1.6 %collective-permute-start.4 = (bf16[56,1536]{1,0:T(8,128)(2,1)S(1)}, bf16[56,1536]{1,0:T(8,128)(2,1)S(1)}, u32[]{:S(2)}, u32[]{:S(2)}) collective-permute-start(bf16[56,1536]{1,0:T(8,128)(2,1)S(1)} %get-tuple-element.34.r0_ref), channel_id=1, source_target_pairs={{0,32},{32,64},{64,96},{96,0},{1,33},{33,65},{65,97},{97,1},{2,34}... | collective-permute-start | bytes 516104 | tf_op jit(solution)/shard_map/ppermute | solution.py:351
  60.0 2.9 %collective-permute-start.5 = (bf16[56,1536]{1,0:T(8,128)(2,1)S(1)}, bf16[56,1536]{1,0:T(8,128)(2,1)S(1)}, u32[]{:S(2)}, u32[]{:S(2)}) collective-permute-start(bf16[56,1536]{1,0:T(8,128)(2,1)S(1)} %get-tuple-element.34.r0_ref), channel_id=1, source_target_pairs={{0,64},{32,96},{64,0},{96,32},{1,65},{33,97},{65,1},{97,33},{2,66}... | collective-permute-start | bytes 516104 | tf_op jit(solution)/shard_map/ppermute | solution.py:351
  62.8 1.3 %collective-permute-start.6 = (bf16[56,1536]{1,0:T(8,128)(2,1)S(1)}, bf16[56,1536]{1,0:T(8,128)(2,1)S(1)}, u32[]{:S(2)}, u32[]{:S(2)}) collective-permute-start(bf16[56,1536]{1,0:T(8,128)(2,1)S(1)} %get-tuple-element.34.r0_ref), channel_id=1, source_target_pairs={{0,96},{32,0},{64,32},{96,64},{1,97},{33,1},{65,33},{97,65},{2,98}... | collective-permute-start | bytes 516104 | tf_op jit(solution)/shard_map/ppermute | solution.py:351
  64.2 6.4 %shard_map.106 = (bf16[3072,1536]{1,0:T(8,128)(2,1)S(1)}, bf16[1536,3072]{1,0:T(8,128)(2,1)S(1)}) custom-call(bf16[16,128]{1,0:T(8,128)(2,1)S(1)} %get-tuple-element.35.after_ref, bf16[3072,1536]{1,0:T(8,128)(2,1)} %refs_0_.3, bf16[1536,3072]{1,0:T(8,128)(2,1)} %refs_1_.3), custom_call_target="tpu_custom_call" | custom-call | bytes 11880000 | tf_op jit(solution)/shard_map/pallas_call | solution.py:234
  70.6 0.1 collective-permute-done.5.r2_ref
  70.7 2.9 %shard_map.107 = (bf16[56,1536]{1,0:T(8,128)(2,1)S(1)}, bf16[56,1536]{1,0:T(8,128)(2,1)S(1)}, bf16[56,1536]{1,0:T(8,128)(2,1)S(1)}, bf16[56,1536]{1,0:T(8,128)(2,1)S(1)}) custom-call(bf16[56,1536]{1,0:T(8,128)(2,1)S(1)} %get-tuple-element.34.r0_ref, bf16[56,1536]{1,0:T(8,128)(2,1)S(1)} %collective-permute-done.4.r1_ref, ...), custom_call_target="tpu_custom_call" | custom-call | bytes 12210000 | tf_op jit(solution)/shard_map/pallas_call | solution.py:354
  73.6 2.7 %collective-permute-start.7 = (bf16[56,1536]{1,0:T(8,128)(2,1)S(1)}, bf16[56,1536]{1,0:T(8,128)(2,1)S(1)}, u32[]{:S(2)}, u32[]{:S(2)}) collective-permute-start(bf16[56,1536]{1,0:T(8,128)(2,1)S(1)} %get-tuple-element.39), channel_id=1, source_target_pairs={{0,64},{32,96},{64,0},{96,32},{1,65},{33,97},{65,1},{97,33},{2,66}... | collective-permute-start | bytes 516104 | tf_op jit(solution)/shard_map/ppermute | solution.py:365
  76.3 1.3 %collective-permute-start.8 = (bf16[56,1536]{1,0:T(8,128)(2,1)S(1)}, bf16[56,1536]{1,0:T(8,128)(2,1)S(1)}, u32[]{:S(2)}, u32[]{:S(2)}) collective-permute-start(bf16[56,1536]{1,0:T(8,128)(2,1)S(1)} %get-tuple-element.40), channel_id=1, source_target_pairs={{0,96},{32,0},{64,32},{96,64},{1,97},{33,1},{65,33},{97,65},{2,98}... | collective-permute-start | bytes 516104 | tf_op jit(solution)/shard_map/ppermute | solution.py:365
  77.6 0.7 collective-permute-start.9
  78.3 4.2 %collective-permute-done.7.t1_ref = bf16[56,1536]{1,0:T(8,128)(2,1)S(1)} collective-permute-done((bf16[56,1536]{1,0:T(8,128)(2,1)S(1)}, bf16[56,1536]{1,0:T(8,128)(2,1)S(1)}, u32[]{:S(2)}, u32[]{:S(2)}) %collective-permute-start.7) | collective-permute-done | bytes 172064 | tf_op jit(solution)/shard_map/ppermute | solution.py:365
  82.5 1.7 %collective-permute-done.8.t2_ref = bf16[56,1536]{1,0:T(8,128)(2,1)S(1)} collective-permute-done((bf16[56,1536]{1,0:T(8,128)(2,1)S(1)}, bf16[56,1536]{1,0:T(8,128)(2,1)S(1)}, u32[]{:S(2)}, u32[]{:S(2)}) %collective-permute-start.8) | collective-permute-done | bytes 172064 | tf_op jit(solution)/shard_map/ppermute | solution.py:365
  84.2 0.8 collective-permute-done.9.t3_ref
  85.0 0.9 shard_map.108
  (16 shorter events, 0.0 us)
Async XLA Ops:
  0.0 64.2 %copy-start.6 = (bf16[1536]{0:T(1024)(128)(2,1)S(1)}, bf16[1536]{0:T(1024)(128)(2,1)}, u32[]{:S(2)}) copy-start(bf16[1536]{0:T(1024)(128)(2,1)} %param.17) | copy-start | bytes 9220
  4.1 8.5 %collective-permute-start = (bf16[4,2,128,384]{3,2,1,0:T(8,128)(2,1)}, bf16[4,2,128,384]{3,2,1,0:T(8,128)(2,1)S(1)}, u32[]{:S(2)}, u32[]{:S(2)}) collective-permute-start(bf16[4,2,128,384]{3,2,1,0:T(8,128)(2,1)} %get-tuple-element.26), channel_id=1, source_target_pairs={{0,1},{1,0},{2,3},{3,2},{4,5},{5,4},{6,7},{7,6},{8,9},{9,8},{10,11... | collective-permute-start | bytes 2359304 | tf_op jit(solution)/shard_map/ppermute | solution.py:317
  4.2 22.9 %all-to-all-start = ((bf16[32,32,384]{2,1,0:T(8,128)(2,1)}), bf16[32,32,384]{2,1,0:T(8,128)(2,1)S(1)}, u32[]{:S(2)}, u32[]{:S(2)}) async-start(bf16[32,32,384]{2,1,0:T(8,128)(2,1)} %get-tuple-element.24), calls=%async_computation | async-start | bytes 1572864 | tf_op jit(solution)/shard_map/all_to_all | solution.py:315
  12.5 1.1 %copy-start = (bf16[4,2,128,384]{3,2,1,0:T(8,128)(2,1)S(1)}, bf16[4,2,128,384]{3,2,1,0:T(8,128)(2,1)}, u32[]{:S(2)}) copy-start(bf16[4,2,128,384]{3,2,1,0:T(8,128)(2,1)} %get-tuple-element.25.keep_ref) | copy-start | bytes 2359300
  14.6 17.3 %collective-permute-start.1 = (bf16[2,2,128,384]{3,2,1,0:T(8,128)(2,1)}, bf16[2,2,128,384]{3,2,1,0:T(8,128)(2,1)S(1)}, u32[]{:S(2)}, u32[]{:S(2)}) collective-permute-start(bf16[2,2,128,384]{3,2,1,0:T(8,128)(2,1)} %get-tuple-element.27), channel_id=1, source_target_pairs={{0,2},{1,9},{2,4},{3,11},{4,6},{5,13},{6,0},{7,15},{8,10},{9,17},{... | collective-permute-start | bytes 1179656 | tf_op jit(solution)/shard_map/ppermute | solution.py:319
  16.3 17.4 %collective-permute-start.2 = (bf16[2,2,128,384]{3,2,1,0:T(8,128)(2,1)S(1)}, bf16[2,2,128,384]{3,2,1,0:T(8,128)(2,1)S(1)}, u32[]{:S(2)}, u32[]{:S(2)}) collective-permute-start(bf16[2,2,128,384]{3,2,1,0:T(8,128)(2,1)S(1)} %get-tuple-element.28), channel_id=1, source_target_pairs={{0,4},{1,17},{2,6},{3,19},{4,0},{5,21},{6,2},{7,23},{8,12},{9,25},... | collective-permute-start | bytes 1179656 | tf_op jit(solution)/shard_map/ppermute | solution.py:319
  19.0 14.7 %collective-permute-start.3 = (bf16[2,2,128,384]{3,2,1,0:T(8,128)(2,1)S(1)}, bf16[2,2,128,384]{3,2,1,0:T(8,128)(2,1)S(1)}, u32[]{:S(2)}, u32[]{:S(2)}) collective-permute-start(bf16[2,2,128,384]{3,2,1,0:T(8,128)(2,1)S(1)} %get-tuple-element.29), channel_id=1, source_target_pairs={{0,6},{1,25},{2,0},{3,27},{4,2},{5,29},{6,4},{7,31},{8,14},{9,1},{... | collective-permute-start | bytes 1179656 | tf_op jit(solution)/shard_map/ppermute | solution.py:319
  27.1 1.1 %copy-start.1 = (bf16[4,2,128,384]{3,2,1,0:T(8,128)(2,1)S(1)}, bf16[4,2,128,384]{3,2,1,0:T(8,128)(2,1)}, u32[]{:S(2)}) copy-start(bf16[4,2,128,384]{3,2,1,0:T(8,128)(2,1)} %get-tuple-element.25.keep_ref) | copy-start | bytes 2359300
  29.9 0.9 %copy-start.2 = (bf16[1,28,3072]{2,1,0:T(8,128)(2,1)S(1)}, bf16[1,28,3072]{2,1,0:T(8,128)(2,1)}, u32[]{:S(2)}) copy-start(bf16[1,28,3072]{2,1,0:T(8,128)(2,1)} %refs_0_.2) | copy-start | bytes 516100
  30.9 0.7 copy-start.3
  58.3 12.3 %collective-permute-start.4 = (bf16[56,1536]{1,0:T(8,128)(2,1)S(1)}, bf16[56,1536]{1,0:T(8,128)(2,1)S(1)}, u32[]{:S(2)}, u32[]{:S(2)}) collective-permute-start(bf16[56,1536]{1,0:T(8,128)(2,1)S(1)} %get-tuple-element.34.r0_ref), channel_id=1, source_target_pairs={{0,32},{32,64},{64,96},{96,0},{1,33},{33,65},{65,97},{97,1},{2,34}... | collective-permute-start | bytes 516104 | tf_op jit(solution)/shard_map/ppermute | solution.py:351
  60.0 10.8 %collective-permute-start.5 = (bf16[56,1536]{1,0:T(8,128)(2,1)S(1)}, bf16[56,1536]{1,0:T(8,128)(2,1)S(1)}, u32[]{:S(2)}, u32[]{:S(2)}) collective-permute-start(bf16[56,1536]{1,0:T(8,128)(2,1)S(1)} %get-tuple-element.34.r0_ref), channel_id=1, source_target_pairs={{0,64},{32,96},{64,0},{96,32},{1,65},{33,97},{65,1},{97,33},{2,66}... | collective-permute-start | bytes 516104 | tf_op jit(solution)/shard_map/ppermute | solution.py:351
  62.8 7.9 %collective-permute-start.6 = (bf16[56,1536]{1,0:T(8,128)(2,1)S(1)}, bf16[56,1536]{1,0:T(8,128)(2,1)S(1)}, u32[]{:S(2)}, u32[]{:S(2)}) collective-permute-start(bf16[56,1536]{1,0:T(8,128)(2,1)S(1)} %get-tuple-element.34.r0_ref), channel_id=1, source_target_pairs={{0,96},{32,0},{64,32},{96,64},{1,97},{33,1},{65,33},{97,65},{2,98}... | collective-permute-start | bytes 516104 | tf_op jit(solution)/shard_map/ppermute | solution.py:351
  70.7 7.6 %copy-start.5 = (bf16[3072]{0:T(1024)(128)(2,1)S(1)}, bf16[3072]{0:T(1024)(128)(2,1)}, u32[]{:S(2)}) copy-start(bf16[3072]{0:T(1024)(128)(2,1)} %param.19) | copy-start | bytes 18436
  70.7 14.3 %copy-start.4 = (bf16[1,4,3072]{2,1,0:T(4,128)(2,1)S(1)}, bf16[1,4,3072]{2,1,0:T(4,128)(2,1)}, u32[]{:S(2)}) copy-start(bf16[1,4,3072]{2,1,0:T(4,128)(2,1)} %mod_ref.1) | copy-start | bytes 73732
  73.6 8.9 %collective-permute-start.7 = (bf16[56,1536]{1,0:T(8,128)(2,1)S(1)}, bf16[56,1536]{1,0:T(8,128)(2,1)S(1)}, u32[]{:S(2)}, u32[]{:S(2)}) collective-permute-start(bf16[56,1536]{1,0:T(8,128)(2,1)S(1)} %get-tuple-element.39), channel_id=1, source_target_pairs={{0,64},{32,96},{64,0},{96,32},{1,65},{33,97},{65,1},{97,33},{2,66}... | collective-permute-start | bytes 516104 | tf_op jit(solution)/shard_map/ppermute | solution.py:365
  76.3 7.9 %collective-permute-start.8 = (bf16[56,1536]{1,0:T(8,128)(2,1)S(1)}, bf16[56,1536]{1,0:T(8,128)(2,1)S(1)}, u32[]{:S(2)}, u32[]{:S(2)}) collective-permute-start(bf16[56,1536]{1,0:T(8,128)(2,1)S(1)} %get-tuple-element.40), channel_id=1, source_target_pairs={{0,96},{32,0},{64,32},{96,64},{1,97},{33,1},{65,33},{97,65},{2,98}... | collective-permute-start | bytes 516104 | tf_op jit(solution)/shard_map/ppermute | solution.py:365
  77.6 7.4 %collective-permute-start.9 = (bf16[56,1536]{1,0:T(8,128)(2,1)S(1)}, bf16[56,1536]{1,0:T(8,128)(2,1)S(1)}, u32[]{:S(2)}, u32[]{:S(2)}) collective-permute-start(bf16[56,1536]{1,0:T(8,128)(2,1)S(1)} %get-tuple-element.41), channel_id=1, source_target_pairs={{0,32},{32,64},{64,96},{96,0},{1,33},{33,65},{65,97},{97,1},{2,34}... | collective-permute-start | bytes 516104 | tf_op jit(solution)/shard_map/ppermute | solution.py:365
